TPU v7x, 32 devices: a whole 2x2x4 slice. The times are simulated.
32 devices in a mesh: groups: 2 (over x), src: 16 (over z, y, core).
Axes of the slice: x: 2, y: 2, z: 4, core: 2. Of those that a mesh axis runs over, the one named last changes fastest.
Arguments:
- kernel_band: float32 [2048, 131072], P('groups', 'src'), parts along dimension 0, may hold values from -0.0234375 to 0.0234375
- slip_field: float32 [1024, 131072], P(('groups', 'src')), parts along dimension 0, may hold values from -6 to 6
- elements: int32 [2048], P('groups'), parts along dimension 0, may hold values from 0 to 131071, as said below
- classes: int32 [2048, 512], P(('groups', 'src')), parts along dimension 0, may hold values from 0 to 7
- shear_load: float32 [2048], P(('groups', 'src')), parts along dimension 0, may hold values from 0.5 to 1.5
- normal_stress: float32 [2048], P(('groups', 'src')), parts along dimension 0, may hold values from 0.5 to 2
- static_friction: float32 [8], replicated, may hold values from 0.6 to 0.9
- dynamic_friction: float32 [8], replicated, may hold values from 0.1 to 0.5
- weakening_slip: float32 [8], replicated, may hold values from 0.3 to 3
Outputs:
- shear_stress: float32 [2048, 512], P(('groups', 'src')), parts along dimension 0
- slip_rate: float32 [2048, 512], P(('groups', 'src')), parts along dimension 0
There are 2 independent parts, one for each index of `groups`. A program takes and returns all parts, laid end to end along the dimension named above; an argument that names none is the same for every part. Nothing has to cross between parts.
Inputs may be any that keep to these rules, and one draw needn't show every extreme that they name: `elements`: the 1024 element numbers are distinct.
All inputs are finite; a program needn't handle non-finite values.
Results may differ from a plain program's by a relative error of at most 0.000059.
Values sent between devices are 32-bit elements; how exact they have to be, the bound alone decides.
No kernel may reach another device: no remote copies, remote signals or barrier semaphores. Data moves between devices by JAX's collectives and lax.ppermute only.
A program may use at most 192 MiB of HBM per device.

v0:
```python
import jax
import jax.numpy as jnp
from jax import lax
from jax.sharding import PartitionSpec as P


def lookup(table, classes):
    total = jnp.zeros(classes.shape, jnp.float32)
    for index in range(table.shape[0]):
        total = total + jnp.where(classes == index, table[index], jnp.float32(0.0))
    return total


def shards(
    kernel_band,
    slip_field,
    elements,
    classes,
    shear_load,
    normal_stress,
    static_friction,
    dynamic_friction,
    weakening_slip,
):
    blocks = lax.all_to_all(slip_field, "src", split_axis=1, concat_axis=0, tiled=True)
    partial_sum = lax.dot_general(
        kernel_band,
        blocks,
        (((1,), (1,)), ((), ())),
        precision=lax.Precision.HIGHEST,
        preferred_element_type=jnp.float32,
    )
    summed = lax.psum_scatter(partial_sum, "src", scatter_dimension=0, tiled=True)
    own_members = jnp.take(slip_field, elements, axis=1).T
    receiver_slip = lax.all_to_all(own_members, "src", split_axis=0, concat_axis=1, tiled=True)
    shear_stress = shear_load[:, None] + summed
    mu_static = lookup(static_friction, classes)
    mu_dynamic = lookup(dynamic_friction, classes)
    slip_scale = lookup(weakening_slip, classes)
    weakening = jnp.maximum(1.0 - jnp.abs(receiver_slip) / slip_scale, 0.0)
    strength = normal_stress[:, None] * (mu_dynamic + (mu_static - mu_dynamic) * weakening)
    slip_rate = jax.nn.softplus((shear_stress - strength) / 0.25)
    return (shear_stress, slip_rate)


def solution(mesh):
    placed = (
        P("groups", "src"),
        P(("groups", "src"), None),
        P("groups"),
        P(("groups", "src"), None),
        P(("groups", "src")),
        P(("groups", "src")),
        P(),
        P(),
        P(),
    )
    return jax.shard_map(
        shards,
        mesh=mesh,
        in_specs=placed,
        out_specs=(P(("groups", "src"), None), P(("groups", "src"), None)),
        check_vma=False,
    )
```

profile of v0, /device:TPU:0, one launch (start us, length us, event | category | flops | bytes accessed | tf_op | source)
XLA Modules:
  0.0 531.0 jit_solution(15168083311280900769)
XLA Ops:
  7.2 0.0 reduce-scatter.2.cloned.1.call-start
  7.2 6.7 %copy.26 = f32[4,16,8,8192]{3,2,0,1:T(8,128)S(1)} copy(f32[4,16,8,8192]{3,2,1,0:T(8,128)} %bitcast.40) | data formatting | bytes 33554432 | tf_op jit(solution)/shard_map/all_to_all | solution.py:25
  14.0 369.2 %all_to_all.32 = f32[32,16,8192]{2,0,1:T(8,128)} all-to-all(f32[32,16,8192]{2,0,1:T(8,128)S(1)} %bitcast.41), channel_id=1, replica_groups=mesh['groups'=2,'src'=16] {'src'}, dimensions={1} | all-to-all | bytes 33554432 | tf_op jit(solution)/shard_map/all_to_all | solution.py:25
  383.2 59.7 %fusion.4 = f32[1024,512]{1,0:T(8,128)} fusion(f32[1024,8192]{1,0:T(8,128)} %param.9, f32[512,8192]{1,0:T(8,128)} %bitcast.42), kind=kOutput, calls=%fused_computation.12 | convolution fusion | flops 51539607552 | bytes 52428800 | tf_op jit(solution)/shard_map/dot_general | solution.py:26
  442.9 0.0 reduce-scatter.2.cloned.1.call-update
  442.9 0.0 copy-start.1
  442.9 0.0 copy-start.2
  443.0 0.0 copy-start
  443.0 35.4 %copy.21 = f32[32,131072]{0,1:T(8,128)} copy(f32[32,131072]{1,0:T(8,128)} %param.10) | data formatting | bytes 33554432 | tf_op args[1]
  478.4 10.7 %gather_fusion = f32[1024,32]{1,0:T(8,128)S(1)} fusion(f32[32,131072]{0,1:T(8,128)} %copy.21, s32[1024]{0:T(1024)S(1)} %fusion), kind=kCustom, calls=%fused_computation | custom fusion | bytes 266240 | tf_op jit(solution)/shard_map/jit(_take)/gather | solution.py:34
  489.2 0.2 broadcast_select_fusion
  489.4 0.2 copy.22
  489.6 0.8 reshape.27
  490.4 6.4 %all-to-all-start.1 = ((f32[16,1,2048]{2,1,0:T(1,128)}), f32[16,1,2048]{2,1,0:T(1,128)S(1)}, u32[]{:S(2)}, u32[]{:S(2)}) async-start(f32[16,1,2048]{2,1,0:T(1,128)} %reshape.27), calls=%async_computation.2 | async-start | bytes 262144 | tf_op jit(solution)/shard_map/all_to_all | solution.py:35
  496.8 0.7 fusion.3
  497.5 0.7 fusion.2
  498.2 0.7 fusion.1
  498.9 6.4 %all-to-all-done.1 = f32[16,1,2048]{2,1,0:T(1,128)S(1)} async-done(((f32[16,1,2048]{2,1,0:T(1,128)}), f32[16,1,2048]{2,1,0:T(1,128)S(1)}, u32[]{:S(2)}, u32[]{:S(2)}) %all-to-all-start.1) | async-done | bytes 131104 | tf_op jit(solution)/shard_map/all_to_all | solution.py:35
  505.3 0.5 broadcast.60
  505.8 1.0 reduce
  506.8 0.1 reshape.28
  506.9 0.1 copy.23
  507.0 0.1 reduce-scatter.2.cloned.1.call-done
  507.1 17.0 %compare_select_fusion = (f32[64,512]{1,0:T(8,128)}, f32[64,512]{1,0:T(8,128)}) fusion(f32[64,512]{1,0:T(8,128)S(1)} %copy.23, s32[64,512]{1,0:T(8,128)S(1)} %copy-done, f32[]{:T(128)} %bitcast.28, f32[]{:T(128)} %bitcast.27, f32[]{:T(128)} %bitcast.26, f32[]{:T(128)} %bitcast.25, f32[]{:T(128)} %bitcast.24, f32[]{:T(128)} %bitcast.23, f32[]{:T(128)} %bitcast.22, ...), kind=kLoop, calls=%fused_computation.2 | loop fusion | flops 2260992 | bytes 655968 | tf_op jit(solution)/shard_map/jit(softplus)/select_n | solution.py:42
  (14 shorter events, 0.1 us)
Async XLA Ops:
  7.2 500.0 %reduce-scatter.2.cloned.1.call-start = ((), (), s32[]{:S(2)}) async-start(), calls=%async_computation.3 | async-start | bytes 2228224 | tf_op jit(solution)/shard_map/reduce_scatter | solution.py:33
  442.9 35.5 %copy-start.4 = (s32[1024]{0:T(1024)S(1)}, s32[1024]{0:T(1024)}, u32[]{:S(2)}) copy-start(s32[1024]{0:T(1024)} %param.11) | copy-start | bytes 12292
  442.9 53.9 %copy-start.1 = (f32[8]{0:T(128)S(1)}, f32[8]{0:T(128)}, u32[]{:S(2)}) copy-start(f32[8]{0:T(128)} %param.17) | copy-start | bytes 100
  442.9 54.5 %copy-start.2 = (f32[8]{0:T(128)S(1)}, f32[8]{0:T(128)}, u32[]{:S(2)}) copy-start(f32[8]{0:T(128)} %param.15) | copy-start | bytes 100
  443.0 55.2 %copy-start.3 = (f32[8]{0:T(128)S(1)}, f32[8]{0:T(128)}, u32[]{:S(2)}) copy-start(f32[8]{0:T(128)} %param.16) | copy-start | bytes 100
  443.0 64.2 %copy-start = (s32[64,512]{1,0:T(8,128)S(1)}, s32[64,512]{1,0:T(8,128)}, u32[]{:S(2)}) copy-start(s32[64,512]{1,0:T(8,128)} %param.12) | copy-start | bytes 393220
  443.0 64.2 %copy-start.5 = (f32[64]{0:T(128)S(1)}, f32[64]{0:T(128)}, u32[]{:S(2)}) copy-start(f32[64]{0:T(128)} %param.14) | copy-start | bytes 772
  443.0 64.1 %copy-start.6 = (f32[64]{0:T(128)S(1)}, f32[64]{0:T(128)}, u32[]{:S(2)}) copy-start(f32[64]{0:T(128)} %param.13) | copy-start | bytes 772
  490.4 14.9 %all-to-all-start.1 = ((f32[16,1,2048]{2,1,0:T(1,128)}), f32[16,1,2048]{2,1,0:T(1,128)S(1)}, u32[]{:S(2)}, u32[]{:S(2)}) async-start(f32[16,1,2048]{2,1,0:T(1,128)} %reshape.27), calls=%async_computation.2 | async-start | bytes 262144 | tf_op jit(solution)/shard_map/all_to_all | solution.py:35
Sparse Core Ops, SparseCore 0:
  443.0 64.0 reduce-scatter.1
where the time goes:
time: 532 us; the launch traced here: 531 us
  blocking collectives  369 us (69%)
  matrix products  59.7 us (11%)
  local copies, waits for them, and re-layouts  56.7 us (11%)
  other arithmetic  18.2 us (3%)
  between operations  14.2 us (3%)
  waiting for transfers between devices  6.55 us (1%)
  starting transfers between devices  6.45 us (1%)
    all_to_all x1, blocking collectives, shards(): lax.all_to_all(slip_field, 'src', split_axis=1, concat_axis=0, tiled=True)  369 us
    dot_general x1, matrix products, shards(): lax.dot_general(kernel_band, blocks, (((1,), (1,)), ((), ())), precision=...  59.7 us
    unnamed x17, local copies, waits for them, and re-layouts  36.4 us
    select_n x1, other arithmetic, shards(): slip_rate = jax.nn.softplus((shear_stress - strength) / 0.25)  17 us
    gather x1, local copies, waits for them, and re-layouts, shards(): own_members = jnp.take(slip_field, elements, axis=1).T  10.7 us
  transfers between devices with their start and end apart: 2, of which 2 were waited for; matrix products, arithmetic and copies ran while one was open for 10% of the time, Pallas kernels for 0%

commit v1 on v0

v1 whole, which is shorter than its diff:
```python
import functools

import jax
import jax.numpy as jnp
from jax import lax
from jax.experimental import pallas as pl
from jax.experimental.pallas import tpu as pltpu
from jax.sharding import PartitionSpec as P

VMEM_LIMIT = 40 * 1024 * 1024
TAIL_ROWS = 8


def halves(x):
    high = x.astype(jnp.bfloat16)
    low = (x - high.astype(jnp.float32)).astype(jnp.bfloat16)
    return high, low


def product_kernel(band_ref, slip_ref, out_ref):
    @pl.when(pl.program_id(0) == 0)
    def _():
        out_ref[...] = jnp.zeros_like(out_ref)

    members = slip_ref.shape[0]
    band_high, band_low = halves(band_ref[...])
    slip_high, slip_low = halves(slip_ref[...])
    over_last = (((1,), (1,)), ((), ()))
    wide = lax.dot_general(
        band_high,
        jnp.concatenate([slip_high, slip_low], axis=0),
        over_last,
        preferred_element_type=jnp.float32,
    )
    narrow = lax.dot_general(band_low, slip_high, over_last, preferred_element_type=jnp.float32)
    out_ref[...] += wide[:, :members] + (wide[:, members:] + narrow)


def product(band, slip, tile=512):
    rows, depth = band.shape
    members = slip.shape[0]
    return pl.pallas_call(
        product_kernel,
        grid=(depth // tile,),
        in_specs=[
            pl.BlockSpec((rows, tile), lambda i: (0, i)),
            pl.BlockSpec((members, tile), lambda i: (0, i)),
        ],
        out_specs=pl.BlockSpec((rows, members), lambda i: (0, 0)),
        out_shape=jax.ShapeDtypeStruct((rows, members), jnp.float32),
        compiler_params=pltpu.CompilerParams(vmem_limit_bytes=VMEM_LIMIT),
        cost_estimate=pl.CostEstimate(
            flops=6 * rows * depth * members,
            bytes_accessed=4 * (rows * depth + members * depth + rows * members),
            transcendentals=0,
        ),
        name="stress_product",
    )(band, slip)


def swap(x, bit, ways):
    return lax.ppermute(x, "src", [(i, i ^ bit) for i in range(ways)])


def owner_sums(partial, me, ways):
    columns = partial.shape[1]
    own = partial.shape[0] // ways
    left, bit = partial, 1
    while bit < ways:
        pairs = left.reshape(ways // bit // 2, 2, own, columns)
        mine = (me // bit) & 1
        kept = lax.dynamic_index_in_dim(pairs, mine, 1, keepdims=False)
        given = lax.dynamic_index_in_dim(pairs, 1 - mine, 1, keepdims=False)
        left = kept + swap(given, bit, ways)
        bit *= 2
    return left.reshape(own, columns)


def friction_kernel(
    static_ref, dynamic_ref, scale_ref, first_ref, last_ref, spread_ref, slip_ref, classes_ref, load_ref, normal_ref, stress_ref, rate_ref
):
    total = first_ref[...] + lax.dot_general(
        last_ref[...],
        spread_ref[...],
        (((1,), (0,)), ((), ())),
        precision=lax.Precision.HIGHEST,
        preferred_element_type=jnp.float32,
    )
    stress = load_ref[...] + total
    classes = classes_ref[...]
    zero = jnp.zeros(classes.shape, jnp.float32)
    mu_static, mu_dynamic, slip_scale = zero, zero, zero
    for index in range(static_ref.shape[0]):
        here = classes == index
        mu_static = jnp.where(here, static_ref[index], mu_static)
        mu_dynamic = jnp.where(here, dynamic_ref[index], mu_dynamic)
        slip_scale = jnp.where(here, scale_ref[index], slip_scale)
    weakening = jnp.maximum(1.0 - jnp.abs(slip_ref[...]) / slip_scale, 0.0)
    strength = normal_ref[...] * (mu_dynamic + (mu_static - mu_dynamic) * weakening)
    excess = (stress - strength) / 0.25
    stress_ref[...] = stress
    rate_ref[...] = jnp.maximum(excess, 0.0) + jnp.log1p(jnp.exp(-jnp.abs(excess)))


def friction(first, last, spread, slip, classes, load, normal, static, dynamic, scale):
    table = pl.BlockSpec(memory_space=pltpu.SMEM)
    whole = pl.BlockSpec(memory_space=pltpu.VMEM)
    shape = jax.ShapeDtypeStruct(classes.shape, jnp.float32)
    return pl.pallas_call(
        friction_kernel,
        in_specs=[table] * 3 + [whole] * 7,
        out_specs=[whole] * 2,
        out_shape=[shape, shape],
        name="friction",
    )(static, dynamic, scale, first, last, spread, slip, classes, load[:, None], normal[:, None])


def shards(
    ways,
    kernel_band,
    slip_field,
    elements,
    classes,
    shear_load,
    normal_stress,
    static_friction,
    dynamic_friction,
    weakening_slip,
):
    me = lax.axis_index("src")
    members, total_elements = slip_field.shape
    depth = total_elements // ways
    own = classes.shape[0]
    tail = min(TAIL_ROWS, members)
    head = members - tail

    def to_blocks(rows):
        return jnp.swapaxes(rows.reshape(rows.shape[0], ways, depth), 0, 1)

    at_receivers = jnp.take(slip_field, elements, axis=1)
    riders = at_receivers.reshape(members // tail, tail, ways, own)
    riders = riders.transpose(2, 1, 0, 3).reshape(ways, tail, -1)

    sums = []
    if head:
        first = lax.all_to_all(to_blocks(slip_field[:head]), "src", 0, 0, tiled=True)
        sums.append((head, product(kernel_band, first.reshape(ways * head, depth))))
    payload = jnp.concatenate([to_blocks(slip_field[head:]), riders], axis=2)
    last = lax.all_to_all(payload, "src", 0, 0, tiled=True)
    last_product = product(kernel_band, last.reshape(ways * tail, -1))
    receiver_slip = last[:, :, depth:].reshape(ways, tail, members // tail, own)
    receiver_slip = receiver_slip.transpose(3, 0, 2, 1).reshape(own, ways * members)

    if head:
        first_sums = owner_sums(sums[0][1], me, ways).reshape(own, ways, head)
        first_sums = jnp.pad(first_sums, ((0, 0), (0, 0), (0, tail))).reshape(own, ways * members)
    else:
        first_sums = jnp.zeros((own, ways * members), jnp.float32)
    last_sums = owner_sums(last_product, me, ways)
    place = lax.broadcasted_iota(jnp.int32, (ways * tail, ways * members), 1)
    source = lax.broadcasted_iota(jnp.int32, (ways * tail, ways * members), 0)
    spread = (place == source // tail * members + head + source % tail).astype(jnp.float32)
    return friction(
        first_sums,
        last_sums,
        spread,
        receiver_slip,
        classes,
        shear_load,
        normal_stress,
        static_friction,
        dynamic_friction,
        weakening_slip,
    )


def solution(mesh):
    placed = (
        P("groups", "src"),
        P(("groups", "src"), None),
        P("groups"),
        P(("groups", "src"), None),
        P(("groups", "src")),
        P(("groups", "src")),
        P(),
        P(),
        P(),
    )
    return jax.shard_map(
        functools.partial(shards, mesh.shape["src"]),
        mesh=mesh,
        in_specs=placed,
        out_specs=(P(("groups", "src"), None), P(("groups", "src"), None)),
        check_vma=False,
    )
```

time: 532 us -> 505 us (0.949)
  blocking collectives: 369 us -> 0 us
  waiting for transfers between devices: 6.55 us -> 273 us
  starting transfers between devices: 6.45 us -> 91.8 us
  matrix products: 59.7 us -> 0 us
  Pallas kernels: 0 us -> 51.7 us
  local copies, waits for them, and re-layouts: 56.7 us -> 77.2 us
  between operations: 14.2 us -> 0.87 us
  other arithmetic: 18.2 us -> 8.56 us
    all_to_all x1 -> x0, blocking collectives: 369 us -> none  [shards(): lax.all_to_all(slip_field, 'src', split_axis=1, concat_axis=0, tiled=True)]
    all_to_all x1 -> x2, waiting for transfers between devices: 6.43 us -> 263 us  [the longest x1 203 us: shards(): lax.all_to_all(to_blocks(slip_field[:head]), 'src', 0, 0, tiled=True)]
    ppermute x0 -> x8, starting transfers between devices: none -> 64.1 us  [swap(): return lax.ppermute(x, 'src', [(i, i ^ bit) for i in range(ways)])]
    dot_general x1 -> x0, matrix products: 59.7 us -> none  [shards(): lax.dot_general(kernel_band, blocks, (((1,), (1,)), ((), ())), precision=...]
    pallas_call x0 -> x3, Pallas kernels: none -> 51.7 us  [the longest x2 49.4 us: product(): pl.pallas_call(product_kernel, grid=(depth // tile,), in_specs=[pl.BlockS...]
    all_to_all x1 -> x2, starting transfers between devices: 6.41 us -> 27.6 us  [the longest x1 20.2 us: shards(): lax.all_to_all(to_blocks(slip_field[:head]), 'src', 0, 0, tiled=True)]
    select_n x2 -> x0, other arithmetic: 17.2 us -> none  [the longest x1 17 us: shards(): slip_rate = jax.nn.softplus((shear_stress - strength) / 0.25)]
    slice x3, local copies, waits for them, and re-layouts: 2.02 us -> 15.2 us  [the longest x1 9.87 us: shards(): slip_field[:head]]
  transfers between devices with their start and end apart: 2 -> 10, of which waited for: 2 -> 6; matrix products, arithmetic and copies ran while one was open for 10% -> 5% of each run, Pallas kernels for 0% -> 4%
where the time goes in v1:
time: 505 us; the launch traced here: 503 us
  waiting for transfers between devices  273 us (54%)
  starting transfers between devices  91.8 us (18%)
  local copies, waits for them, and re-layouts  77.2 us (15%)
  Pallas kernels  51.7 us (10%)
  other arithmetic  8.56 us (2%)
    all_to_all x1, waiting for transfers between devices, shards(): lax.all_to_all(to_blocks(slip_field[:head]), 'src', 0, 0, tiled=True)  203 us
    ppermute x8, starting transfers between devices, swap(): return lax.ppermute(x, 'src', [(i, i ^ bit) for i in range(ways)])  64.1 us
    all_to_all x1, waiting for transfers between devices, shards(): last = lax.all_to_all(payload, 'src', 0, 0, tiled=True)  59.6 us
    pallas_call x2, Pallas kernels, product(): pl.pallas_call(product_kernel, grid=(depth // tile,), in_specs=[pl.BlockS...  49.4 us
    unnamed x5, local copies, waits for them, and re-layouts  35.2 us
    all_to_all x1, starting transfers between devices, shards(): lax.all_to_all(to_blocks(slip_field[:head]), 'src', 0, 0, tiled=True)  20.2 us
    gather x3, local copies, waits for them, and re-layouts, shards(): at_receivers = jnp.take(slip_field, elements, axis=1)  10.7 us
    reshape x1, local copies, waits for them, and re-layouts, to_blocks(): return jnp.swapaxes(rows.reshape(rows.shape[0], ways, depth), 0, 1)  10.5 us
  transfers between devices with their start and end apart: 10, of which 6 were waited for; matrix products, arithmetic and copies ran while one was open for 5% of the time, Pallas kernels for 4%

profile of v1, /device:TPU:0, one launch (start us, length us, event | category | flops | bytes accessed | tf_op | source)
XLA Modules:
  0.0 502.8 jit_solution(10965969312052100204)
XLA Ops:
  2.0 35.2 %copy.26 = f32[32,131072]{0,1:T(8,128)} copy(f32[32,131072]{1,0:T(8,128)} %param.10) | data formatting | bytes 33554432 | tf_op args[1]
  37.2 4.5 slice.10
  41.6 10.4 %gather_fusion = f32[1024,32]{1,0:T(8,128)S(1)} fusion(f32[32,131072]{0,1:T(8,128)} %copy.26, s32[1024]{0:T(1024)S(1)} %fusion.1), kind=kCustom, calls=%fused_computation | custom fusion | bytes 266240 | tf_op jit(solution)/shard_map/jit(_take)/gather | solution.py:140
  52.9 4.5 pad_maximum_fusion
  57.4 7.4 %all-to-all-start.1 = ((f32[16,8,8448]{2,1,0:T(8,128)}), f32[16,8,8448]{2,1,0:T(8,128)}, u32[]{:S(2)}, u32[]{:S(2)}) async-start(f32[16,8,8448]{2,1,0:T(8,128)} %pad_maximum_fusion), calls=%async_computation.1 | async-start | bytes 8650752 | tf_op jit(solution)/shard_map/all_to_all | solution.py:149
  64.8 9.9 %slice.9 = f32[24,131072]{1,0:T(8,128)} slice(f32[32,131072]{1,0:T(8,128)} %param.10), slice={[0:24], [0:131072]} | slice | bytes 25165824 | tf_op jit(solution)/shard_map/slice | solution.py:146
  74.7 10.5 %copy.36 = f32[3,16,8,8192]{3,2,0,1:T(8,128)} copy(f32[3,16,8,8192]{3,2,1,0:T(8,128)} %bitcast.58) | data formatting | bytes 25165824 | tf_op jit(solution)/shard_map/reshape | solution.py:138
  85.2 59.6 %all-to-all-done.1 = f32[16,8,8448]{2,1,0:T(8,128)} async-done(((f32[16,8,8448]{2,1,0:T(8,128)}), f32[16,8,8448]{2,1,0:T(8,128)}, u32[]{:S(2)}, u32[]{:S(2)}) %all-to-all-start.1) | async-done | bytes 4325408 | tf_op jit(solution)/shard_map/all_to_all | solution.py:149
  144.8 20.2 %all-to-all-start = ((f32[16,24,8192]{2,1,0:T(8,128)}), f32[16,24,8192]{2,1,0:T(8,128)}, u32[]{:S(2)}, u32[]{:S(2)}) async-start(f32[16,24,8192]{2,1,0:T(8,128)} %bitcast.57), calls=%async_computation | async-start | bytes 25165824 | tf_op jit(solution)/shard_map/all_to_all | solution.py:146
  165.0 20.7 %stress_product.3 = f32[1024,128]{1,0:T(8,128)S(1)} custom-call(f32[1024,8192]{1,0:T(8,128)} %band_ref.3, f32[128,8448]{1,0:T(8,128)} %bitcast.17.slip_ref), custom_call_target="tpu_custom_call" | custom-call | flops 6442450944 | bytes 38273024 | tf_op jit(solution)/shard_map/stress_product/pallas_call | solution.py:42
  185.7 203.0 %all-to-all-done = f32[16,24,8192]{2,1,0:T(8,128)} async-done(((f32[16,24,8192]{2,1,0:T(8,128)}), f32[16,24,8192]{2,1,0:T(8,128)}, u32[]{:S(2)}, u32[]{:S(2)}) %all-to-all-start) | async-done | bytes 12582944 | tf_op jit(solution)/shard_map/all_to_all | solution.py:146
  388.7 28.7 %stress_product.2 = f32[1024,384]{1,0:T(8,128)S(1)} custom-call(f32[1024,8192]{1,0:T(8,128)} %band_ref.3, f32[384,8192]{1,0:T(8,128)} %bitcast.1.slip_ref), custom_call_target="tpu_custom_call" | custom-call | flops 19327352832 | bytes 47710208 | tf_op jit(solution)/shard_map/stress_product/pallas_call | solution.py:42
  417.5 1.0 dynamic-slice_bitcast_fusion
  419.4 2.3 collective-permute-done.4
  421.6 1.0 bitcast_add_fusion.2
  423.3 17.5 %collective-permute-start.5 = (f32[4,64,128]{2,1,0:T(8,128)}, f32[4,64,128]{2,1,0:T(8,128)S(1)}, u32[]{:S(2)}, u32[]{:S(2)}) collective-permute-start(f32[4,64,128]{2,1,0:T(8,128)} %dynamic-slice_bitcast_fusion.4), channel_id=1, source_target_pairs={{0,2},{1,3},{2,0},{3,1},{4,6},{5,7},{6,4},{7,5},{8,10},{9,11},{10,... | collective-permute-start | bytes 393224 | tf_op jit(solution)/shard_map/ppermute | solution.py:62
  443.3 0.9 slice.14
  445.4 33.8 %collective-permute-start.6 = (f32[2,64,128]{2,1,0:T(8,128)S(1)}, f32[2,64,128]{2,1,0:T(8,128)S(1)}, u32[]{:S(2)}, u32[]{:S(2)}) collective-permute-start(f32[2,64,128]{2,1,0:T(8,128)S(1)} %dynamic-slice_bitcast_fusion.5), channel_id=1, source_target_pairs={{0,4},{1,5},{2,6},{3,7},{4,0},{5,1},{6,2},{7,3},{8,12},{9,13},{10,... | collective-permute-start | bytes 196616 | tf_op jit(solution)/shard_map/ppermute | solution.py:62
  479.3 8.1 %collective-permute-start.2 = (f32[2,64,384]{2,1,0:T(8,128)S(1)}, f32[2,64,384]{2,1,0:T(8,128)S(1)}, u32[]{:S(2)}, u32[]{:S(2)}) collective-permute-start(f32[2,64,384]{2,1,0:T(8,128)S(1)} %dynamic-slice_bitcast_fusion.3), channel_id=1, source_target_pairs={{0,4},{1,5},{2,6},{3,7},{4,0},{5,1},{6,2},{7,3},{8,12},{9,13},{10,... | collective-permute-start | bytes 589832 | tf_op jit(solution)/shard_map/ppermute | solution.py:62
  487.4 1.5 collective-permute-start.7
  488.9 4.0 collective-permute-done.2
  492.9 2.4 collective-permute-start.3
  495.9 3.7 collective-permute-done.3
  500.6 2.2 friction.1
  (46 shorter events, 9.0 us)
Async XLA Ops:
  57.4 87.4 %all-to-all-start.1 = ((f32[16,8,8448]{2,1,0:T(8,128)}), f32[16,8,8448]{2,1,0:T(8,128)}, u32[]{:S(2)}, u32[]{:S(2)}) async-start(f32[16,8,8448]{2,1,0:T(8,128)} %pad_maximum_fusion), calls=%async_computation.1 | async-start | bytes 8650752 | tf_op jit(solution)/shard_map/all_to_all | solution.py:149
  144.8 244.0 %all-to-all-start = ((f32[16,24,8192]{2,1,0:T(8,128)}), f32[16,24,8192]{2,1,0:T(8,128)}, u32[]{:S(2)}, u32[]{:S(2)}) async-start(f32[16,24,8192]{2,1,0:T(8,128)} %bitcast.57), calls=%async_computation | async-start | bytes 25165824 | tf_op jit(solution)/shard_map/all_to_all | solution.py:146
  417.5 24.4 %copy-start = (f32[64]{0:T(128)S(1)}, f32[64]{0:T(128)}, u32[]{:S(2)}) copy-start(f32[64]{0:T(128)} %param.13) | copy-start | bytes 772
  417.5 25.1 %copy-start.1 = (f32[64]{0:T(128)S(1)}, f32[64]{0:T(128)}, u32[]{:S(2)}) copy-start(f32[64]{0:T(128)} %param.14) | copy-start | bytes 772
  418.4 22.3 %collective-permute-start = (f32[8,64,384]{2,1,0:T(8,128)}, f32[8,64,384]{2,1,0:T(8,128)S(1)}, u32[]{:S(2)}, u32[]{:S(2)}) collective-permute-start(f32[8,64,384]{2,1,0:T(8,128)} %dynamic-slice_bitcast_fusion), channel_id=1, source_target_pairs={{0,1},{1,0},{2,3},{3,2},{4,5},{5,4},{6,7},{7,6},{8,9},{9,8},{10,11... | collective-permute-start | bytes 2359304 | tf_op jit(solution)/shard_map/ppermute | solution.py:62
  419.2 2.4 collective-permute-start.4
  423.3 22.0 %collective-permute-start.5 = (f32[4,64,128]{2,1,0:T(8,128)}, f32[4,64,128]{2,1,0:T(8,128)S(1)}, u32[]{:S(2)}, u32[]{:S(2)}) collective-permute-start(f32[4,64,128]{2,1,0:T(8,128)} %dynamic-slice_bitcast_fusion.4), channel_id=1, source_target_pairs={{0,2},{1,3},{2,0},{3,1},{4,6},{5,7},{6,4},{7,5},{8,10},{9,11},{10,... | collective-permute-start | bytes 393224 | tf_op jit(solution)/shard_map/ppermute | solution.py:62
  440.9 38.3 %collective-permute-start.1 = (f32[4,64,384]{2,1,0:T(8,128)S(1)}, f32[4,64,384]{2,1,0:T(8,128)S(1)}, u32[]{:S(2)}, u32[]{:S(2)}) collective-permute-start(f32[4,64,384]{2,1,0:T(8,128)S(1)} %dynamic-slice_bitcast_fusion.1), channel_id=1, source_target_pairs={{0,2},{1,3},{2,0},{3,1},{4,6},{5,7},{6,4},{7,5},{8,10},{9,11},{10,... | collective-permute-start | bytes 1179656 | tf_op jit(solution)/shard_map/ppermute | solution.py:62
  445.4 42.0 %collective-permute-start.6 = (f32[2,64,128]{2,1,0:T(8,128)S(1)}, f32[2,64,128]{2,1,0:T(8,128)S(1)}, u32[]{:S(2)}, u32[]{:S(2)}) collective-permute-start(f32[2,64,128]{2,1,0:T(8,128)S(1)} %dynamic-slice_bitcast_fusion.5), channel_id=1, source_target_pairs={{0,4},{1,5},{2,6},{3,7},{4,0},{5,1},{6,2},{7,3},{8,12},{9,13},{10,... | collective-permute-start | bytes 196616 | tf_op jit(solution)/shard_map/ppermute | solution.py:62
  479.3 13.6 %collective-permute-start.2 = (f32[2,64,384]{2,1,0:T(8,128)S(1)}, f32[2,64,384]{2,1,0:T(8,128)S(1)}, u32[]{:S(2)}, u32[]{:S(2)}) collective-permute-start(f32[2,64,384]{2,1,0:T(8,128)S(1)} %dynamic-slice_bitcast_fusion.3), channel_id=1, source_target_pairs={{0,4},{1,5},{2,6},{3,7},{4,0},{5,1},{6,2},{7,3},{8,12},{9,13},{10,... | collective-permute-start | bytes 589832 | tf_op jit(solution)/shard_map/ppermute | solution.py:62
  487.4 8.0 %collective-permute-start.7 = (f32[1,64,128]{2,1,0:T(8,128)S(1)}, f32[1,64,128]{2,1,0:T(8,128)S(1)}, u32[]{:S(2)}, u32[]{:S(2)}) collective-permute-start(f32[1,64,128]{2,1,0:T(8,128)S(1)} %constant_dynamic-slice_fusion), channel_id=1, source_target_pairs={{0,8},{1,9},{2,10},{3,11},{4,12},{5,13},{6,14},{7,15},{8,0},{9,1},... | collective-permute-start | bytes 98312 | tf_op jit(solution)/shard_map/ppermute | solution.py:62
  492.9 6.7 %collective-permute-start.3 = (f32[1,64,384]{2,1,0:T(8,128)S(1)}, f32[1,64,384]{2,1,0:T(8,128)S(1)}, u32[]{:S(2)}, u32[]{:S(2)}) collective-permute-start(f32[1,64,384]{2,1,0:T(8,128)S(1)} %constant_dynamic-slice_fusion.1), channel_id=1, source_target_pairs={{0,8},{1,9},{2,10},{3,11},{4,12},{5,13},{6,14},{7,15},{8,0},{9,1},... | collective-permute-start | bytes 294920 | tf_op jit(solution)/shard_map/ppermute | solution.py:62

commit v2 on v0

v2 whole, which is shorter than its diff:
```python
import functools

import jax
import jax.numpy as jnp
from jax import lax
from jax.experimental import pallas as pl
from jax.experimental.pallas import tpu as pltpu
from jax.sharding import PartitionSpec as P

VMEM_LIMIT = 48 * 1024 * 1024
TAIL_ROWS = 8
IN_FLIGHT = 4
TILE = 2048
FIRST_WEIGHT = 10
LANES = 128
ANY = pl.BlockSpec(memory_space=pl.ANY)
AFTER = pl.BlockSpec(memory_space=pltpu.HBM)
SCALARS = pl.BlockSpec(memory_space=pltpu.SMEM)
WHOLE = pl.BlockSpec(memory_space=pltpu.VMEM)
OVER_LAST = (((1,), (1,)), ((), ()))


def halves(x):
    high = x.astype(jnp.bfloat16)
    low = (x - high.astype(jnp.float32)).astype(jnp.bfloat16)
    return high, low


def split_kernel(band_ref, after_ref, out_ref):
    del after_ref
    tile = band_ref.shape[1]
    out_ref[:, pl.ds(0, tile)], out_ref[:, pl.ds(tile, tile)] = halves(band_ref[...])


def split(band, after):
    receivers, depth = band.shape
    tile, rows = min(TILE, depth), receivers // 4
    return pl.pallas_call(
        split_kernel,
        grid=(4, depth // tile),
        in_specs=[pl.BlockSpec((rows, tile), lambda i, j: (i, j)), AFTER],
        out_specs=pl.BlockSpec((rows, 2 * tile), lambda i, j: (i, j)),
        out_shape=jax.ShapeDtypeStruct((receivers, 2 * depth), jnp.bfloat16),
        compiler_params=pltpu.CompilerParams(vmem_limit_bytes=VMEM_LIMIT),
        cost_estimate=pl.CostEstimate(flops=0, bytes_accessed=8 * receivers * depth, transcendentals=0),
        name="band_halves",
    )(band, after)


def multiply(band_ref, slip):
    members = slip.shape[0]
    high, low = halves(slip)
    both = jnp.concatenate([high, low], axis=0)
    mixed = lax.dot_general(
        band_ref[...], jnp.concatenate([both, both], axis=1), OVER_LAST, preferred_element_type=jnp.float32
    )
    return mixed[:, :members] + mixed[:, members:]


def accumulate(total_scr, band_ref, slip):
    step = pl.program_id(0)
    now = multiply(band_ref, slip)

    @pl.when(step == 0)
    def _():
        total_scr[...] = now

    @pl.when(step > 0)
    def _():
        total_scr[...] += now


def in_order(me_ref, ks, slip_refs, slip_scr):
    rows = slip_refs[0].shape[0]
    for k, ref in zip(ks, slip_refs):
        place = pl.multiple_of(((me_ref[0] ^ k) >> 1) * rows, 8)
        slip_scr[pl.ds(place, rows), :] = ref[...]
    return slip_scr[...]


def like_product_kernel(ks, me_ref, band_ref, *refs):
    slip_refs, (after_ref, out_ref, slip_scr) = refs[: len(ks)], refs[len(ks) :]
    del after_ref
    accumulate(out_ref, band_ref, in_order(me_ref, ks, slip_refs, slip_scr))


def part_rows(me_ref, kept_ref, given_ref, parts, crossed):
    pairs, own, _ = kept_ref.shape
    mine = me_ref[0] & 1
    for pair in range(pairs):
        for out_ref, order, parity in ((kept_ref, parts, mine), (given_ref, crossed, 1 - mine)):
            rows = pl.ds(pl.multiple_of((2 * pair + parity) * own, 8), own)
            out_ref[pair] = jnp.concatenate([ref[rows, :] for ref in order], axis=1)


def unlike_product_kernel(ks, me_ref, band_ref, *refs):
    slip_refs, (like_ref, kept_ref, given_ref, slip_scr, total_scr) = refs[: len(ks)], refs[len(ks) :]
    accumulate(total_scr, band_ref, in_order(me_ref, ks, slip_refs, slip_scr))

    @pl.when(pl.program_id(0) == pl.num_programs(0) - 1)
    def _():
        part_rows(me_ref, kept_ref, given_ref, (like_ref, total_scr), (total_scr, like_ref))


def last_product_kernel(me_ref, band_ref, slip_ref, after_ref, kept_ref, given_ref, total_scr):
    del after_ref
    accumulate(total_scr, band_ref, slip_ref[...])

    @pl.when(pl.program_id(0) == pl.num_programs(0) - 1)
    def _():
        part_rows(me_ref, kept_ref, given_ref, (total_scr,), (total_scr,))


def product(kernel, name, me, band, slip, slip_specs, extra, extra_spec, members, ways, scratch, weight, columns=None):
    receivers, depth = band.shape[0], band.shape[1] // 2
    tile = min(TILE, depth)
    if columns is None:
        shape, many = (receivers, members), 1
    else:
        shape, many = (ways // 2, receivers // ways, columns), 2
    out = pl.BlockSpec(shape, lambda i, me_ref: (0,) * len(shape))
    outs = pl.pallas_call(
        kernel,
        grid_spec=pltpu.PrefetchScalarGridSpec(
            num_scalar_prefetch=1,
            grid=(depth // tile,),
            in_specs=[pl.BlockSpec((receivers, 2 * tile), lambda i, me_ref: (0, i)), *slip_specs, extra_spec],
            out_specs=[out] * many,
            scratch_shapes=[pltpu.VMEM(rows_columns, jnp.float32) for rows_columns in scratch],
        ),
        out_shape=[jax.ShapeDtypeStruct(shape, jnp.float32)] * many,
        compiler_params=pltpu.CompilerParams(vmem_limit_bytes=VMEM_LIMIT),
        cost_estimate=pl.CostEstimate(
            flops=weight * 8 * receivers * depth * members,
            bytes_accessed=4 * (receivers * depth + members * depth),
            transcendentals=0,
        ),
        name=name,
    )(me, band, *slip, extra)
    return outs if many == 2 else outs[0]


def first_products(me, band, slip_field, got, ways, after):
    receivers, depth = band.shape[0], band.shape[1] // 2
    tile = min(TILE, depth)
    rows = got[2].shape[0]
    members, steps = ways // 2 * rows, depth // tile
    mine = pl.BlockSpec((rows, tile), lambda i, me_ref: (0, me_ref[0] * steps + i))
    block = pl.BlockSpec((rows, tile), lambda i, me_ref: (0, i))
    even, odd = list(range(0, ways, 2)), list(range(1, ways, 2))
    like = product(
        functools.partial(like_product_kernel, even), "like_product", me, band,
        [slip_field] + [got[k] for k in even[1:]], [mine] + [block] * (len(even) - 1), after, AFTER,
        members, ways, [(members, tile)], 1,
    )
    whole = pl.BlockSpec((receivers, members), lambda i, me_ref: (0, 0))
    return like, lambda: product(
        functools.partial(unlike_product_kernel, odd), "unlike_product", me, band,
        [got[k] for k in odd], [block] * len(odd), like, whole,
        members, ways, [(members, tile), (receivers, members)], FIRST_WEIGHT, 2 * members,
    )


def last_product(me, band, slip, after, ways):
    receivers, depth = band.shape[0], band.shape[1] // 2
    members = slip.shape[0]
    spec = pl.BlockSpec((members, min(TILE, depth)), lambda i, me_ref: (0, i))
    return product(
        last_product_kernel, "last_product", me, band, [slip], [spec], after, AFTER,
        members, ways, [(receivers, members)], 1, members,
    )


def fold_kernel(me_ref, kept_ref, came_ref, *out_refs):
    for k, out_ref in enumerate(out_refs):
        pair = (me_ref[0] >> 1) ^ k
        out_ref[...] = kept_ref[pair] + came_ref[pair]


def last_sums(me, kept, given, ways):
    pairs = ways // 2
    shape = jax.ShapeDtypeStruct(kept.shape[1:], jnp.float32)
    blocks = pl.pallas_call(
        fold_kernel,
        in_specs=[SCALARS, WHOLE, WHOLE],
        out_specs=[WHOLE] * pairs,
        out_shape=[shape] * pairs,
        name="pair_sums",
    )(me, kept, swap(given, 1, ways))
    return [blocks[0]] + [swap(blocks[k], 2 * k, ways) for k in range(1, pairs)]


def pack_kernel(to_ref, slip_ref, *refs):
    del to_ref
    out_ref = refs[-1]
    out_ref[...] = slip_ref[...]


def pack(to, slip_field, rows, depth, after):
    return pl.pallas_call(
        pack_kernel,
        grid_spec=pltpu.PrefetchScalarGridSpec(
            num_scalar_prefetch=1,
            grid=(1,),
            in_specs=[pl.BlockSpec((rows, depth), lambda i, to_ref: (0, to_ref[0]))] + [AFTER] * len(after),
            out_specs=pl.BlockSpec((rows, depth), lambda i, to_ref: (0, 0)),
        ),
        out_shape=jax.ShapeDtypeStruct((rows, depth), jnp.float32),
        cost_estimate=pl.CostEstimate(flops=0, bytes_accessed=8 * rows * depth, transcendentals=0),
        name="pack_block",
    )(to, slip_field, *after)


def pack_all_kernel(slip_ref, riders_ref, *refs):
    out_ref = refs[-1]
    depth = slip_ref.shape[1]
    out_ref[0, :, pl.ds(0, depth)] = slip_ref[...]
    out_ref[0, :, pl.ds(depth, riders_ref.shape[2])] = riders_ref[0]


def pack_all(slip_field, start, rows, riders, after):
    ways, _, width = riders.shape
    depth = slip_field.shape[1] // ways
    return pl.pallas_call(
        pack_all_kernel,
        grid=(ways,),
        in_specs=[
            pl.BlockSpec((rows, depth), lambda i: (start // rows, i)),
            pl.BlockSpec((1, rows, width), lambda i: (i, 0, 0)),
        ]
        + [AFTER] * len(after),
        out_specs=pl.BlockSpec((1, rows, depth + width), lambda i: (i, 0, 0)),
        out_shape=jax.ShapeDtypeStruct((ways, rows, depth + width), jnp.float32),
        cost_estimate=pl.CostEstimate(flops=0, bytes_accessed=8 * ways * rows * (depth + width), transcendentals=0),
        name="pack_all",
    )(slip_field, riders, *after)


def gather_kernel(elements_ref, slip_ref, after_ref, out_ref, tiles, sems):
    del after_ref
    groups = out_ref.shape[1] // LANES

    def fetch(g):
        def one(j, carry):
            first = pl.multiple_of((elements_ref[g * LANES + j] >> 7) << 7, LANES)
            pltpu.make_async_copy(slip_ref.at[:, pl.ds(first, LANES)], tiles.at[g & 1, j], sems.at[g & 1]).start()
            return carry

        lax.fori_loop(0, LANES, one, 0, unroll=8)

    lanes = lax.broadcasted_iota(jnp.int32, tiles.shape[2:], 1)
    fetch(0)
    for g in range(groups):
        if g + 1 < groups:
            fetch(g + 1)
        slot = tiles.at[g & 1]
        pltpu.make_async_copy(slot, slot, sems.at[g & 1]).wait()

        def one(j, found, g=g, slot=slot):
            shift = (j - elements_ref[g * LANES + j]) & (LANES - 1)
            return jnp.where(lanes == j, pltpu.roll(slot[j], shift, axis=1), found)

        found = lax.fori_loop(0, LANES, one, jnp.zeros(tiles.shape[2:], jnp.float32), unroll=16)
        out_ref[:, pl.ds(g * LANES, LANES)] = found


def gather(elements, slip_field, after):
    members, count = slip_field.shape[0], elements.shape[0]
    return pl.pallas_call(
        gather_kernel,
        in_specs=[SCALARS, ANY, AFTER],
        out_specs=WHOLE,
        out_shape=jax.ShapeDtypeStruct((members, count), jnp.float32),
        scratch_shapes=[pltpu.VMEM((2, LANES, members, LANES), jnp.float32), pltpu.SemaphoreType.DMA((2,))],
        cost_estimate=pl.CostEstimate(flops=0, bytes_accessed=4 * members * LANES * count, transcendentals=0),
        name="slip_at_receivers",
    )(elements, slip_field, after)


def swap(x, bit, ways):
    return lax.ppermute(x, "src", [(i, i ^ bit) for i in range(ways)])


def owner_sums(kept, given, me, ways):
    _, own, columns = kept.shape
    bit = 1
    while True:
        came = swap(given, bit, ways)
        bit *= 2
        if bit >= ways:
            return [kept.reshape(own, columns), came.reshape(own, columns)], given
        pairs = (kept + came).reshape(ways // bit // 2, 2, own, columns)
        mine = (me // bit) & 1
        kept = lax.dynamic_index_in_dim(pairs, mine, 1, keepdims=False)
        given = lax.dynamic_index_in_dim(pairs, 1 - mine, 1, keepdims=False)


def spread(x, columns, place):
    shape = (x.shape[1], columns)
    wanted = place(lax.broadcasted_iota(jnp.int32, shape, 0))
    chosen = jnp.where(lax.broadcasted_iota(jnp.int32, shape, 1) == wanted, 1.0, 0.0).astype(jnp.float32)
    return lax.dot_general(
        x, chosen, (((1,), (0,)), ((), ())), precision=lax.Precision.HIGHEST, preferred_element_type=jnp.float32
    )


def upright(row):
    shape = (row.shape[1], row.shape[1])
    diagonal = lax.broadcasted_iota(jnp.int32, shape, 0) == lax.broadcasted_iota(jnp.int32, shape, 1)
    return jnp.sum(jnp.where(diagonal, row, 0.0), axis=1, keepdims=True)


def strength_kernel(static_ref, dynamic_ref, scale_ref, riders_ref, classes_ref, normal_ref, after_ref, out_ref):
    del after_ref
    ways, tail, width = riders_ref.shape
    own, columns = classes_ref.shape
    members = columns // ways
    turned = riders_ref[...].reshape(ways * tail, width).T
    groups = [turned[g * own : (g + 1) * own] for g in range(members // tail)]
    count = ways * tail
    slip = spread(
        jnp.concatenate(groups, axis=1),
        columns,
        lambda j: j % count // tail * members + j // count * tail + j % tail,
    )
    classes = classes_ref[...]
    zero = jnp.zeros(classes.shape, jnp.float32)
    mu_static, mu_dynamic, slip_scale = zero, zero, zero
    for index in range(static_ref.shape[0]):
        here = classes == index
        mu_static = jnp.where(here, static_ref[index], mu_static)
        mu_dynamic = jnp.where(here, dynamic_ref[index], mu_dynamic)
        slip_scale = jnp.where(here, scale_ref[index], slip_scale)
    weakening = jnp.maximum(1.0 - jnp.abs(slip) / slip_scale, 0.0)
    out_ref[...] = upright(normal_ref[...]) * (mu_dynamic + (mu_static - mu_dynamic) * weakening)


def strength(last, width, classes, normal, static, dynamic, scale, after):
    ways, tail, total = last.shape
    return pl.pallas_call(
        strength_kernel,
        grid=(1,),
        in_specs=[SCALARS] * 3
        + [pl.BlockSpec((ways, tail, width), lambda i: (0, 0, total // width - 1))]
        + [pl.BlockSpec(classes.shape, lambda i: (0, 0)), pl.BlockSpec((1, normal.shape[0]), lambda i: (0, 0)), AFTER],
        out_specs=pl.BlockSpec(classes.shape, lambda i: (0, 0)),
        out_shape=jax.ShapeDtypeStruct(classes.shape, jnp.float32),
        name="strength",
    )(static, dynamic, scale, last, classes, normal[None, :], after)


def slip_rate_kernel(ways, n_first, me_ref, load_ref, strength_ref, *refs):
    *term_refs, stress_ref, rate_ref = refs
    columns = stress_ref.shape[1]
    members = columns // ways
    last = sum(ref[...] for ref in term_refs[n_first:])
    tail = last.shape[1] // ways
    head = members - tail
    total = spread(last, columns, lambda j: j // tail * members + head + j % tail)
    if n_first:
        first = sum(ref[...] for ref in term_refs[:n_first])
        half = ways // 2 * head
        parity = me_ref[0] & 1
        total = total + spread(
            first,
            columns,
            lambda j: (j % half // head * 2 + (j // half ^ parity)) * members + j % half % head,
        )
    stress = upright(load_ref[...]) + total
    excess = (stress - strength_ref[...]) / 0.25
    stress_ref[...] = stress
    rate_ref[...] = jnp.maximum(excess, 0.0) + jnp.log1p(jnp.exp(-jnp.abs(excess)))


def slip_rate(ways, me, load, strong, first, last):
    terms = [*first, *last]
    shape = jax.ShapeDtypeStruct(strong.shape, jnp.float32)
    return pl.pallas_call(
        functools.partial(slip_rate_kernel, ways, len(first)),
        in_specs=[SCALARS] + [WHOLE] * (2 + len(terms)),
        out_specs=[WHOLE] * 2,
        out_shape=[shape, shape],
        name="slip_rate",
    )(me, load[None, :], strong, *terms)


def partners(ways):
    half, quarter = ways // 2, ways // 4
    order = []
    for parity in (0, 1):
        near = [k for k in [*range(quarter, half), *range(1, quarter)] if k % 2 == parity]
        for far in range(half + parity, ways, 2):
            order.append(far)
            if near:
                order.append(near.pop(0))
    return order


def shards(
    ways,
    kernel_band,
    slip_field,
    elements,
    classes,
    shear_load,
    normal_stress,
    static_friction,
    dynamic_friction,
    weakening_slip,
):
    me = lax.axis_index("src").astype(jnp.int32)
    here = me.reshape(1)
    members, total_elements = slip_field.shape
    depth = total_elements // ways
    own = classes.shape[0]
    tail = min(TAIL_ROWS, members)
    head = members - tail

    came, got, block = [slip_field] * IN_FLIGHT, {}, slip_field
    if head:
        for turn, k in enumerate(partners(ways)):
            block = pack(here ^ k, slip_field, head, depth, (came[-IN_FLIGHT], block))
            got[k] = swap(block, k, ways)
            came.append(got[k])
            if turn == 2:
                came[-1] = at_receivers = gather(elements, slip_field, came[-1])
            if turn == 4:
                came[-1] = band = split(kernel_band, came[-1])
            if turn == 7:
                came[-1], unlike = first_products(here, band, slip_field, got, ways, came[-1])
    else:
        at_receivers = gather(elements, slip_field, slip_field)
        band = split(kernel_band, slip_field)

    riders = at_receivers.reshape(members // tail, tail, ways, own)
    riders = riders.transpose(2, 1, 0, 3).reshape(ways, tail, -1)
    riders = jnp.pad(riders, ((0, 0), (0, 0), (0, -riders.shape[2] % LANES)))
    last = lax.all_to_all(pack_all(slip_field, head, tail, riders, (came[-IN_FLIGHT], block)), "src", 0, 0, tiled=True)

    first_terms, after = [], slip_field
    if head:
        first_terms, after = owner_sums(*unlike(), me, ways)
    kept, given = last_product(here, band, last.reshape(ways * tail, -1), after, ways)
    strong = strength(
        last, riders.shape[2], classes, normal_stress, static_friction, dynamic_friction, weakening_slip, given
    )
    return slip_rate(ways, here, shear_load, strong, first_terms, last_sums(here, kept, given, ways))


def solution(mesh):
    placed = (
        P("groups", "src"),
        P(("groups", "src"), None),
        P("groups"),
        P(("groups", "src"), None),
        P(("groups", "src")),
        P(("groups", "src")),
        P(),
        P(),
        P(),
    )
    return jax.shard_map(
        functools.partial(shards, mesh.shape["src"]),
        mesh=mesh,
        in_specs=placed,
        out_specs=(P(("groups", "src"), None), P(("groups", "src"), None)),
        check_vma=False,
    )
```

time: 532 us -> 417 us (0.78)
  blocking collectives: 369 us -> 0 us
  Pallas kernels: 0 us -> 154 us
  starting transfers between devices: 6.45 us -> 132 us
  waiting for transfers between devices: 6.55 us -> 121 us
  matrix products: 59.7 us -> 0 us
  local copies, waits for them, and re-layouts: 56.7 us -> 8.26 us
  other arithmetic: 18.2 us -> 0.15 us
  between operations: 14.2 us -> 0.86 us
    all_to_all x1 -> x0, blocking collectives: 369 us -> none  [shards(): lax.all_to_all(slip_field, 'src', split_axis=1, concat_axis=0, tiled=True)]
    pallas_call x0 -> x24, Pallas kernels: none -> 154 us  [the longest x3 62.6 us: product(): pl.pallas_call(kernel, grid_spec=pltpu.PrefetchScalarGridSpec(num_scalar_...]
    ppermute x0 -> x27, waiting for transfers between devices: none -> 116 us  [swap(): return lax.ppermute(x, 'src', [(i, i ^ bit) for i in range(ways)])]
    ppermute x0 -> x27, starting transfers between devices: none -> 108 us  [swap(): return lax.ppermute(x, 'src', [(i, i ^ bit) for i in range(ways)])]
    dot_general x1 -> x0, matrix products: 59.7 us -> none  [shards(): lax.dot_general(kernel_band, blocks, (((1,), (1,)), ((), ())), precision=...]
    unnamed x17 -> x40, local copies, waits for them, and re-layouts: 36.4 us -> 4.75 us
    select_n x2 -> x0, other arithmetic: 17.2 us -> none  [the longest x1 17 us: shards(): slip_rate = jax.nn.softplus((shear_stress - strength) / 0.25)]
    all_to_all x1, starting transfers between devices: 6.41 us -> 23.4 us  [shards(): lax.all_to_all(pack_all(slip_field, head, tail, riders, (came[-IN_FLIGHT]...]
  transfers between devices with their start and end apart: 2 -> 28, of which waited for: 2 -> 9; matrix products, arithmetic and copies ran while one was open for 10% -> 1% of each run, Pallas kernels for 0% -> 32%
where the time goes in v2:
time: 417 us; the launch traced here: 416 us
  Pallas kernels  154 us (37%)
  starting transfers between devices  132 us (32%)
  waiting for transfers between devices  121 us (29%)
  local copies, waits for them, and re-layouts  8.26 us (2%)
    ppermute x27, waiting for transfers between devices, swap(): return lax.ppermute(x, 'src', [(i, i ^ bit) for i in range(ways)])  116 us
    ppermute x27, starting transfers between devices, swap(): return lax.ppermute(x, 'src', [(i, i ^ bit) for i in range(ways)])  108 us
    pallas_call x3, Pallas kernels, product(): pl.pallas_call(kernel, grid_spec=pltpu.PrefetchScalarGridSpec(num_scalar_...  62.6 us
    pallas_call x15, Pallas kernels, pack(): pl.pallas_call(pack_kernel, grid_spec=pltpu.PrefetchScalarGridSpec(num_sc...  31.3 us
    pallas_call x1, Pallas kernels, split(): pl.pallas_call(split_kernel, grid=(4, depth // tile), in_specs=[pl.BlockS...  28.2 us
    all_to_all x1, starting transfers between devices, shards(): lax.all_to_all(pack_all(slip_field, head, tail, riders, (came[-IN_FLIGHT]...  23.4 us
    pallas_call x1, Pallas kernels, gather(): pl.pallas_call(gather_kernel, in_specs=[SCALARS, ANY, AFTER], out_specs=W...  14.2 us
    pallas_call x1, Pallas kernels, pack_all(): pl.pallas_call(pack_all_kernel, grid=(ways,), in_specs=[pl.BlockSpec((row...  10.2 us
  transfers between devices with their start and end apart: 28, of which 9 were waited for; matrix products, arithmetic and copies ran while one was open for 1% of the time, Pallas kernels for 32%

profile of v2, /device:TPU:0, one launch (start us, length us, event | category | flops | bytes accessed | tf_op | source)
XLA Modules:
  0.0 415.7 jit_solution(15255901276463810690)
XLA Ops:
  2.7 4.0 collective-permute-start.1
  16.0 27.1 %collective-permute-done.1.refs_0_.refs_4_ = f32[24,8192]{1,0:T(8,128)S(1)} collective-permute-done((f32[24,8192]{1,0:T(8,128)}, f32[24,8192]{1,0:T(8,128)S(1)}, u32[]{:S(2)}, u32[]{:S(2)}) %collective-permute-start.1) | collective-permute-done | bytes 786464 | tf_op jit(solution)/shard_map/ppermute | solution.py:281
  46.0 3.1 collective-permute-start.2
  52.2 7.0 %collective-permute-start.4 = (f32[24,8192]{1,0:T(8,128)}, f32[24,8192]{1,0:T(8,128)}, u32[]{:S(2)}, u32[]{:S(2)}) collective-permute-start(f32[24,8192]{1,0:T(8,128)} %pack_block.20.refs_1_), channel_id=1, source_target_pairs={{0,2},{1,3},{2,0},{3,1},{4,6},{5,7},{6,4},{7,5},{8,10},{9,11},{10,... | collective-permute-start | bytes 2359304 | tf_op jit(solution)/shard_map/ppermute | solution.py:281
  59.1 18.2 %collective-permute-done.after_ref.refs_5_ = f32[24,8192]{1,0:T(8,128)S(1)} collective-permute-done((f32[24,8192]{1,0:T(8,128)}, f32[24,8192]{1,0:T(8,128)S(1)}, u32[]{:S(2)}, u32[]{:S(2)}) %collective-permute-start) | collective-permute-done | bytes 786464 | tf_op jit(solution)/shard_map/ppermute | solution.py:281
  78.3 14.2 %slip_at_receivers.1.refs_0_ = f32[32,1024]{1,0:T(8,128)} custom-call(s32[1024]{0:T(1024)} %elements_ref.1, f32[32,131072]{1,0:T(8,128)} %slip_ref.33, f32[24,8192]{1,0:T(8,128)} %copy-done.4), custom_call_target="tpu_custom_call" | custom-call | bytes 16777216 | tf_op jit(solution)/shard_map/slip_at_receivers/pallas_call | solution.py:269
  94.5 3.5 collective-permute-start.6
  100.1 28.2 %band_halves.1.band_ref.refs_0_ = bf16[1024,16384]{1,0:T(8,128)(2,1)} custom-call(f32[1024,8192]{1,0:T(8,128)} %band_ref.1, f32[24,8192]{1,0:T(8,128)S(1)} %collective-permute-done.2.after_ref.refs_6_), custom_call_target="tpu_custom_call" | custom-call | bytes 67108864 | tf_op jit(solution)/shard_map/band_halves/pallas_call | solution.py:38
  130.4 42.9 %collective-permute-start.11 = (f32[24,8192]{1,0:T(8,128)}, f32[24,8192]{1,0:T(8,128)}, u32[]{:S(2)}, u32[]{:S(2)}) collective-permute-start(f32[24,8192]{1,0:T(8,128)} %pack_block.23.refs_1_), channel_id=1, source_target_pairs={{0,5},{1,4},{2,7},{3,6},{4,1},{5,0},{6,3},{7,2},{8,13},{9,12},{10,... | collective-permute-start | bytes 2359304 | tf_op jit(solution)/shard_map/ppermute | solution.py:281
  175.4 2.9 collective-permute-start.10
  182.0 23.9 %like_product.1.refs_0_.refs_8_ = f32[1024,192]{1,0:T(8,128)} custom-call(s32[1]{0:T(128)} %bitcast.me_ref, bf16[1024,16384]{1,0:T(8,128)(2,1)} %band_halves.1.band_ref.refs_0_, f32[32,131072]{1,0:T(8,128)} %slip_ref.33, f32[24,8192]{1,0:T(8,128)} %collective-permute-done.4.refs_1_.refs_0_, f32[24,8192]{1,0:T(8,128)S(1)} %copy-done.3, ...), custom_call_target="tpu_custom_call" | custom-call | flops 12884901888 | bytes 39845888 | tf_op jit(solution)/shard_map/like_product/pallas_call | solution.py:122
  213.5 14.4 %collective-permute-done.9.refs_0_.refs_3_ = f32[24,8192]{1,0:T(8,128)} collective-permute-done((f32[24,8192]{1,0:T(8,128)}, f32[24,8192]{1,0:T(8,128)}, u32[]{:S(2)}, u32[]{:S(2)}) %collective-permute-start.9) | collective-permute-done | bytes 786464 | tf_op jit(solution)/shard_map/ppermute | solution.py:281
  231.0 3.6 collective-permute-start.14
  237.5 8.2 %collective-permute-done.8.refs_0_.refs_6_ = f32[24,8192]{1,0:T(8,128)} collective-permute-done((f32[24,8192]{1,0:T(8,128)}, f32[24,8192]{1,0:T(8,128)}, u32[]{:S(2)}, u32[]{:S(2)}) %collective-permute-start.8) | collective-permute-done | bytes 786464 | tf_op jit(solution)/shard_map/ppermute | solution.py:281
  245.8 10.2 %pack_all.1 = f32[16,8,8448]{2,1,0:T(8,128)} custom-call(f32[32,131072]{1,0:T(8,128)} %slip_ref.33, f32[16,8,256]{2,1,0:T(8,128)} %reshape.36.riders_ref, f32[24,8192]{1,0:T(8,128)} %collective-permute-done.8.refs_0_.refs_6_, f32[24,8192]{1,0:T(8,128)} %pack_block.29.refs_1_), custom_call_target="tpu_custom_call" | custom-call | bytes 8650752 | tf_op jit(solution)/shard_map/pack_all/pallas_call | solution.py:224
  256.0 23.4 %all-to-all-start = ((f32[16,8,8448]{2,1,0:T(8,128)}), f32[16,8,8448]{2,1,0:T(8,128)}, u32[]{:S(2)}, u32[]{:S(2)}) async-start(f32[16,8,8448]{2,1,0:T(8,128)} %pack_all.1), calls=%async_computation | async-start | bytes 8650752 | tf_op jit(solution)/shard_map/all_to_all | solution.py:438
  279.4 23.6 %unlike_product.1 = (f32[8,64,384]{2,1,0:T(8,128)S(1)}, f32[8,64,384]{2,1,0:T(8,128)S(1)}) custom-call(s32[1]{0:T(128)} %bitcast.me_ref, bf16[1024,16384]{1,0:T(8,128)(2,1)} %band_halves.1.band_ref.refs_0_, f32[24,8192]{1,0:T(8,128)S(1)} %collective-permute-done.12.refs_0_, f32[24,8192]{1,0:T(8,128)S(1)} %collective-permute-done.13.refs_1_, ...), custom_call_target="tpu_custom_call" | custom-call | flops 128849018880 | bytes 39845888 | tf_op jit(solution)/shard_map/unlike_product/pallas_call | solution.py:122
  307.4 16.2 %collective-permute-done.16 = f32[4,64,384]{2,1,0:T(8,128)S(1)} collective-permute-done((f32[4,64,384]{2,1,0:T(8,128)S(1)}, f32[4,64,384]{2,1,0:T(8,128)S(1)}, u32[]{:S(2)}, u32[]{:S(2)}) %collective-permute-start.16) | collective-permute-done | bytes 393248 | tf_op jit(solution)/shard_map/ppermute | solution.py:281
  326.6 27.7 %collective-permute-done.17 = f32[2,64,384]{2,1,0:T(8,128)S(1)} collective-permute-done((f32[2,64,384]{2,1,0:T(8,128)S(1)}, f32[2,64,384]{2,1,0:T(8,128)S(1)}, u32[]{:S(2)}, u32[]{:S(2)}) %collective-permute-start.17) | collective-permute-done | bytes 196640 | tf_op jit(solution)/shard_map/ppermute | solution.py:281
  355.0 4.5 %all-to-all-done.riders_ref = f32[16,8,8448]{2,1,0:T(8,128)} async-done(((f32[16,8,8448]{2,1,0:T(8,128)}), f32[16,8,8448]{2,1,0:T(8,128)}, u32[]{:S(2)}, u32[]{:S(2)}) %all-to-all-start) | async-done | bytes 4325408 | tf_op jit(solution)/shard_map/all_to_all | solution.py:438
  359.5 15.0 %last_product.1 = (f32[8,64,128]{2,1,0:T(8,128)S(1)}, f32[8,64,128]{2,1,0:T(8,128)S(1)}) custom-call(s32[1]{0:T(128)} %bitcast.me_ref, bf16[1024,16384]{1,0:T(8,128)(2,1)} %band_halves.1.band_ref.refs_0_, f32[128,8448]{1,0:T(8,128)} %bitcast.4.slip_ref, f32[1,64,384]{2,1,0:T(8,128)S(1)} %get-tuple-element.27.after_ref), custom_call_target="tpu_custom_call" | custom-call | flops 8589934592 | bytes 37748736 | tf_op jit(solution)/shard_map/last_product/pallas_call | solution.py:122
  375.9 17.6 %collective-permute-start.18 = (f32[1,64,384]{2,1,0:T(8,128)S(1)}, f32[1,64,384]{2,1,0:T(8,128)S(1)}, u32[]{:S(2)}, u32[]{:S(2)}) collective-permute-start(f32[1,64,384]{2,1,0:T(8,128)S(1)} %get-tuple-element.27.after_ref), channel_id=1, source_target_pairs={{0,8},{1,9},{2,10},{3,11},{4,12},{5,13},{6,14},{7,15},{8,0},{9,1},... | collective-permute-start | bytes 294920 | tf_op jit(solution)/shard_map/ppermute | solution.py:281
  402.5 3.0 collective-permute-start.25
  412.9 2.9 slip_rate.1
  (105 shorter events, 69.5 us)
Async XLA Ops:
  2.7 40.4 %collective-permute-start.1 = (f32[24,8192]{1,0:T(8,128)}, f32[24,8192]{1,0:T(8,128)S(1)}, u32[]{:S(2)}, u32[]{:S(2)}) collective-permute-start(f32[24,8192]{1,0:T(8,128)} %pack_block.15.refs_1_), channel_id=1, source_target_pairs={{0,8},{1,9},{2,10},{3,11},{4,12},{5,13},{6,14},{7,15},{8,0},{9,1},... | collective-permute-start | bytes 2359304 | tf_op jit(solution)/shard_map/ppermute | solution.py:281
  8.8 40.3 %collective-permute-start.3 = (f32[24,8192]{1,0:T(8,128)}, f32[24,8192]{1,0:T(8,128)S(1)}, u32[]{:S(2)}, u32[]{:S(2)}) collective-permute-start(f32[24,8192]{1,0:T(8,128)} %pack_block.16.refs_1_), channel_id=1, source_target_pairs={{0,4},{1,5},{2,6},{3,7},{4,0},{5,1},{6,2},{7,3},{8,12},{9,13},{10,... | collective-permute-start | bytes 2359304 | tf_op jit(solution)/shard_map/ppermute | solution.py:281
  12.5 64.9 %collective-permute-start = (f32[24,8192]{1,0:T(8,128)}, f32[24,8192]{1,0:T(8,128)S(1)}, u32[]{:S(2)}, u32[]{:S(2)}) collective-permute-start(f32[24,8192]{1,0:T(8,128)} %pack_block.17.refs_1_), channel_id=1, source_target_pairs={{0,10},{1,11},{2,8},{3,9},{4,14},{5,15},{6,12},{7,13},{8,2},{9,3},... | collective-permute-start | bytes 2359304 | tf_op jit(solution)/shard_map/ppermute | solution.py:281
  15.9 82.1 %collective-permute-start.5 = (f32[24,8192]{1,0:T(8,128)}, f32[24,8192]{1,0:T(8,128)}, u32[]{:S(2)}, u32[]{:S(2)}) collective-permute-start(f32[24,8192]{1,0:T(8,128)} %pack_block.18.refs_1_), channel_id=1, source_target_pairs={{0,6},{1,7},{2,4},{3,5},{4,2},{5,3},{6,0},{7,1},{8,14},{9,15},{10,... | collective-permute-start | bytes 2359304 | tf_op jit(solution)/shard_map/ppermute | solution.py:281
  46.0 54.1 %collective-permute-start.2 = (f32[24,8192]{1,0:T(8,128)}, f32[24,8192]{1,0:T(8,128)S(1)}, u32[]{:S(2)}, u32[]{:S(2)}) collective-permute-start(f32[24,8192]{1,0:T(8,128)} %pack_block.19.refs_1_), channel_id=1, source_target_pairs={{0,12},{1,13},{2,14},{3,15},{4,8},{5,9},{6,10},{7,11},{8,4},{9,5},... | collective-permute-start | bytes 2359304 | tf_op jit(solution)/shard_map/ppermute | solution.py:281
  52.2 121.1 %collective-permute-start.4 = (f32[24,8192]{1,0:T(8,128)}, f32[24,8192]{1,0:T(8,128)}, u32[]{:S(2)}, u32[]{:S(2)}) collective-permute-start(f32[24,8192]{1,0:T(8,128)} %pack_block.20.refs_1_), channel_id=1, source_target_pairs={{0,2},{1,3},{2,0},{3,1},{4,6},{5,7},{6,4},{7,5},{8,10},{9,11},{10,... | collective-permute-start | bytes 2359304 | tf_op jit(solution)/shard_map/ppermute | solution.py:281
  94.5 83.8 %collective-permute-start.6 = (f32[24,8192]{1,0:T(8,128)}, f32[24,8192]{1,0:T(8,128)}, u32[]{:S(2)}, u32[]{:S(2)}) collective-permute-start(f32[24,8192]{1,0:T(8,128)} %pack_block.21.refs_1_), channel_id=1, source_target_pairs={{0,14},{1,15},{2,12},{3,13},{4,10},{5,11},{6,8},{7,9},{8,6},{9,7},... | collective-permute-start | bytes 2359304 | tf_op jit(solution)/shard_map/ppermute | solution.py:281
  100.1 81.8 %collective-permute-start.7 = (f32[24,8192]{1,0:T(8,128)}, f32[24,8192]{1,0:T(8,128)}, u32[]{:S(2)}, u32[]{:S(2)}) collective-permute-start(f32[24,8192]{1,0:T(8,128)} %pack_block.22.refs_1_), channel_id=1, source_target_pairs={{0,9},{1,8},{2,11},{3,10},{4,13},{5,12},{6,15},{7,14},{8,1},{9,0},... | collective-permute-start | bytes 2359304 | tf_op jit(solution)/shard_map/ppermute | solution.py:281
  130.4 78.8 %collective-permute-start.11 = (f32[24,8192]{1,0:T(8,128)}, f32[24,8192]{1,0:T(8,128)}, u32[]{:S(2)}, u32[]{:S(2)}) collective-permute-start(f32[24,8192]{1,0:T(8,128)} %pack_block.23.refs_1_), channel_id=1, source_target_pairs={{0,5},{1,4},{2,7},{3,6},{4,1},{5,0},{6,3},{7,2},{8,13},{9,12},{10,... | collective-permute-start | bytes 2359304 | tf_op jit(solution)/shard_map/ppermute | solution.py:281
  175.4 35.9 %collective-permute-start.10 = (f32[24,8192]{1,0:T(8,128)}, f32[24,8192]{1,0:T(8,128)}, u32[]{:S(2)}, u32[]{:S(2)}) collective-permute-start(f32[24,8192]{1,0:T(8,128)} %pack_block.24.refs_1_), channel_id=1, source_target_pairs={{0,11},{1,10},{2,9},{3,8},{4,15},{5,14},{6,13},{7,12},{8,3},{9,2},... | collective-permute-start | bytes 2359304 | tf_op jit(solution)/shard_map/ppermute | solution.py:281
  180.4 47.4 %collective-permute-start.9 = (f32[24,8192]{1,0:T(8,128)}, f32[24,8192]{1,0:T(8,128)}, u32[]{:S(2)}, u32[]{:S(2)}) collective-permute-start(f32[24,8192]{1,0:T(8,128)} %pack_block.25.refs_1_), channel_id=1, source_target_pairs={{0,7},{1,6},{2,5},{3,4},{4,3},{5,2},{6,1},{7,0},{8,15},{9,14},{10,... | collective-permute-start | bytes 2359304 | tf_op jit(solution)/shard_map/ppermute | solution.py:281
  208.0 37.7 %collective-permute-start.8 = (f32[24,8192]{1,0:T(8,128)}, f32[24,8192]{1,0:T(8,128)}, u32[]{:S(2)}, u32[]{:S(2)}) collective-permute-start(f32[24,8192]{1,0:T(8,128)} %pack_block.26.refs_1_), channel_id=1, source_target_pairs={{0,13},{1,12},{2,15},{3,14},{4,9},{5,8},{6,11},{7,10},{8,5},{9,4},... | collective-permute-start | bytes 2359304 | tf_op jit(solution)/shard_map/ppermute | solution.py:281
  229.9 49.5 %collective-permute-start.13 = (f32[24,8192]{1,0:T(8,128)}, f32[24,8192]{1,0:T(8,128)S(1)}, u32[]{:S(2)}, u32[]{:S(2)}) collective-permute-start(f32[24,8192]{1,0:T(8,128)} %pack_block.29.refs_1_), channel_id=1, source_target_pairs={{0,3},{1,2},{2,1},{3,0},{4,7},{5,6},{6,5},{7,4},{8,11},{9,10},{10,... | collective-permute-start | bytes 2359304 | tf_op jit(solution)/shard_map/ppermute | solution.py:281
  231.0 48.4 %collective-permute-start.14 = (f32[24,8192]{1,0:T(8,128)S(1)}, f32[24,8192]{1,0:T(8,128)}, u32[]{:S(2)}, u32[]{:S(2)}) collective-permute-start(f32[24,8192]{1,0:T(8,128)S(1)} %copy-done.9), channel_id=1, source_target_pairs={{0,15},{1,14},{2,13},{3,12},{4,11},{5,10},{6,9},{7,8},{8,7},{9,6},... | collective-permute-start | bytes 2359304 | tf_op jit(solution)/shard_map/ppermute | solution.py:281
  234.7 44.8 %collective-permute-start.12 = (f32[24,8192]{1,0:T(8,128)S(1)}, f32[24,8192]{1,0:T(8,128)S(1)}, u32[]{:S(2)}, u32[]{:S(2)}) collective-permute-start(f32[24,8192]{1,0:T(8,128)S(1)} %copy-done.8), channel_id=1, source_target_pairs={{0,1},{1,0},{2,3},{3,2},{4,5},{5,4},{6,7},{7,6},{8,9},{9,8},{10,11... | collective-permute-start | bytes 2359304 | tf_op jit(solution)/shard_map/ppermute | solution.py:281
  256.0 103.5 %all-to-all-start = ((f32[16,8,8448]{2,1,0:T(8,128)}), f32[16,8,8448]{2,1,0:T(8,128)}, u32[]{:S(2)}, u32[]{:S(2)}) async-start(f32[16,8,8448]{2,1,0:T(8,128)} %pack_all.1), calls=%async_computation | async-start | bytes 8650752 | tf_op jit(solution)/shard_map/all_to_all | solution.py:438
  305.5 18.2 %collective-permute-start.16 = (f32[4,64,384]{2,1,0:T(8,128)S(1)}, f32[4,64,384]{2,1,0:T(8,128)S(1)}, u32[]{:S(2)}, u32[]{:S(2)}) collective-permute-start(f32[4,64,384]{2,1,0:T(8,128)S(1)} %dynamic-slice_bitcast_fusion), channel_id=1, source_target_pairs={{0,2},{1,3},{2,0},{3,1},{4,6},{5,7},{6,4},{7,5},{8,10},{9,11},{10,... | collective-permute-start | bytes 1179656 | tf_op jit(solution)/shard_map/ppermute | solution.py:281
  323.8 30.6 %collective-permute-start.17 = (f32[2,64,384]{2,1,0:T(8,128)S(1)}, f32[2,64,384]{2,1,0:T(8,128)S(1)}, u32[]{:S(2)}, u32[]{:S(2)}) collective-permute-start(f32[2,64,384]{2,1,0:T(8,128)S(1)} %dynamic-slice_bitcast_fusion.1), channel_id=1, source_target_pairs={{0,4},{1,5},{2,6},{3,7},{4,0},{5,1},{6,2},{7,3},{8,12},{9,13},{10,... | collective-permute-start | bytes 589832 | tf_op jit(solution)/shard_map/ppermute | solution.py:281
  375.2 18.2 %collective-permute-start.19 = (f32[8,64,128]{2,1,0:T(8,128)S(1)}, f32[8,64,128]{2,1,0:T(8,128)S(1)}, u32[]{:S(2)}, u32[]{:S(2)}) collective-permute-start(f32[8,64,128]{2,1,0:T(8,128)S(1)} %get-tuple-element.16.after_ref), channel_id=1, source_target_pairs={{0,1},{1,0},{2,3},{3,2},{4,5},{5,4},{6,7},{7,6},{8,9},{9,8},{10,11... | collective-permute-start | bytes 786440 | tf_op jit(solution)/shard_map/ppermute | solution.py:281
  375.9 25.0 %collective-permute-start.18 = (f32[1,64,384]{2,1,0:T(8,128)S(1)}, f32[1,64,384]{2,1,0:T(8,128)S(1)}, u32[]{:S(2)}, u32[]{:S(2)}) collective-permute-start(f32[1,64,384]{2,1,0:T(8,128)S(1)} %get-tuple-element.27.after_ref), channel_id=1, source_target_pairs={{0,8},{1,9},{2,10},{3,11},{4,12},{5,13},{6,14},{7,15},{8,0},{9,1},... | collective-permute-start | bytes 294920 | tf_op jit(solution)/shard_map/ppermute | solution.py:281
  395.9 9.5 %collective-permute-start.21 = (f32[64,128]{1,0:T(8,128)}, f32[64,128]{1,0:T(8,128)S(1)}, u32[]{:S(2)}, u32[]{:S(2)}) collective-permute-start(f32[64,128]{1,0:T(8,128)} %get-tuple-element.20), channel_id=1, source_target_pairs={{0,4},{1,5},{2,6},{3,7},{4,0},{5,1},{6,2},{7,3},{8,12},{9,13},{10,... | collective-permute-start | bytes 98312 | tf_op jit(solution)/shard_map/ppermute | solution.py:281
  398.6 11.0 %collective-permute-start.22 = (f32[64,128]{1,0:T(8,128)}, f32[64,128]{1,0:T(8,128)S(1)}, u32[]{:S(2)}, u32[]{:S(2)}) collective-permute-start(f32[64,128]{1,0:T(8,128)} %get-tuple-element.21), channel_id=1, source_target_pairs={{0,6},{1,7},{2,4},{3,5},{4,2},{5,3},{6,0},{7,1},{8,14},{9,15},{10,... | collective-permute-start | bytes 98312 | tf_op jit(solution)/shard_map/ppermute | solution.py:281
  399.4 10.3 %collective-permute-start.23 = (f32[64,128]{1,0:T(8,128)}, f32[64,128]{1,0:T(8,128)S(1)}, u32[]{:S(2)}, u32[]{:S(2)}) collective-permute-start(f32[64,128]{1,0:T(8,128)} %get-tuple-element.22), channel_id=1, source_target_pairs={{0,8},{1,9},{2,10},{3,11},{4,12},{5,13},{6,14},{7,15},{8,0},{9,1},... | collective-permute-start | bytes 98312 | tf_op jit(solution)/shard_map/ppermute | solution.py:281
  400.9 8.8 %collective-permute-start.24 = (f32[64,128]{1,0:T(8,128)}, f32[64,128]{1,0:T(8,128)S(1)}, u32[]{:S(2)}, u32[]{:S(2)}) collective-permute-start(f32[64,128]{1,0:T(8,128)} %get-tuple-element.23), channel_id=1, source_target_pairs={{0,10},{1,11},{2,8},{3,9},{4,14},{5,15},{6,12},{7,13},{8,2},{9,3},... | collective-permute-start | bytes 98312 | tf_op jit(solution)/shard_map/ppermute | solution.py:281
  (24 other events, 316.9 us)

commit v3 on v2

--- a/solution.py
+++ b/solution.py
@@ -8,6 +8,7 @@
 from jax.sharding import PartitionSpec as P
 
 VMEM_LIMIT = 48 * 1024 * 1024
+SMALL = pltpu.CompilerParams(vmem_limit_bytes=8 * 1024 * 1024)
 TAIL_ROWS = 8
 IN_FLIGHT = 4
 TILE = 2048
@@ -102,8 +103,8 @@
         part_rows(me_ref, kept_ref, given_ref, (like_ref, total_scr), (total_scr, like_ref))
 
 
-def last_product_kernel(me_ref, band_ref, slip_ref, after_ref, kept_ref, given_ref, total_scr):
-    del after_ref
+def last_product_kernel(me_ref, band_ref, slip_ref, *refs):
+    kept_ref, given_ref, total_scr = refs[-3:]
     accumulate(total_scr, band_ref, slip_ref[...])
 
     @pl.when(pl.program_id(0) == pl.num_programs(0) - 1)
@@ -111,7 +112,7 @@
         part_rows(me_ref, kept_ref, given_ref, (total_scr,), (total_scr,))
 
 
-def product(kernel, name, me, band, slip, slip_specs, extra, extra_spec, members, ways, scratch, weight, columns=None):
+def product(kernel, name, me, band, slip, slip_specs, extra, extra_specs, members, ways, scratch, weight, columns=None):
     receivers, depth = band.shape[0], band.shape[1] // 2
     tile = min(TILE, depth)
     if columns is None:
@@ -124,7 +125,7 @@
         grid_spec=pltpu.PrefetchScalarGridSpec(
             num_scalar_prefetch=1,
             grid=(depth // tile,),
-            in_specs=[pl.BlockSpec((receivers, 2 * tile), lambda i, me_ref: (0, i)), *slip_specs, extra_spec],
+            in_specs=[pl.BlockSpec((receivers, 2 * tile), lambda i, me_ref: (0, i)), *slip_specs, *extra_specs],
             out_specs=[out] * many,
             scratch_shapes=[pltpu.VMEM(rows_columns, jnp.float32) for rows_columns in scratch],
         ),
@@ -136,7 +137,7 @@
             transcendentals=0,
         ),
         name=name,
-    )(me, band, *slip, extra)
+    )(me, band, *slip, *extra)
     return outs if many == 2 else outs[0]
 
 
@@ -150,13 +151,13 @@
     even, odd = list(range(0, ways, 2)), list(range(1, ways, 2))
     like = product(
         functools.partial(like_product_kernel, even), "like_product", me, band,
-        [slip_field] + [got[k] for k in even[1:]], [mine] + [block] * (len(even) - 1), after, AFTER,
+        [slip_field] + [got[k] for k in even[1:]], [mine] + [block] * (len(even) - 1), [after], [AFTER],
         members, ways, [(members, tile)], 1,
     )
     whole = pl.BlockSpec((receivers, members), lambda i, me_ref: (0, 0))
     return like, lambda: product(
         functools.partial(unlike_product_kernel, odd), "unlike_product", me, band,
-        [got[k] for k in odd], [block] * len(odd), like, whole,
+        [got[k] for k in odd], [block] * len(odd), [like], [whole],
         members, ways, [(members, tile), (receivers, members)], FIRST_WEIGHT, 2 * members,
     )
 
@@ -166,7 +167,7 @@
     members = slip.shape[0]
     spec = pl.BlockSpec((members, min(TILE, depth)), lambda i, me_ref: (0, i))
     return product(
-        last_product_kernel, "last_product", me, band, [slip], [spec], after, AFTER,
+        last_product_kernel, "last_product", me, band, [slip], [spec], after, [ANY] * len(after),
         members, ways, [(receivers, members)], 1, members,
     )
 
@@ -185,6 +186,7 @@
         in_specs=[SCALARS, WHOLE, WHOLE],
         out_specs=[WHOLE] * pairs,
         out_shape=[shape] * pairs,
+        compiler_params=SMALL,
         name="pair_sums",
     )(me, kept, swap(given, 1, ways))
     return [blocks[0]] + [swap(blocks[k], 2 * k, ways) for k in range(1, pairs)]
@@ -295,13 +297,19 @@
         given = lax.dynamic_index_in_dim(pairs, 1 - mine, 1, keepdims=False)
 
 
-def spread(x, columns, place):
-    shape = (x.shape[1], columns)
-    wanted = place(lax.broadcasted_iota(jnp.int32, shape, 0))
-    chosen = jnp.where(lax.broadcasted_iota(jnp.int32, shape, 1) == wanted, 1.0, 0.0).astype(jnp.float32)
-    return lax.dot_general(
-        x, chosen, (((1,), (0,)), ((), ())), precision=lax.Precision.HIGHEST, preferred_element_type=jnp.float32
-    )
+def place(count, columns, where):
+    shape = (count, columns)
+    wanted = where(lax.broadcasted_iota(jnp.int32, shape, 0))
+    return jnp.where(lax.broadcasted_iota(jnp.int32, shape, 1) == wanted, 1.0, 0.0).astype(jnp.bfloat16)
+
+
+def moved(x, places):
+    rows = x.shape[0]
+    high, rest = halves(x)
+    middle = rest.astype(jnp.float32)
+    low = (x - high.astype(jnp.float32) - middle).astype(jnp.bfloat16)
+    parts = jnp.dot(jnp.concatenate([high, rest, low], axis=0), places, preferred_element_type=jnp.float32)
+    return parts[:rows] + (parts[rows : 2 * rows] + parts[2 * rows :])
 
 
 def upright(row):
@@ -318,11 +326,8 @@
     turned = riders_ref[...].reshape(ways * tail, width).T
     groups = [turned[g * own : (g + 1) * own] for g in range(members // tail)]
     count = ways * tail
-    slip = spread(
-        jnp.concatenate(groups, axis=1),
-        columns,
-        lambda j: j % count // tail * members + j // count * tail + j % tail,
-    )
+    places = place(columns, columns, lambda j: j % count // tail * members + j // count * tail + j % tail)
+    slip = moved(jnp.concatenate(groups, axis=1), places)
     classes = classes_ref[...]
     zero = jnp.zeros(classes.shape, jnp.float32)
     mu_static, mu_dynamic, slip_scale = zero, zero, zero
@@ -335,53 +340,43 @@
     out_ref[...] = upright(normal_ref[...]) * (mu_dynamic + (mu_static - mu_dynamic) * weakening)
 
 
-def strength(last, width, classes, normal, static, dynamic, scale, after):
-    ways, tail, total = last.shape
+def strength(came, width, classes, normal, static, dynamic, scale, after):
+    ways, tail, total = came.shape
     return pl.pallas_call(
         strength_kernel,
         grid=(1,),
         in_specs=[SCALARS] * 3
         + [pl.BlockSpec((ways, tail, width), lambda i: (0, 0, total // width - 1))]
-        + [pl.BlockSpec(classes.shape, lambda i: (0, 0)), pl.BlockSpec((1, normal.shape[0]), lambda i: (0, 0)), AFTER],
+        + [pl.BlockSpec(classes.shape, lambda i: (0, 0)), pl.BlockSpec((1, normal.shape[0]), lambda i: (0, 0)), ANY],
         out_specs=pl.BlockSpec(classes.shape, lambda i: (0, 0)),
         out_shape=jax.ShapeDtypeStruct(classes.shape, jnp.float32),
+        compiler_params=SMALL,
         name="strength",
-    )(static, dynamic, scale, last, classes, normal[None, :], after)
-
-
-def slip_rate_kernel(ways, n_first, me_ref, load_ref, strength_ref, *refs):
+    )(static, dynamic, scale, came, classes, normal[None, :], after)
+
+
+def slip_rate_kernel(n_first, load_ref, strength_ref, places_ref, *refs):
     *term_refs, stress_ref, rate_ref = refs
-    columns = stress_ref.shape[1]
-    members = columns // ways
-    last = sum(ref[...] for ref in term_refs[n_first:])
-    tail = last.shape[1] // ways
-    head = members - tail
-    total = spread(last, columns, lambda j: j // tail * members + head + j % tail)
+    total = sum(ref[...] for ref in term_refs[n_first:])
     if n_first:
-        first = sum(ref[...] for ref in term_refs[:n_first])
-        half = ways // 2 * head
-        parity = me_ref[0] & 1
-        total = total + spread(
-            first,
-            columns,
-            lambda j: (j % half // head * 2 + (j // half ^ parity)) * members + j % half % head,
-        )
-    stress = upright(load_ref[...]) + total
+        total = jnp.concatenate([sum(ref[...] for ref in term_refs[:n_first]), total], axis=1)
+    stress = upright(load_ref[...]) + moved(total, places_ref[...])
     excess = (stress - strength_ref[...]) / 0.25
     stress_ref[...] = stress
     rate_ref[...] = jnp.maximum(excess, 0.0) + jnp.log1p(jnp.exp(-jnp.abs(excess)))
 
 
-def slip_rate(ways, me, load, strong, first, last):
+def slip_rate(load, strong, places, first, last):
     terms = [*first, *last]
     shape = jax.ShapeDtypeStruct(strong.shape, jnp.float32)
     return pl.pallas_call(
-        functools.partial(slip_rate_kernel, ways, len(first)),
-        in_specs=[SCALARS] + [WHOLE] * (2 + len(terms)),
+        functools.partial(slip_rate_kernel, len(first)),
+        in_specs=[WHOLE] * (3 + len(terms)),
         out_specs=[WHOLE] * 2,
         out_shape=[shape, shape],
+        compiler_params=SMALL,
         name="slip_rate",
-    )(me, load[None, :], strong, *terms)
+    )(load[None, :], strong, places, *terms)
 
 
 def partners(ways):
@@ -440,11 +435,20 @@
     first_terms, after = [], slip_field
     if head:
         first_terms, after = owner_sums(*unlike(), me, ways)
-    kept, given = last_product(here, band, last.reshape(ways * tail, -1), after, ways)
+    places = place(ways * tail, ways * members, lambda j: j // tail * members + head + j % tail)
+    if head:
+        half = ways // 2 * head
+        first_places = place(
+            ways * head,
+            ways * members,
+            lambda j: (j % half // head * 2 + (j // half ^ (me & 1))) * members + j % half % head,
+        )
+        places = jnp.concatenate([first_places, places], axis=0)
+    kept, given = last_product(here, band, last.reshape(ways * tail, -1), (after, places), ways)
     strong = strength(
         last, riders.shape[2], classes, normal_stress, static_friction, dynamic_friction, weakening_slip, given
     )
-    return slip_rate(ways, here, shear_load, strong, first_terms, last_sums(here, kept, given, ways))
+    return slip_rate(shear_load, strong, places, first_terms, last_sums(here, kept, given, ways))
 
 
 def solution(mesh):

time: 417 us -> 412 us (0.988)
  Pallas kernels: 154 us -> 149 us
  transfers between devices with their start and end apart: 28 -> 28, of which waited for: 9 -> 10; matrix products, arithmetic and copies ran while one was open for 1% -> 1% of each run, Pallas kernels for 32% -> 32%
where the time goes in v3:
time: 412 us; the launch traced here: 410 us
  Pallas kernels  149 us (36%)
  starting transfers between devices  132 us (32%)
  waiting for transfers between devices  122 us (30%)
  local copies, waits for them, and re-layouts  5.65 us (1%)
    ppermute x27, waiting for transfers between devices, swap(): return lax.ppermute(x, 'src', [(i, i ^ bit) for i in range(ways)])  117 us
    ppermute x27, starting transfers between devices, swap(): return lax.ppermute(x, 'src', [(i, i ^ bit) for i in range(ways)])  108 us
    pallas_call x3, Pallas kernels, product(): pl.pallas_call(kernel, grid_spec=pltpu.PrefetchScalarGridSpec(num_scalar_...  62.7 us
    pallas_call x15, Pallas kernels, pack(): pl.pallas_call(pack_kernel, grid_spec=pltpu.PrefetchScalarGridSpec(num_sc...  31.3 us
    pallas_call x1, Pallas kernels, split(): pl.pallas_call(split_kernel, grid=(4, depth // tile), in_specs=[pl.BlockS...  28.2 us
    all_to_all x1, starting transfers between devices, shards(): lax.all_to_all(pack_all(slip_field, head, tail, riders, (came[-IN_FLIGHT]...  23.4 us
    pallas_call x1, Pallas kernels, gather(): pl.pallas_call(gather_kernel, in_specs=[SCALARS, ANY, AFTER], out_specs=W...  14.2 us
    pallas_call x1, Pallas kernels, pack_all(): pl.pallas_call(pack_all_kernel, grid=(ways,), in_specs=[pl.BlockSpec((row...  10.2 us
  transfers between devices with their start and end apart: 28, of which 10 were waited for; matrix products, arithmetic and copies ran while one was open for 1% of the time, Pallas kernels for 32%

profile of v3, /device:TPU:0, one launch (start us, length us, event | category | flops | bytes accessed | tf_op | source)
XLA Modules:
  0.0 410.2 jit_solution(6640606640954083479)
XLA Ops:
  2.7 4.0 collective-permute-start.1
  16.0 27.1 %collective-permute-done.1.refs_0_.refs_4_ = f32[24,8192]{1,0:T(8,128)S(1)} collective-permute-done((f32[24,8192]{1,0:T(8,128)}, f32[24,8192]{1,0:T(8,128)S(1)}, u32[]{:S(2)}, u32[]{:S(2)}) %collective-permute-start.1) | collective-permute-done | bytes 786464 | tf_op jit(solution)/shard_map/ppermute | solution.py:283
  46.0 3.1 collective-permute-start.2
  52.1 6.9 %collective-permute-start.4 = (f32[24,8192]{1,0:T(8,128)}, f32[24,8192]{1,0:T(8,128)}, u32[]{:S(2)}, u32[]{:S(2)}) collective-permute-start(f32[24,8192]{1,0:T(8,128)} %pack_block.20.refs_1_), channel_id=1, source_target_pairs={{0,2},{1,3},{2,0},{3,1},{4,6},{5,7},{6,4},{7,5},{8,10},{9,11},{10,... | collective-permute-start | bytes 2359304 | tf_op jit(solution)/shard_map/ppermute | solution.py:283
  59.1 18.3 %collective-permute-done.after_ref.refs_5_ = f32[24,8192]{1,0:T(8,128)S(1)} collective-permute-done((f32[24,8192]{1,0:T(8,128)}, f32[24,8192]{1,0:T(8,128)S(1)}, u32[]{:S(2)}, u32[]{:S(2)}) %collective-permute-start) | collective-permute-done | bytes 786464 | tf_op jit(solution)/shard_map/ppermute | solution.py:283
  78.3 14.2 %slip_at_receivers.1.refs_0_ = f32[32,1024]{1,0:T(8,128)} custom-call(s32[1024]{0:T(1024)} %elements_ref.1, f32[32,131072]{1,0:T(8,128)} %slip_ref.33, f32[24,8192]{1,0:T(8,128)} %copy-done.4), custom_call_target="tpu_custom_call" | custom-call | bytes 16777216 | tf_op jit(solution)/shard_map/slip_at_receivers/pallas_call | solution.py:271
  94.5 3.5 collective-permute-start.6
  100.1 28.2 %band_halves.1.band_ref.refs_0_ = bf16[1024,16384]{1,0:T(8,128)(2,1)} custom-call(f32[1024,8192]{1,0:T(8,128)} %band_ref.1, f32[24,8192]{1,0:T(8,128)S(1)} %collective-permute-done.2.after_ref.refs_6_), custom_call_target="tpu_custom_call" | custom-call | bytes 67108864 | tf_op jit(solution)/shard_map/band_halves/pallas_call | solution.py:39
  130.4 42.9 %collective-permute-start.11 = (f32[24,8192]{1,0:T(8,128)}, f32[24,8192]{1,0:T(8,128)}, u32[]{:S(2)}, u32[]{:S(2)}) collective-permute-start(f32[24,8192]{1,0:T(8,128)} %pack_block.23.refs_1_), channel_id=1, source_target_pairs={{0,5},{1,4},{2,7},{3,6},{4,1},{5,0},{6,3},{7,2},{8,13},{9,12},{10,... | collective-permute-start | bytes 2359304 | tf_op jit(solution)/shard_map/ppermute | solution.py:283
  175.4 2.9 collective-permute-start.10
  181.9 23.9 %like_product.1.refs_0_.refs_8_ = f32[1024,192]{1,0:T(8,128)} custom-call(s32[1]{0:T(128)} %bitcast.1.me_ref, bf16[1024,16384]{1,0:T(8,128)(2,1)} %band_halves.1.band_ref.refs_0_, f32[32,131072]{1,0:T(8,128)} %slip_ref.33, f32[24,8192]{1,0:T(8,128)} %collective-permute-done.4.refs_1_.refs_0_, f32[24,8192]{1,0:T(8,128)S(1)} %copy-done.3, ...), custom_call_target="tpu_custom_call" | custom-call | flops 12884901888 | bytes 39845888 | tf_op jit(solution)/shard_map/like_product/pallas_call | solution.py:123
  213.4 14.4 %collective-permute-done.9.refs_0_.refs_3_ = f32[24,8192]{1,0:T(8,128)} collective-permute-done((f32[24,8192]{1,0:T(8,128)}, f32[24,8192]{1,0:T(8,128)}, u32[]{:S(2)}, u32[]{:S(2)}) %collective-permute-start.9) | collective-permute-done | bytes 786464 | tf_op jit(solution)/shard_map/ppermute | solution.py:283
  230.9 3.7 collective-permute-start.14
  237.5 8.2 %collective-permute-done.8.refs_0_.refs_6_ = f32[24,8192]{1,0:T(8,128)} collective-permute-done((f32[24,8192]{1,0:T(8,128)}, f32[24,8192]{1,0:T(8,128)}, u32[]{:S(2)}, u32[]{:S(2)}) %collective-permute-start.8) | collective-permute-done | bytes 786464 | tf_op jit(solution)/shard_map/ppermute | solution.py:283
  245.7 10.2 %pack_all.1 = f32[16,8,8448]{2,1,0:T(8,128)} custom-call(f32[32,131072]{1,0:T(8,128)} %slip_ref.33, f32[16,8,256]{2,1,0:T(8,128)} %reshape.36.riders_ref, f32[24,8192]{1,0:T(8,128)} %collective-permute-done.8.refs_0_.refs_6_, f32[24,8192]{1,0:T(8,128)} %pack_block.29.refs_1_), custom_call_target="tpu_custom_call" | custom-call | bytes 8650752 | tf_op jit(solution)/shard_map/pack_all/pallas_call | solution.py:226
  255.9 23.4 %all-to-all-start = ((f32[16,8,8448]{2,1,0:T(8,128)}), f32[16,8,8448]{2,1,0:T(8,128)}, u32[]{:S(2)}, u32[]{:S(2)}) async-start(f32[16,8,8448]{2,1,0:T(8,128)} %pack_all.1), calls=%async_computation | async-start | bytes 8650752 | tf_op jit(solution)/shard_map/all_to_all | solution.py:433
  279.4 23.6 %unlike_product.1 = (f32[8,64,384]{2,1,0:T(8,128)S(1)}, f32[8,64,384]{2,1,0:T(8,128)S(1)}) custom-call(s32[1]{0:T(128)} %bitcast.1.me_ref, bf16[1024,16384]{1,0:T(8,128)(2,1)} %band_halves.1.band_ref.refs_0_, f32[24,8192]{1,0:T(8,128)S(1)} %collective-permute-done.12.refs_0_, f32[24,8192]{1,0:T(8,128)S(1)} %collective-permute-done.13.refs_1_, ...), custom_call_target="tpu_custom_call" | custom-call | flops 128849018880 | bytes 39845888 | tf_op jit(solution)/shard_map/unlike_product/pallas_call | solution.py:123
  308.1 15.6 %collective-permute-done.16 = f32[4,64,384]{2,1,0:T(8,128)S(1)} collective-permute-done((f32[4,64,384]{2,1,0:T(8,128)S(1)}, f32[4,64,384]{2,1,0:T(8,128)S(1)}, u32[]{:S(2)}, u32[]{:S(2)}) %collective-permute-start.16) | collective-permute-done | bytes 393248 | tf_op jit(solution)/shard_map/ppermute | solution.py:283
  326.8 27.5 %collective-permute-done.17 = f32[2,64,384]{2,1,0:T(8,128)S(1)} collective-permute-done((f32[2,64,384]{2,1,0:T(8,128)S(1)}, f32[2,64,384]{2,1,0:T(8,128)S(1)}, u32[]{:S(2)}, u32[]{:S(2)}) %collective-permute-start.17) | collective-permute-done | bytes 196640 | tf_op jit(solution)/shard_map/ppermute | solution.py:283
  354.3 5.1 %all-to-all-done.riders_ref = f32[16,8,8448]{2,1,0:T(8,128)} async-done(((f32[16,8,8448]{2,1,0:T(8,128)}), f32[16,8,8448]{2,1,0:T(8,128)}, u32[]{:S(2)}, u32[]{:S(2)}) %all-to-all-start) | async-done | bytes 4325408 | tf_op jit(solution)/shard_map/all_to_all | solution.py:433
  359.5 15.1 %last_product.1 = (f32[8,64,128]{2,1,0:T(8,128)S(1)}, f32[8,64,128]{2,1,0:T(8,128)S(1)}) custom-call(s32[1]{0:T(128)} %bitcast.1.me_ref, bf16[1024,16384]{1,0:T(8,128)(2,1)} %band_halves.1.band_ref.refs_0_, f32[128,8448]{1,0:T(8,128)} %bitcast.4.slip_ref, f32[1,64,384]{2,1,0:T(8,128)S(1)} %get-tuple-element.27.refs_0_, ...), custom_call_target="tpu_custom_call" | custom-call | flops 8589934592 | bytes 37748736 | tf_op jit(solution)/shard_map/last_product/pallas_call | solution.py:123
  375.3 17.6 %collective-permute-start.18 = (f32[1,64,384]{2,1,0:T(8,128)S(1)}, f32[1,64,384]{2,1,0:T(8,128)S(1)}, u32[]{:S(2)}, u32[]{:S(2)}) collective-permute-start(f32[1,64,384]{2,1,0:T(8,128)S(1)} %get-tuple-element.27.refs_0_), channel_id=1, source_target_pairs={{0,8},{1,9},{2,10},{3,11},{4,12},{5,13},{6,14},{7,15},{8,0},{9,1},... | collective-permute-start | bytes 294920 | tf_op jit(solution)/shard_map/ppermute | solution.py:283
  399.5 3.0 collective-permute-start.25
  405.6 3.5 collective-permute-done.26.refs_9_
  (104 shorter events, 63.3 us)
Async XLA Ops:
  2.7 40.4 %collective-permute-start.1 = (f32[24,8192]{1,0:T(8,128)}, f32[24,8192]{1,0:T(8,128)S(1)}, u32[]{:S(2)}, u32[]{:S(2)}) collective-permute-start(f32[24,8192]{1,0:T(8,128)} %pack_block.15.refs_1_), channel_id=1, source_target_pairs={{0,8},{1,9},{2,10},{3,11},{4,12},{5,13},{6,14},{7,15},{8,0},{9,1},... | collective-permute-start | bytes 2359304 | tf_op jit(solution)/shard_map/ppermute | solution.py:283
  8.8 40.3 %collective-permute-start.3 = (f32[24,8192]{1,0:T(8,128)}, f32[24,8192]{1,0:T(8,128)S(1)}, u32[]{:S(2)}, u32[]{:S(2)}) collective-permute-start(f32[24,8192]{1,0:T(8,128)} %pack_block.16.refs_1_), channel_id=1, source_target_pairs={{0,4},{1,5},{2,6},{3,7},{4,0},{5,1},{6,2},{7,3},{8,12},{9,13},{10,... | collective-permute-start | bytes 2359304 | tf_op jit(solution)/shard_map/ppermute | solution.py:283
  12.5 64.9 %collective-permute-start = (f32[24,8192]{1,0:T(8,128)}, f32[24,8192]{1,0:T(8,128)S(1)}, u32[]{:S(2)}, u32[]{:S(2)}) collective-permute-start(f32[24,8192]{1,0:T(8,128)} %pack_block.17.refs_1_), channel_id=1, source_target_pairs={{0,10},{1,11},{2,8},{3,9},{4,14},{5,15},{6,12},{7,13},{8,2},{9,3},... | collective-permute-start | bytes 2359304 | tf_op jit(solution)/shard_map/ppermute | solution.py:283
  15.9 82.1 %collective-permute-start.5 = (f32[24,8192]{1,0:T(8,128)}, f32[24,8192]{1,0:T(8,128)}, u32[]{:S(2)}, u32[]{:S(2)}) collective-permute-start(f32[24,8192]{1,0:T(8,128)} %pack_block.18.refs_1_), channel_id=1, source_target_pairs={{0,6},{1,7},{2,4},{3,5},{4,2},{5,3},{6,0},{7,1},{8,14},{9,15},{10,... | collective-permute-start | bytes 2359304 | tf_op jit(solution)/shard_map/ppermute | solution.py:283
  46.0 54.1 %collective-permute-start.2 = (f32[24,8192]{1,0:T(8,128)}, f32[24,8192]{1,0:T(8,128)S(1)}, u32[]{:S(2)}, u32[]{:S(2)}) collective-permute-start(f32[24,8192]{1,0:T(8,128)} %pack_block.19.refs_1_), channel_id=1, source_target_pairs={{0,12},{1,13},{2,14},{3,15},{4,8},{5,9},{6,10},{7,11},{8,4},{9,5},... | collective-permute-start | bytes 2359304 | tf_op jit(solution)/shard_map/ppermute | solution.py:283
  52.1 121.1 %collective-permute-start.4 = (f32[24,8192]{1,0:T(8,128)}, f32[24,8192]{1,0:T(8,128)}, u32[]{:S(2)}, u32[]{:S(2)}) collective-permute-start(f32[24,8192]{1,0:T(8,128)} %pack_block.20.refs_1_), channel_id=1, source_target_pairs={{0,2},{1,3},{2,0},{3,1},{4,6},{5,7},{6,4},{7,5},{8,10},{9,11},{10,... | collective-permute-start | bytes 2359304 | tf_op jit(solution)/shard_map/ppermute | solution.py:283
  94.5 83.8 %collective-permute-start.6 = (f32[24,8192]{1,0:T(8,128)}, f32[24,8192]{1,0:T(8,128)}, u32[]{:S(2)}, u32[]{:S(2)}) collective-permute-start(f32[24,8192]{1,0:T(8,128)} %pack_block.21.refs_1_), channel_id=1, source_target_pairs={{0,14},{1,15},{2,12},{3,13},{4,10},{5,11},{6,8},{7,9},{8,6},{9,7},... | collective-permute-start | bytes 2359304 | tf_op jit(solution)/shard_map/ppermute | solution.py:283
  100.1 81.8 %collective-permute-start.7 = (f32[24,8192]{1,0:T(8,128)}, f32[24,8192]{1,0:T(8,128)}, u32[]{:S(2)}, u32[]{:S(2)}) collective-permute-start(f32[24,8192]{1,0:T(8,128)} %pack_block.22.refs_1_), channel_id=1, source_target_pairs={{0,9},{1,8},{2,11},{3,10},{4,13},{5,12},{6,15},{7,14},{8,1},{9,0},... | collective-permute-start | bytes 2359304 | tf_op jit(solution)/shard_map/ppermute | solution.py:283
  130.4 78.8 %collective-permute-start.11 = (f32[24,8192]{1,0:T(8,128)}, f32[24,8192]{1,0:T(8,128)}, u32[]{:S(2)}, u32[]{:S(2)}) collective-permute-start(f32[24,8192]{1,0:T(8,128)} %pack_block.23.refs_1_), channel_id=1, source_target_pairs={{0,5},{1,4},{2,7},{3,6},{4,1},{5,0},{6,3},{7,2},{8,13},{9,12},{10,... | collective-permute-start | bytes 2359304 | tf_op jit(solution)/shard_map/ppermute | solution.py:283
  175.4 35.9 %collective-permute-start.10 = (f32[24,8192]{1,0:T(8,128)}, f32[24,8192]{1,0:T(8,128)}, u32[]{:S(2)}, u32[]{:S(2)}) collective-permute-start(f32[24,8192]{1,0:T(8,128)} %pack_block.24.refs_1_), channel_id=1, source_target_pairs={{0,11},{1,10},{2,9},{3,8},{4,15},{5,14},{6,13},{7,12},{8,3},{9,2},... | collective-permute-start | bytes 2359304 | tf_op jit(solution)/shard_map/ppermute | solution.py:283
  180.4 47.5 %collective-permute-start.9 = (f32[24,8192]{1,0:T(8,128)}, f32[24,8192]{1,0:T(8,128)}, u32[]{:S(2)}, u32[]{:S(2)}) collective-permute-start(f32[24,8192]{1,0:T(8,128)} %pack_block.25.refs_1_), channel_id=1, source_target_pairs={{0,7},{1,6},{2,5},{3,4},{4,3},{5,2},{6,1},{7,0},{8,15},{9,14},{10,... | collective-permute-start | bytes 2359304 | tf_op jit(solution)/shard_map/ppermute | solution.py:283
  208.0 37.8 %collective-permute-start.8 = (f32[24,8192]{1,0:T(8,128)}, f32[24,8192]{1,0:T(8,128)}, u32[]{:S(2)}, u32[]{:S(2)}) collective-permute-start(f32[24,8192]{1,0:T(8,128)} %pack_block.26.refs_1_), channel_id=1, source_target_pairs={{0,13},{1,12},{2,15},{3,14},{4,9},{5,8},{6,11},{7,10},{8,5},{9,4},... | collective-permute-start | bytes 2359304 | tf_op jit(solution)/shard_map/ppermute | solution.py:283
  229.9 49.4 %collective-permute-start.13 = (f32[24,8192]{1,0:T(8,128)}, f32[24,8192]{1,0:T(8,128)S(1)}, u32[]{:S(2)}, u32[]{:S(2)}) collective-permute-start(f32[24,8192]{1,0:T(8,128)} %pack_block.29.refs_1_), channel_id=1, source_target_pairs={{0,3},{1,2},{2,1},{3,0},{4,7},{5,6},{6,5},{7,4},{8,11},{9,10},{10,... | collective-permute-start | bytes 2359304 | tf_op jit(solution)/shard_map/ppermute | solution.py:283
  230.9 48.4 %collective-permute-start.14 = (f32[24,8192]{1,0:T(8,128)S(1)}, f32[24,8192]{1,0:T(8,128)}, u32[]{:S(2)}, u32[]{:S(2)}) collective-permute-start(f32[24,8192]{1,0:T(8,128)S(1)} %copy-done.13), channel_id=1, source_target_pairs={{0,15},{1,14},{2,13},{3,12},{4,11},{5,10},{6,9},{7,8},{8,7},{9,6},... | collective-permute-start | bytes 2359304 | tf_op jit(solution)/shard_map/ppermute | solution.py:283
  234.6 44.7 %collective-permute-start.12 = (f32[24,8192]{1,0:T(8,128)S(1)}, f32[24,8192]{1,0:T(8,128)S(1)}, u32[]{:S(2)}, u32[]{:S(2)}) collective-permute-start(f32[24,8192]{1,0:T(8,128)S(1)} %copy-done.12), channel_id=1, source_target_pairs={{0,1},{1,0},{2,3},{3,2},{4,5},{5,4},{6,7},{7,6},{8,9},{9,8},{10,11... | collective-permute-start | bytes 2359304 | tf_op jit(solution)/shard_map/ppermute | solution.py:283
  255.9 103.5 %all-to-all-start = ((f32[16,8,8448]{2,1,0:T(8,128)}), f32[16,8,8448]{2,1,0:T(8,128)}, u32[]{:S(2)}, u32[]{:S(2)}) async-start(f32[16,8,8448]{2,1,0:T(8,128)} %pack_all.1), calls=%async_computation | async-start | bytes 8650752 | tf_op jit(solution)/shard_map/all_to_all | solution.py:433
  305.5 18.2 %collective-permute-start.16 = (f32[4,64,384]{2,1,0:T(8,128)S(1)}, f32[4,64,384]{2,1,0:T(8,128)S(1)}, u32[]{:S(2)}, u32[]{:S(2)}) collective-permute-start(f32[4,64,384]{2,1,0:T(8,128)S(1)} %dynamic-slice_bitcast_fusion), channel_id=1, source_target_pairs={{0,2},{1,3},{2,0},{3,1},{4,6},{5,7},{6,4},{7,5},{8,10},{9,11},{10,... | collective-permute-start | bytes 1179656 | tf_op jit(solution)/shard_map/ppermute | solution.py:283
  323.7 30.6 %collective-permute-start.17 = (f32[2,64,384]{2,1,0:T(8,128)S(1)}, f32[2,64,384]{2,1,0:T(8,128)S(1)}, u32[]{:S(2)}, u32[]{:S(2)}) collective-permute-start(f32[2,64,384]{2,1,0:T(8,128)S(1)} %dynamic-slice_bitcast_fusion.1), channel_id=1, source_target_pairs={{0,4},{1,5},{2,6},{3,7},{4,0},{5,1},{6,2},{7,3},{8,12},{9,13},{10,... | collective-permute-start | bytes 589832 | tf_op jit(solution)/shard_map/ppermute | solution.py:283
  374.6 18.3 %collective-permute-start.19 = (f32[8,64,128]{2,1,0:T(8,128)S(1)}, f32[8,64,128]{2,1,0:T(8,128)S(1)}, u32[]{:S(2)}, u32[]{:S(2)}) collective-permute-start(f32[8,64,128]{2,1,0:T(8,128)S(1)} %get-tuple-element.16.after_ref), channel_id=1, source_target_pairs={{0,1},{1,0},{2,3},{3,2},{4,5},{5,4},{6,7},{7,6},{8,9},{9,8},{10,11... | collective-permute-start | bytes 786440 | tf_op jit(solution)/shard_map/ppermute | solution.py:283
  375.3 23.0 %collective-permute-start.18 = (f32[1,64,384]{2,1,0:T(8,128)S(1)}, f32[1,64,384]{2,1,0:T(8,128)S(1)}, u32[]{:S(2)}, u32[]{:S(2)}) collective-permute-start(f32[1,64,384]{2,1,0:T(8,128)S(1)} %get-tuple-element.27.refs_0_), channel_id=1, source_target_pairs={{0,8},{1,9},{2,10},{3,11},{4,12},{5,13},{6,14},{7,15},{8,0},{9,1},... | collective-permute-start | bytes 294920 | tf_op jit(solution)/shard_map/ppermute | solution.py:283
  393.0 9.5 %collective-permute-start.21 = (f32[64,128]{1,0:T(8,128)S(1)}, f32[64,128]{1,0:T(8,128)S(1)}, u32[]{:S(2)}, u32[]{:S(2)}) collective-permute-start(f32[64,128]{1,0:T(8,128)S(1)} %get-tuple-element.20), channel_id=1, source_target_pairs={{0,4},{1,5},{2,6},{3,7},{4,0},{5,1},{6,2},{7,3},{8,12},{9,13},{10,... | collective-permute-start | bytes 98312 | tf_op jit(solution)/shard_map/ppermute | solution.py:283
  395.7 9.9 %collective-permute-start.22 = (f32[64,128]{1,0:T(8,128)S(1)}, f32[64,128]{1,0:T(8,128)S(1)}, u32[]{:S(2)}, u32[]{:S(2)}) collective-permute-start(f32[64,128]{1,0:T(8,128)S(1)} %get-tuple-element.21), channel_id=1, source_target_pairs={{0,6},{1,7},{2,4},{3,5},{4,2},{5,3},{6,0},{7,1},{8,14},{9,15},{10,... | collective-permute-start | bytes 98312 | tf_op jit(solution)/shard_map/ppermute | solution.py:283
  396.5 9.1 %collective-permute-start.23 = (f32[64,128]{1,0:T(8,128)S(1)}, f32[64,128]{1,0:T(8,128)S(1)}, u32[]{:S(2)}, u32[]{:S(2)}) collective-permute-start(f32[64,128]{1,0:T(8,128)S(1)} %get-tuple-element.22), channel_id=1, source_target_pairs={{0,8},{1,9},{2,10},{3,11},{4,12},{5,13},{6,14},{7,15},{8,0},{9,1},... | collective-permute-start | bytes 98312 | tf_op jit(solution)/shard_map/ppermute | solution.py:283
  398.3 7.3 %collective-permute-start.24 = (f32[64,128]{1,0:T(8,128)S(1)}, f32[64,128]{1,0:T(8,128)S(1)}, u32[]{:S(2)}, u32[]{:S(2)}) collective-permute-start(f32[64,128]{1,0:T(8,128)S(1)} %get-tuple-element.23), channel_id=1, source_target_pairs={{0,10},{1,11},{2,8},{3,9},{4,14},{5,15},{6,12},{7,13},{8,2},{9,3},... | collective-permute-start | bytes 98312 | tf_op jit(solution)/shard_map/ppermute | solution.py:283
  (19 other events, 516.8 us)

commit v4 on v3

--- a/solution.py
+++ b/solution.py
@@ -10,7 +10,7 @@
 VMEM_LIMIT = 48 * 1024 * 1024
 SMALL = pltpu.CompilerParams(vmem_limit_bytes=8 * 1024 * 1024)
 TAIL_ROWS = 8
-IN_FLIGHT = 4
+IN_FLIGHT = 5
 TILE = 2048
 FIRST_WEIGHT = 10
 LANES = 128
@@ -208,6 +208,7 @@
             out_specs=pl.BlockSpec((rows, depth), lambda i, to_ref: (0, 0)),
         ),
         out_shape=jax.ShapeDtypeStruct((rows, depth), jnp.float32),
+        compiler_params=pltpu.CompilerParams(vmem_limit_bytes=VMEM_LIMIT),
         cost_estimate=pl.CostEstimate(flops=0, bytes_accessed=8 * rows * depth, transcendentals=0),
         name="pack_block",
     )(to, slip_field, *after)

time: 412 us -> 406 us (0.985)
  waiting for transfers between devices: 122 us -> 98.8 us
  starting transfers between devices: 132 us -> 154 us
  Pallas kernels: 149 us -> 140 us
    ppermute x27, starting transfers between devices: 108 us -> 147 us  [swap(): return lax.ppermute(x, 'src', [(i, i ^ bit) for i in range(ways)])]
    ppermute x27, waiting for transfers between devices: 117 us -> 98.8 us  [swap(): return lax.ppermute(x, 'src', [(i, i ^ bit) for i in range(ways)])]
    all_to_all x1, starting transfers between devices: 23.4 us -> 6.99 us  [shards(): lax.all_to_all(pack_all(slip_field, head, tail, riders, (came[-IN_FLIGHT]...]
    pallas_call x15, Pallas kernels: 31.3 us -> 22.8 us  [pack(): pl.pallas_call(pack_kernel, grid_spec=pltpu.PrefetchScalarGridSpec(num_sc...]
    all_to_all x1, waiting for transfers between devices: 5.09 us -> 0.01 us  [shards(): lax.all_to_all(pack_all(slip_field, head, tail, riders, (came[-IN_FLIGHT]...]
  transfers between devices with their start and end apart: 28 -> 28, of which waited for: 10 -> 8; matrix products, arithmetic and copies ran while one was open for 1% -> 1% of each run, Pallas kernels for 32% -> 30%
where the time goes in v4:
time: 406 us; the launch traced here: 404 us
  starting transfers between devices  154 us (38%)
  Pallas kernels  140 us (34%)
  waiting for transfers between devices  98.8 us (24%)
  local copies, waits for them, and re-layouts  9.12 us (2%)
    ppermute x27, starting transfers between devices, swap(): return lax.ppermute(x, 'src', [(i, i ^ bit) for i in range(ways)])  147 us
    ppermute x27, waiting for transfers between devices, swap(): return lax.ppermute(x, 'src', [(i, i ^ bit) for i in range(ways)])  98.8 us
    pallas_call x3, Pallas kernels, product(): pl.pallas_call(kernel, grid_spec=pltpu.PrefetchScalarGridSpec(num_scalar_...  62.7 us
    pallas_call x1, Pallas kernels, split(): pl.pallas_call(split_kernel, grid=(4, depth // tile), in_specs=[pl.BlockS...  28.2 us
    pallas_call x15, Pallas kernels, pack(): pl.pallas_call(pack_kernel, grid_spec=pltpu.PrefetchScalarGridSpec(num_sc...  22.8 us
    pallas_call x1, Pallas kernels, gather(): pl.pallas_call(gather_kernel, in_specs=[SCALARS, ANY, AFTER], out_specs=W...  14.2 us
    pallas_call x1, Pallas kernels, pack_all(): pl.pallas_call(pack_all_kernel, grid=(ways,), in_specs=[pl.BlockSpec((row...  10.2 us
  transfers between devices with their start and end apart: 28, of which 8 were waited for; matrix products, arithmetic and copies ran while one was open for 1% of the time, Pallas kernels for 30%

profile of v4, /device:TPU:0, one launch (start us, length us, event | category | flops | bytes accessed | tf_op | source)
XLA Modules:
  0.0 404.5 jit_solution(18326679717385069421)
XLA Ops:
  1.8 4.1 %collective-permute-start.1 = (f32[24,8192]{1,0:T(8,128)S(1)}, f32[24,8192]{1,0:T(8,128)S(1)}, u32[]{:S(2)}, u32[]{:S(2)}) collective-permute-start(f32[24,8192]{1,0:T(8,128)S(1)} %pack_block.15.refs_1_), channel_id=1, source_target_pairs={{0,8},{1,9},{2,10},{3,11},{4,12},{5,13},{6,14},{7,15},{8,0},{9,1},... | collective-permute-start | bytes 2359304 | tf_op jit(solution)/shard_map/ppermute | solution.py:284
  15.6 3.9 collective-permute-start.3
  19.4 22.6 %collective-permute-done.1.refs_0_.refs_4_ = f32[24,8192]{1,0:T(8,128)S(1)} collective-permute-done((f32[24,8192]{1,0:T(8,128)S(1)}, f32[24,8192]{1,0:T(8,128)S(1)}, u32[]{:S(2)}, u32[]{:S(2)}) %collective-permute-start.1) | collective-permute-done | bytes 786464 | tf_op jit(solution)/shard_map/ppermute | solution.py:284
  44.1 6.0 %collective-permute-start.2 = (f32[24,8192]{1,0:T(8,128)}, f32[24,8192]{1,0:T(8,128)}, u32[]{:S(2)}, u32[]{:S(2)}) collective-permute-start(f32[24,8192]{1,0:T(8,128)} %pack_block.20.refs_1_), channel_id=1, source_target_pairs={{0,2},{1,3},{2,0},{3,1},{4,6},{5,7},{6,4},{7,5},{8,10},{9,11},{10,... | collective-permute-start | bytes 2359304 | tf_op jit(solution)/shard_map/ppermute | solution.py:284
  50.1 2.1 pack_block.21.refs_1_
  52.2 24.2 %collective-permute-done.after_ref.refs_5_ = f32[24,8192]{1,0:T(8,128)S(1)} collective-permute-done((f32[24,8192]{1,0:T(8,128)S(1)}, f32[24,8192]{1,0:T(8,128)S(1)}, u32[]{:S(2)}, u32[]{:S(2)}) %collective-permute-start) | collective-permute-done | bytes 786464 | tf_op jit(solution)/shard_map/ppermute | solution.py:284
  77.3 14.2 %slip_at_receivers.1.refs_0_ = f32[32,1024]{1,0:T(8,128)} custom-call(s32[1024]{0:T(1024)} %elements_ref.1, f32[32,131072]{1,0:T(8,128)} %slip_ref.33, f32[24,8192]{1,0:T(8,128)} %copy-done.1), custom_call_target="tpu_custom_call" | custom-call | bytes 16777216 | tf_op jit(solution)/shard_map/slip_at_receivers/pallas_call | solution.py:272
  94.9 3.8 collective-permute-start.8
  98.7 28.2 %band_halves.1.refs_0_.band_ref = bf16[1024,16384]{1,0:T(8,128)(2,1)} custom-call(f32[1024,8192]{1,0:T(8,128)} %band_ref.1, f32[24,8192]{1,0:T(8,128)S(1)} %collective-permute-done.3.after_ref.refs_6_), custom_call_target="tpu_custom_call" | custom-call | bytes 67108864 | tf_op jit(solution)/shard_map/band_halves/pallas_call | solution.py:39
  128.1 46.2 %collective-permute-start.7 = (f32[24,8192]{1,0:T(8,128)S(1)}, f32[24,8192]{1,0:T(8,128)S(1)}, u32[]{:S(2)}, u32[]{:S(2)}) collective-permute-start(f32[24,8192]{1,0:T(8,128)S(1)} %pack_block.24.refs_1_), channel_id=1, source_target_pairs={{0,11},{1,10},{2,9},{3,8},{4,15},{5,14},{6,13},{7,12},{8,3},{9,2},... | collective-permute-start | bytes 2359304 | tf_op jit(solution)/shard_map/ppermute | solution.py:284
  180.2 23.9 %like_product.1.refs_0_.refs_8_ = f32[1024,192]{1,0:T(8,128)} custom-call(s32[1]{0:T(128)} %bitcast.1.me_ref, bf16[1024,16384]{1,0:T(8,128)(2,1)} %band_halves.1.refs_0_.band_ref, f32[32,131072]{1,0:T(8,128)} %slip_ref.33, f32[24,8192]{1,0:T(8,128)} %collective-permute-done.2.refs_0_.refs_1_, f32[24,8192]{1,0:T(8,128)S(1)} %collective-permute-done.5.refs_0_.refs_2_, ...), custom_call_target="tpu_custom_call" | custom-call | flops 12884901888 | bytes 39845888 | tf_op jit(solution)/shard_map/like_product/pallas_call | solution.py:123
  208.1 16.8 %collective-permute-start.14 = (f32[24,8192]{1,0:T(8,128)S(1)}, f32[24,8192]{1,0:T(8,128)}, u32[]{:S(2)}, u32[]{:S(2)}) collective-permute-start(f32[24,8192]{1,0:T(8,128)S(1)} %pack_block.28.refs_1_), channel_id=1, source_target_pairs={{0,15},{1,14},{2,13},{3,12},{4,11},{5,10},{6,9},{7,8},{8,7},{9,6},... | collective-permute-start | bytes 2359304 | tf_op jit(solution)/shard_map/ppermute | solution.py:284
  229.3 17.8 %collective-permute-done.6.refs_0_.refs_3_ = f32[24,8192]{1,0:T(8,128)} collective-permute-done((f32[24,8192]{1,0:T(8,128)}, f32[24,8192]{1,0:T(8,128)}, u32[]{:S(2)}, u32[]{:S(2)}) %collective-permute-start.6) | collective-permute-done | bytes 786464 | tf_op jit(solution)/shard_map/ppermute | solution.py:284
  247.2 10.2 %pack_all.1 = f32[16,8,8448]{2,1,0:T(8,128)} custom-call(f32[32,131072]{1,0:T(8,128)} %slip_ref.33, f32[16,8,256]{2,1,0:T(8,128)} %reshape.36.riders_ref, f32[24,8192]{1,0:T(8,128)} %collective-permute-done.6.refs_0_.refs_3_, f32[24,8192]{1,0:T(8,128)} %copy-done.3), custom_call_target="tpu_custom_call" | custom-call | bytes 8650752 | tf_op jit(solution)/shard_map/pack_all/pallas_call | solution.py:227
  257.4 7.0 %all-to-all-start = ((f32[16,8,8448]{2,1,0:T(8,128)}), f32[16,8,8448]{2,1,0:T(8,128)}, u32[]{:S(2)}, u32[]{:S(2)}) async-start(f32[16,8,8448]{2,1,0:T(8,128)} %pack_all.1), calls=%async_computation | async-start | bytes 8650752 | tf_op jit(solution)/shard_map/all_to_all | solution.py:434
  266.9 23.7 %unlike_product.1 = (f32[8,64,384]{2,1,0:T(8,128)S(1)}, f32[8,64,384]{2,1,0:T(8,128)S(1)}) custom-call(s32[1]{0:T(128)} %bitcast.1.me_ref, bf16[1024,16384]{1,0:T(8,128)(2,1)} %band_halves.1.refs_0_.band_ref, f32[24,8192]{1,0:T(8,128)} %collective-permute-done.11.refs_0_, f32[24,8192]{1,0:T(8,128)} %collective-permute-done.12.refs_1_, ...), custom_call_target="tpu_custom_call" | custom-call | flops 128849018880 | bytes 39845888 | tf_op jit(solution)/shard_map/unlike_product/pallas_call | solution.py:123
  295.5 18.1 %collective-permute-done.16 = f32[4,64,384]{2,1,0:T(8,128)S(1)} collective-permute-done((f32[4,64,384]{2,1,0:T(8,128)S(1)}, f32[4,64,384]{2,1,0:T(8,128)S(1)}, u32[]{:S(2)}, u32[]{:S(2)}) %collective-permute-start.16) | collective-permute-done | bytes 393248 | tf_op jit(solution)/shard_map/ppermute | solution.py:284
  313.7 36.7 %collective-permute-start.17 = (f32[2,64,384]{2,1,0:T(8,128)S(1)}, f32[2,64,384]{2,1,0:T(8,128)S(1)}, u32[]{:S(2)}, u32[]{:S(2)}) collective-permute-start(f32[2,64,384]{2,1,0:T(8,128)S(1)} %dynamic-slice_bitcast_fusion.1), channel_id=1, source_target_pairs={{0,4},{1,5},{2,6},{3,7},{4,0},{5,1},{6,2},{7,3},{8,12},{9,13},{10,... | collective-permute-start | bytes 589832 | tf_op jit(solution)/shard_map/ppermute | solution.py:284
  350.7 11.1 %collective-permute-done.17 = f32[2,64,384]{2,1,0:T(8,128)S(1)} collective-permute-done((f32[2,64,384]{2,1,0:T(8,128)S(1)}, f32[2,64,384]{2,1,0:T(8,128)S(1)}, u32[]{:S(2)}, u32[]{:S(2)}) %collective-permute-start.17) | collective-permute-done | bytes 196640 | tf_op jit(solution)/shard_map/ppermute | solution.py:284
  361.9 15.1 %last_product.1 = (f32[8,64,128]{2,1,0:T(8,128)S(1)}, f32[8,64,128]{2,1,0:T(8,128)S(1)}) custom-call(s32[1]{0:T(128)} %bitcast.1.me_ref, bf16[1024,16384]{1,0:T(8,128)(2,1)} %band_halves.1.refs_0_.band_ref, f32[128,8448]{1,0:T(8,128)} %bitcast.4.slip_ref, f32[1,64,384]{2,1,0:T(8,128)S(1)} %get-tuple-element.27.refs_0_, ...), custom_call_target="tpu_custom_call" | custom-call | flops 8589934592 | bytes 37748736 | tf_op jit(solution)/shard_map/last_product/pallas_call | solution.py:123
  377.2 11.0 %collective-permute-start.18 = (f32[1,64,384]{2,1,0:T(8,128)S(1)}, f32[1,64,384]{2,1,0:T(8,128)S(1)}, u32[]{:S(2)}, u32[]{:S(2)}) collective-permute-start(f32[1,64,384]{2,1,0:T(8,128)S(1)} %get-tuple-element.27.refs_0_), channel_id=1, source_target_pairs={{0,8},{1,9},{2,10},{3,11},{4,12},{5,13},{6,14},{7,15},{8,0},{9,1},... | collective-permute-start | bytes 294920 | tf_op jit(solution)/shard_map/ppermute | solution.py:284
  394.2 2.6 collective-permute-start.25
  396.8 2.6 collective-permute-start.26
  400.8 2.6 collective-permute-done.26.refs_9_
  (108 shorter events, 48.9 us)
Async XLA Ops:
  1.8 40.2 %collective-permute-start.1 = (f32[24,8192]{1,0:T(8,128)S(1)}, f32[24,8192]{1,0:T(8,128)S(1)}, u32[]{:S(2)}, u32[]{:S(2)}) collective-permute-start(f32[24,8192]{1,0:T(8,128)S(1)} %pack_block.15.refs_1_), channel_id=1, source_target_pairs={{0,8},{1,9},{2,10},{3,11},{4,12},{5,13},{6,14},{7,15},{8,0},{9,1},... | collective-permute-start | bytes 2359304 | tf_op jit(solution)/shard_map/ppermute | solution.py:284
  7.1 43.0 %collective-permute-start.5 = (f32[24,8192]{1,0:T(8,128)S(1)}, f32[24,8192]{1,0:T(8,128)S(1)}, u32[]{:S(2)}, u32[]{:S(2)}) collective-permute-start(f32[24,8192]{1,0:T(8,128)S(1)} %pack_block.16.refs_1_), channel_id=1, source_target_pairs={{0,4},{1,5},{2,6},{3,7},{4,0},{5,1},{6,2},{7,3},{8,12},{9,13},{10,... | collective-permute-start | bytes 2359304 | tf_op jit(solution)/shard_map/ppermute | solution.py:284
  9.9 66.5 %collective-permute-start = (f32[24,8192]{1,0:T(8,128)S(1)}, f32[24,8192]{1,0:T(8,128)S(1)}, u32[]{:S(2)}, u32[]{:S(2)}) collective-permute-start(f32[24,8192]{1,0:T(8,128)S(1)} %pack_block.17.refs_1_), channel_id=1, source_target_pairs={{0,10},{1,11},{2,8},{3,9},{4,14},{5,15},{6,12},{7,13},{8,2},{9,3},... | collective-permute-start | bytes 2359304 | tf_op jit(solution)/shard_map/ppermute | solution.py:284
  13.4 80.3 %collective-permute-start.4 = (f32[24,8192]{1,0:T(8,128)}, f32[24,8192]{1,0:T(8,128)}, u32[]{:S(2)}, u32[]{:S(2)}) collective-permute-start(f32[24,8192]{1,0:T(8,128)} %pack_block.18.refs_1_), channel_id=1, source_target_pairs={{0,6},{1,7},{2,4},{3,5},{4,2},{5,3},{6,0},{7,1},{8,14},{9,15},{10,... | collective-permute-start | bytes 2359304 | tf_op jit(solution)/shard_map/ppermute | solution.py:284
  15.6 83.1 %collective-permute-start.3 = (f32[24,8192]{1,0:T(8,128)}, f32[24,8192]{1,0:T(8,128)S(1)}, u32[]{:S(2)}, u32[]{:S(2)}) collective-permute-start(f32[24,8192]{1,0:T(8,128)} %pack_block.19.refs_1_), channel_id=1, source_target_pairs={{0,12},{1,13},{2,14},{3,15},{4,8},{5,9},{6,10},{7,11},{8,4},{9,5},... | collective-permute-start | bytes 2359304 | tf_op jit(solution)/shard_map/ppermute | solution.py:284
  44.1 130.1 %collective-permute-start.2 = (f32[24,8192]{1,0:T(8,128)}, f32[24,8192]{1,0:T(8,128)}, u32[]{:S(2)}, u32[]{:S(2)}) collective-permute-start(f32[24,8192]{1,0:T(8,128)} %pack_block.20.refs_1_), channel_id=1, source_target_pairs={{0,2},{1,3},{2,0},{3,1},{4,6},{5,7},{6,4},{7,5},{8,10},{9,11},{10,... | collective-permute-start | bytes 2359304 | tf_op jit(solution)/shard_map/ppermute | solution.py:284
  52.2 124.1 %collective-permute-start.9 = (f32[24,8192]{1,0:T(8,128)}, f32[24,8192]{1,0:T(8,128)}, u32[]{:S(2)}, u32[]{:S(2)}) collective-permute-start(f32[24,8192]{1,0:T(8,128)} %pack_block.21.refs_1_), channel_id=1, source_target_pairs={{0,14},{1,15},{2,12},{3,13},{4,10},{5,11},{6,8},{7,9},{8,6},{9,7},... | collective-permute-start | bytes 2359304 | tf_op jit(solution)/shard_map/ppermute | solution.py:284
  93.6 85.7 %collective-permute-start.10 = (f32[24,8192]{1,0:T(8,128)S(1)}, f32[24,8192]{1,0:T(8,128)S(1)}, u32[]{:S(2)}, u32[]{:S(2)}) collective-permute-start(f32[24,8192]{1,0:T(8,128)S(1)} %pack_block.22.refs_1_), channel_id=1, source_target_pairs={{0,9},{1,8},{2,11},{3,10},{4,13},{5,12},{6,15},{7,14},{8,1},{9,0},... | collective-permute-start | bytes 2359304 | tf_op jit(solution)/shard_map/ppermute | solution.py:284
  94.9 111.8 %collective-permute-start.8 = (f32[24,8192]{1,0:T(8,128)S(1)}, f32[24,8192]{1,0:T(8,128)S(1)}, u32[]{:S(2)}, u32[]{:S(2)}) collective-permute-start(f32[24,8192]{1,0:T(8,128)S(1)} %pack_block.23.refs_1_), channel_id=1, source_target_pairs={{0,5},{1,4},{2,7},{3,6},{4,1},{5,0},{6,3},{7,2},{8,13},{9,12},{10,... | collective-permute-start | bytes 2359304 | tf_op jit(solution)/shard_map/ppermute | solution.py:284
  128.1 96.9 %collective-permute-start.7 = (f32[24,8192]{1,0:T(8,128)S(1)}, f32[24,8192]{1,0:T(8,128)S(1)}, u32[]{:S(2)}, u32[]{:S(2)}) collective-permute-start(f32[24,8192]{1,0:T(8,128)S(1)} %pack_block.24.refs_1_), channel_id=1, source_target_pairs={{0,11},{1,10},{2,9},{3,8},{4,15},{5,14},{6,13},{7,12},{8,3},{9,2},... | collective-permute-start | bytes 2359304 | tf_op jit(solution)/shard_map/ppermute | solution.py:284
  176.3 70.9 %collective-permute-start.6 = (f32[24,8192]{1,0:T(8,128)}, f32[24,8192]{1,0:T(8,128)}, u32[]{:S(2)}, u32[]{:S(2)}) collective-permute-start(f32[24,8192]{1,0:T(8,128)} %pack_block.25.refs_1_), channel_id=1, source_target_pairs={{0,7},{1,6},{2,5},{3,4},{4,3},{5,2},{6,1},{7,0},{8,15},{9,14},{10,... | collective-permute-start | bytes 2359304 | tf_op jit(solution)/shard_map/ppermute | solution.py:284
  177.5 86.9 %collective-permute-start.13 = (f32[24,8192]{1,0:T(8,128)S(1)}, f32[24,8192]{1,0:T(8,128)}, u32[]{:S(2)}, u32[]{:S(2)}) collective-permute-start(f32[24,8192]{1,0:T(8,128)S(1)} %pack_block.26.refs_1_), channel_id=1, source_target_pairs={{0,13},{1,12},{2,15},{3,14},{4,9},{5,8},{6,11},{7,10},{8,5},{9,4},... | collective-permute-start | bytes 2359304 | tf_op jit(solution)/shard_map/ppermute | solution.py:284
  206.5 57.8 %collective-permute-start.11 = (f32[24,8192]{1,0:T(8,128)S(1)}, f32[24,8192]{1,0:T(8,128)}, u32[]{:S(2)}, u32[]{:S(2)}) collective-permute-start(f32[24,8192]{1,0:T(8,128)S(1)} %pack_block.27.refs_1_), channel_id=1, source_target_pairs={{0,1},{1,0},{2,3},{3,2},{4,5},{5,4},{6,7},{7,6},{8,9},{9,8},{10,11... | collective-permute-start | bytes 2359304 | tf_op jit(solution)/shard_map/ppermute | solution.py:284
  208.1 56.2 %collective-permute-start.14 = (f32[24,8192]{1,0:T(8,128)S(1)}, f32[24,8192]{1,0:T(8,128)}, u32[]{:S(2)}, u32[]{:S(2)}) collective-permute-start(f32[24,8192]{1,0:T(8,128)S(1)} %pack_block.28.refs_1_), channel_id=1, source_target_pairs={{0,15},{1,14},{2,13},{3,12},{4,11},{5,10},{6,9},{7,8},{8,7},{9,6},... | collective-permute-start | bytes 2359304 | tf_op jit(solution)/shard_map/ppermute | solution.py:284
  226.4 38.2 %collective-permute-start.12 = (f32[24,8192]{1,0:T(8,128)S(1)}, f32[24,8192]{1,0:T(8,128)}, u32[]{:S(2)}, u32[]{:S(2)}) collective-permute-start(f32[24,8192]{1,0:T(8,128)S(1)} %pack_block.29.refs_1_), channel_id=1, source_target_pairs={{0,3},{1,2},{2,1},{3,0},{4,7},{5,6},{6,5},{7,4},{8,11},{9,10},{10,... | collective-permute-start | bytes 2359304 | tf_op jit(solution)/shard_map/ppermute | solution.py:284
  257.4 104.5 %all-to-all-start = ((f32[16,8,8448]{2,1,0:T(8,128)}), f32[16,8,8448]{2,1,0:T(8,128)}, u32[]{:S(2)}, u32[]{:S(2)}) async-start(f32[16,8,8448]{2,1,0:T(8,128)} %pack_all.1), calls=%async_computation | async-start | bytes 8650752 | tf_op jit(solution)/shard_map/all_to_all | solution.py:434
  293.0 20.6 %collective-permute-start.16 = (f32[4,64,384]{2,1,0:T(8,128)S(1)}, f32[4,64,384]{2,1,0:T(8,128)S(1)}, u32[]{:S(2)}, u32[]{:S(2)}) collective-permute-start(f32[4,64,384]{2,1,0:T(8,128)S(1)} %dynamic-slice_bitcast_fusion), channel_id=1, source_target_pairs={{0,2},{1,3},{2,0},{3,1},{4,6},{5,7},{6,4},{7,5},{8,10},{9,11},{10,... | collective-permute-start | bytes 1179656 | tf_op jit(solution)/shard_map/ppermute | solution.py:284
  313.7 48.1 %collective-permute-start.17 = (f32[2,64,384]{2,1,0:T(8,128)S(1)}, f32[2,64,384]{2,1,0:T(8,128)S(1)}, u32[]{:S(2)}, u32[]{:S(2)}) collective-permute-start(f32[2,64,384]{2,1,0:T(8,128)S(1)} %dynamic-slice_bitcast_fusion.1), channel_id=1, source_target_pairs={{0,4},{1,5},{2,6},{3,7},{4,0},{5,1},{6,2},{7,3},{8,12},{9,13},{10,... | collective-permute-start | bytes 589832 | tf_op jit(solution)/shard_map/ppermute | solution.py:284
  377.0 11.1 %collective-permute-start.19 = (f32[8,64,128]{2,1,0:T(8,128)S(1)}, f32[8,64,128]{2,1,0:T(8,128)S(1)}, u32[]{:S(2)}, u32[]{:S(2)}) collective-permute-start(f32[8,64,128]{2,1,0:T(8,128)S(1)} %get-tuple-element.16.after_ref), channel_id=1, source_target_pairs={{0,1},{1,0},{2,3},{3,2},{4,5},{5,4},{6,7},{7,6},{8,9},{9,8},{10,11... | collective-permute-start | bytes 786440 | tf_op jit(solution)/shard_map/ppermute | solution.py:284
  377.2 16.0 %collective-permute-start.18 = (f32[1,64,384]{2,1,0:T(8,128)S(1)}, f32[1,64,384]{2,1,0:T(8,128)S(1)}, u32[]{:S(2)}, u32[]{:S(2)}) collective-permute-start(f32[1,64,384]{2,1,0:T(8,128)S(1)} %get-tuple-element.27.refs_0_), channel_id=1, source_target_pairs={{0,8},{1,9},{2,10},{3,11},{4,12},{5,13},{6,14},{7,15},{8,0},{9,1},... | collective-permute-start | bytes 294920 | tf_op jit(solution)/shard_map/ppermute | solution.py:284
  388.3 8.6 %collective-permute-start.21 = (f32[64,128]{1,0:T(8,128)S(1)}, f32[64,128]{1,0:T(8,128)S(1)}, u32[]{:S(2)}, u32[]{:S(2)}) collective-permute-start(f32[64,128]{1,0:T(8,128)S(1)} %get-tuple-element.20), channel_id=1, source_target_pairs={{0,4},{1,5},{2,6},{3,7},{4,0},{5,1},{6,2},{7,3},{8,12},{9,13},{10,... | collective-permute-start | bytes 98312 | tf_op jit(solution)/shard_map/ppermute | solution.py:284
  390.1 10.7 %collective-permute-start.22 = (f32[64,128]{1,0:T(8,128)S(1)}, f32[64,128]{1,0:T(8,128)S(1)}, u32[]{:S(2)}, u32[]{:S(2)}) collective-permute-start(f32[64,128]{1,0:T(8,128)S(1)} %get-tuple-element.21), channel_id=1, source_target_pairs={{0,6},{1,7},{2,4},{3,5},{4,2},{5,3},{6,0},{7,1},{8,14},{9,15},{10,... | collective-permute-start | bytes 98312 | tf_op jit(solution)/shard_map/ppermute | solution.py:284
  391.8 9.1 %collective-permute-start.23 = (f32[64,128]{1,0:T(8,128)S(1)}, f32[64,128]{1,0:T(8,128)S(1)}, u32[]{:S(2)}, u32[]{:S(2)}) collective-permute-start(f32[64,128]{1,0:T(8,128)S(1)} %get-tuple-element.22), channel_id=1, source_target_pairs={{0,8},{1,9},{2,10},{3,11},{4,12},{5,13},{6,14},{7,15},{8,0},{9,1},... | collective-permute-start | bytes 98312 | tf_op jit(solution)/shard_map/ppermute | solution.py:284
  393.2 7.6 %collective-permute-start.24 = (f32[64,128]{1,0:T(8,128)S(1)}, f32[64,128]{1,0:T(8,128)S(1)}, u32[]{:S(2)}, u32[]{:S(2)}) collective-permute-start(f32[64,128]{1,0:T(8,128)S(1)} %get-tuple-element.23), channel_id=1, source_target_pairs={{0,10},{1,11},{2,8},{3,9},{4,14},{5,15},{6,12},{7,13},{8,2},{9,3},... | collective-permute-start | bytes 98312 | tf_op jit(solution)/shard_map/ppermute | solution.py:284
  (21 other events, 371.1 us)

commit v5 on v4

--- a/solution.py
+++ b/solution.py
@@ -189,7 +189,7 @@
         compiler_params=SMALL,
         name="pair_sums",
     )(me, kept, swap(given, 1, ways))
-    return [blocks[0]] + [swap(blocks[k], 2 * k, ways) for k in range(1, pairs)]
+    return [blocks[0]] + [swap(blocks[k], 2 * k, ways) for k in reversed(range(1, pairs))]
 
 
 def pack_kernel(to_ref, slip_ref, *refs):

time: 406 us -> 404 us (level)
  transfers between devices with their start and end apart: 28 -> 28, of which waited for: 8 -> 8; matrix products, arithmetic and copies ran while one was open for 1% -> 1% of each run, Pallas kernels for 30% -> 31%
where the time goes in v5:
time: 404 us; the launch traced here: 402 us
  starting transfers between devices  154 us (38%)
  Pallas kernels  140 us (35%)
  waiting for transfers between devices  96.7 us (24%)
  local copies, waits for them, and re-layouts  9.12 us (2%)
    ppermute x27, starting transfers between devices, swap(): return lax.ppermute(x, 'src', [(i, i ^ bit) for i in range(ways)])  147 us
    ppermute x27, waiting for transfers between devices, swap(): return lax.ppermute(x, 'src', [(i, i ^ bit) for i in range(ways)])  96.7 us
    pallas_call x3, Pallas kernels, product(): pl.pallas_call(kernel, grid_spec=pltpu.PrefetchScalarGridSpec(num_scalar_...  62.7 us
    pallas_call x1, Pallas kernels, split(): pl.pallas_call(split_kernel, grid=(4, depth // tile), in_specs=[pl.BlockS...  28.2 us
    pallas_call x15, Pallas kernels, pack(): pl.pallas_call(pack_kernel, grid_spec=pltpu.PrefetchScalarGridSpec(num_sc...  22.8 us
    pallas_call x1, Pallas kernels, gather(): pl.pallas_call(gather_kernel, in_specs=[SCALARS, ANY, AFTER], out_specs=W...  14.2 us
    pallas_call x1, Pallas kernels, pack_all(): pl.pallas_call(pack_all_kernel, grid=(ways,), in_specs=[pl.BlockSpec((row...  10.2 us
  transfers between devices with their start and end apart: 28, of which 8 were waited for; matrix products, arithmetic and copies ran while one was open for 1% of the time, Pallas kernels for 31%

profile of v5, /device:TPU:0, one launch (start us, length us, event | category | flops | bytes accessed | tf_op | source)
XLA Modules:
  0.0 402.3 jit_solution(8542269501446146332)
XLA Ops:
  1.8 4.1 %collective-permute-start.1 = (f32[24,8192]{1,0:T(8,128)S(1)}, f32[24,8192]{1,0:T(8,128)S(1)}, u32[]{:S(2)}, u32[]{:S(2)}) collective-permute-start(f32[24,8192]{1,0:T(8,128)S(1)} %pack_block.15.refs_1_), channel_id=1, source_target_pairs={{0,8},{1,9},{2,10},{3,11},{4,12},{5,13},{6,14},{7,15},{8,0},{9,1},... | collective-permute-start | bytes 2359304 | tf_op jit(solution)/shard_map/ppermute | solution.py:284
  15.6 3.9 collective-permute-start.3
  19.4 22.6 %collective-permute-done.1.refs_0_.refs_4_ = f32[24,8192]{1,0:T(8,128)S(1)} collective-permute-done((f32[24,8192]{1,0:T(8,128)S(1)}, f32[24,8192]{1,0:T(8,128)S(1)}, u32[]{:S(2)}, u32[]{:S(2)}) %collective-permute-start.1) | collective-permute-done | bytes 786464 | tf_op jit(solution)/shard_map/ppermute | solution.py:284
  44.1 6.0 %collective-permute-start.2 = (f32[24,8192]{1,0:T(8,128)}, f32[24,8192]{1,0:T(8,128)}, u32[]{:S(2)}, u32[]{:S(2)}) collective-permute-start(f32[24,8192]{1,0:T(8,128)} %pack_block.20.refs_1_), channel_id=1, source_target_pairs={{0,2},{1,3},{2,0},{3,1},{4,6},{5,7},{6,4},{7,5},{8,10},{9,11},{10,... | collective-permute-start | bytes 2359304 | tf_op jit(solution)/shard_map/ppermute | solution.py:284
  52.2 24.2 %collective-permute-done.after_ref.refs_5_ = f32[24,8192]{1,0:T(8,128)S(1)} collective-permute-done((f32[24,8192]{1,0:T(8,128)S(1)}, f32[24,8192]{1,0:T(8,128)S(1)}, u32[]{:S(2)}, u32[]{:S(2)}) %collective-permute-start) | collective-permute-done | bytes 786464 | tf_op jit(solution)/shard_map/ppermute | solution.py:284
  77.3 14.2 %slip_at_receivers.1.refs_0_ = f32[32,1024]{1,0:T(8,128)} custom-call(s32[1024]{0:T(1024)} %elements_ref.1, f32[32,131072]{1,0:T(8,128)} %slip_ref.33, f32[24,8192]{1,0:T(8,128)} %copy-done.1), custom_call_target="tpu_custom_call" | custom-call | bytes 16777216 | tf_op jit(solution)/shard_map/slip_at_receivers/pallas_call | solution.py:272
  94.9 3.8 collective-permute-start.8
  98.7 28.2 %band_halves.1.refs_0_.band_ref = bf16[1024,16384]{1,0:T(8,128)(2,1)} custom-call(f32[1024,8192]{1,0:T(8,128)} %band_ref.1, f32[24,8192]{1,0:T(8,128)S(1)} %collective-permute-done.3.after_ref.refs_6_), custom_call_target="tpu_custom_call" | custom-call | bytes 67108864 | tf_op jit(solution)/shard_map/band_halves/pallas_call | solution.py:39
  128.1 46.2 %collective-permute-start.7 = (f32[24,8192]{1,0:T(8,128)S(1)}, f32[24,8192]{1,0:T(8,128)S(1)}, u32[]{:S(2)}, u32[]{:S(2)}) collective-permute-start(f32[24,8192]{1,0:T(8,128)S(1)} %pack_block.24.refs_1_), channel_id=1, source_target_pairs={{0,11},{1,10},{2,9},{3,8},{4,15},{5,14},{6,13},{7,12},{8,3},{9,2},... | collective-permute-start | bytes 2359304 | tf_op jit(solution)/shard_map/ppermute | solution.py:284
  180.2 23.9 %like_product.1.refs_0_.refs_8_ = f32[1024,192]{1,0:T(8,128)} custom-call(s32[1]{0:T(128)} %bitcast.1.me_ref, bf16[1024,16384]{1,0:T(8,128)(2,1)} %band_halves.1.refs_0_.band_ref, f32[32,131072]{1,0:T(8,128)} %slip_ref.33, f32[24,8192]{1,0:T(8,128)} %collective-permute-done.2.refs_0_.refs_1_, f32[24,8192]{1,0:T(8,128)S(1)} %collective-permute-done.5.refs_0_.refs_2_, ...), custom_call_target="tpu_custom_call" | custom-call | flops 12884901888 | bytes 39845888 | tf_op jit(solution)/shard_map/like_product/pallas_call | solution.py:123
  208.1 16.8 %collective-permute-start.14 = (f32[24,8192]{1,0:T(8,128)S(1)}, f32[24,8192]{1,0:T(8,128)}, u32[]{:S(2)}, u32[]{:S(2)}) collective-permute-start(f32[24,8192]{1,0:T(8,128)S(1)} %pack_block.28.refs_1_), channel_id=1, source_target_pairs={{0,15},{1,14},{2,13},{3,12},{4,11},{5,10},{6,9},{7,8},{8,7},{9,6},... | collective-permute-start | bytes 2359304 | tf_op jit(solution)/shard_map/ppermute | solution.py:284
  229.3 17.8 %collective-permute-done.6.refs_0_.refs_3_ = f32[24,8192]{1,0:T(8,128)} collective-permute-done((f32[24,8192]{1,0:T(8,128)}, f32[24,8192]{1,0:T(8,128)}, u32[]{:S(2)}, u32[]{:S(2)}) %collective-permute-start.6) | collective-permute-done | bytes 786464 | tf_op jit(solution)/shard_map/ppermute | solution.py:284
  247.2 10.2 %pack_all.1 = f32[16,8,8448]{2,1,0:T(8,128)} custom-call(f32[32,131072]{1,0:T(8,128)} %slip_ref.33, f32[16,8,256]{2,1,0:T(8,128)} %reshape.36.riders_ref, f32[24,8192]{1,0:T(8,128)} %collective-permute-done.6.refs_0_.refs_3_, f32[24,8192]{1,0:T(8,128)} %copy-done.3), custom_call_target="tpu_custom_call" | custom-call | bytes 8650752 | tf_op jit(solution)/shard_map/pack_all/pallas_call | solution.py:227
  257.4 7.0 %all-to-all-start = ((f32[16,8,8448]{2,1,0:T(8,128)}), f32[16,8,8448]{2,1,0:T(8,128)}, u32[]{:S(2)}, u32[]{:S(2)}) async-start(f32[16,8,8448]{2,1,0:T(8,128)} %pack_all.1), calls=%async_computation | async-start | bytes 8650752 | tf_op jit(solution)/shard_map/all_to_all | solution.py:434
  266.9 23.7 %unlike_product.1 = (f32[8,64,384]{2,1,0:T(8,128)S(1)}, f32[8,64,384]{2,1,0:T(8,128)S(1)}) custom-call(s32[1]{0:T(128)} %bitcast.1.me_ref, bf16[1024,16384]{1,0:T(8,128)(2,1)} %band_halves.1.refs_0_.band_ref, f32[24,8192]{1,0:T(8,128)} %collective-permute-done.11.refs_0_, f32[24,8192]{1,0:T(8,128)} %collective-permute-done.12.refs_1_, ...), custom_call_target="tpu_custom_call" | custom-call | flops 128849018880 | bytes 39845888 | tf_op jit(solution)/shard_map/unlike_product/pallas_call | solution.py:123
  295.5 18.1 %collective-permute-done.16 = f32[4,64,384]{2,1,0:T(8,128)S(1)} collective-permute-done((f32[4,64,384]{2,1,0:T(8,128)S(1)}, f32[4,64,384]{2,1,0:T(8,128)S(1)}, u32[]{:S(2)}, u32[]{:S(2)}) %collective-permute-start.16) | collective-permute-done | bytes 393248 | tf_op jit(solution)/shard_map/ppermute | solution.py:284
  313.7 36.7 %collective-permute-start.17 = (f32[2,64,384]{2,1,0:T(8,128)S(1)}, f32[2,64,384]{2,1,0:T(8,128)S(1)}, u32[]{:S(2)}, u32[]{:S(2)}) collective-permute-start(f32[2,64,384]{2,1,0:T(8,128)S(1)} %dynamic-slice_bitcast_fusion.1), channel_id=1, source_target_pairs={{0,4},{1,5},{2,6},{3,7},{4,0},{5,1},{6,2},{7,3},{8,12},{9,13},{10,... | collective-permute-start | bytes 589832 | tf_op jit(solution)/shard_map/ppermute | solution.py:284
  350.7 11.1 %collective-permute-done.17 = f32[2,64,384]{2,1,0:T(8,128)S(1)} collective-permute-done((f32[2,64,384]{2,1,0:T(8,128)S(1)}, f32[2,64,384]{2,1,0:T(8,128)S(1)}, u32[]{:S(2)}, u32[]{:S(2)}) %collective-permute-start.17) | collective-permute-done | bytes 196640 | tf_op jit(solution)/shard_map/ppermute | solution.py:284
  361.9 15.1 %last_product.1 = (f32[8,64,128]{2,1,0:T(8,128)S(1)}, f32[8,64,128]{2,1,0:T(8,128)S(1)}) custom-call(s32[1]{0:T(128)} %bitcast.1.me_ref, bf16[1024,16384]{1,0:T(8,128)(2,1)} %band_halves.1.refs_0_.band_ref, f32[128,8448]{1,0:T(8,128)} %bitcast.4.slip_ref, f32[1,64,384]{2,1,0:T(8,128)S(1)} %get-tuple-element.27.refs_0_, ...), custom_call_target="tpu_custom_call" | custom-call | flops 8589934592 | bytes 37748736 | tf_op jit(solution)/shard_map/last_product/pallas_call | solution.py:123
  377.2 11.0 %collective-permute-start.18 = (f32[1,64,384]{2,1,0:T(8,128)S(1)}, f32[1,64,384]{2,1,0:T(8,128)S(1)}, u32[]{:S(2)}, u32[]{:S(2)}) collective-permute-start(f32[1,64,384]{2,1,0:T(8,128)S(1)} %get-tuple-element.27.refs_0_), channel_id=1, source_target_pairs={{0,8},{1,9},{2,10},{3,11},{4,12},{5,13},{6,14},{7,15},{8,0},{9,1},... | collective-permute-start | bytes 294920 | tf_op jit(solution)/shard_map/ppermute | solution.py:284
  388.2 2.2 collective-permute-start.20
  390.4 2.2 collective-permute-start.22
  392.6 3.3 collective-permute-start.23
  396.3 3.1 collective-permute-start.26
  (108 shorter events, 45.8 us)
Async XLA Ops:
  1.8 40.2 %collective-permute-start.1 = (f32[24,8192]{1,0:T(8,128)S(1)}, f32[24,8192]{1,0:T(8,128)S(1)}, u32[]{:S(2)}, u32[]{:S(2)}) collective-permute-start(f32[24,8192]{1,0:T(8,128)S(1)} %pack_block.15.refs_1_), channel_id=1, source_target_pairs={{0,8},{1,9},{2,10},{3,11},{4,12},{5,13},{6,14},{7,15},{8,0},{9,1},... | collective-permute-start | bytes 2359304 | tf_op jit(solution)/shard_map/ppermute | solution.py:284
  7.1 43.0 %collective-permute-start.5 = (f32[24,8192]{1,0:T(8,128)S(1)}, f32[24,8192]{1,0:T(8,128)S(1)}, u32[]{:S(2)}, u32[]{:S(2)}) collective-permute-start(f32[24,8192]{1,0:T(8,128)S(1)} %pack_block.16.refs_1_), channel_id=1, source_target_pairs={{0,4},{1,5},{2,6},{3,7},{4,0},{5,1},{6,2},{7,3},{8,12},{9,13},{10,... | collective-permute-start | bytes 2359304 | tf_op jit(solution)/shard_map/ppermute | solution.py:284
  9.9 66.5 %collective-permute-start = (f32[24,8192]{1,0:T(8,128)S(1)}, f32[24,8192]{1,0:T(8,128)S(1)}, u32[]{:S(2)}, u32[]{:S(2)}) collective-permute-start(f32[24,8192]{1,0:T(8,128)S(1)} %pack_block.17.refs_1_), channel_id=1, source_target_pairs={{0,10},{1,11},{2,8},{3,9},{4,14},{5,15},{6,12},{7,13},{8,2},{9,3},... | collective-permute-start | bytes 2359304 | tf_op jit(solution)/shard_map/ppermute | solution.py:284
  13.4 80.3 %collective-permute-start.4 = (f32[24,8192]{1,0:T(8,128)}, f32[24,8192]{1,0:T(8,128)}, u32[]{:S(2)}, u32[]{:S(2)}) collective-permute-start(f32[24,8192]{1,0:T(8,128)} %pack_block.18.refs_1_), channel_id=1, source_target_pairs={{0,6},{1,7},{2,4},{3,5},{4,2},{5,3},{6,0},{7,1},{8,14},{9,15},{10,... | collective-permute-start | bytes 2359304 | tf_op jit(solution)/shard_map/ppermute | solution.py:284
  15.6 83.1 %collective-permute-start.3 = (f32[24,8192]{1,0:T(8,128)}, f32[24,8192]{1,0:T(8,128)S(1)}, u32[]{:S(2)}, u32[]{:S(2)}) collective-permute-start(f32[24,8192]{1,0:T(8,128)} %pack_block.19.refs_1_), channel_id=1, source_target_pairs={{0,12},{1,13},{2,14},{3,15},{4,8},{5,9},{6,10},{7,11},{8,4},{9,5},... | collective-permute-start | bytes 2359304 | tf_op jit(solution)/shard_map/ppermute | solution.py:284
  44.1 130.1 %collective-permute-start.2 = (f32[24,8192]{1,0:T(8,128)}, f32[24,8192]{1,0:T(8,128)}, u32[]{:S(2)}, u32[]{:S(2)}) collective-permute-start(f32[24,8192]{1,0:T(8,128)} %pack_block.20.refs_1_), channel_id=1, source_target_pairs={{0,2},{1,3},{2,0},{3,1},{4,6},{5,7},{6,4},{7,5},{8,10},{9,11},{10,... | collective-permute-start | bytes 2359304 | tf_op jit(solution)/shard_map/ppermute | solution.py:284
  52.2 124.1 %collective-permute-start.9 = (f32[24,8192]{1,0:T(8,128)}, f32[24,8192]{1,0:T(8,128)}, u32[]{:S(2)}, u32[]{:S(2)}) collective-permute-start(f32[24,8192]{1,0:T(8,128)} %pack_block.21.refs_1_), channel_id=1, source_target_pairs={{0,14},{1,15},{2,12},{3,13},{4,10},{5,11},{6,8},{7,9},{8,6},{9,7},... | collective-permute-start | bytes 2359304 | tf_op jit(solution)/shard_map/ppermute | solution.py:284
  93.6 85.7 %collective-permute-start.10 = (f32[24,8192]{1,0:T(8,128)S(1)}, f32[24,8192]{1,0:T(8,128)S(1)}, u32[]{:S(2)}, u32[]{:S(2)}) collective-permute-start(f32[24,8192]{1,0:T(8,128)S(1)} %pack_block.22.refs_1_), channel_id=1, source_target_pairs={{0,9},{1,8},{2,11},{3,10},{4,13},{5,12},{6,15},{7,14},{8,1},{9,0},... | collective-permute-start | bytes 2359304 | tf_op jit(solution)/shard_map/ppermute | solution.py:284
  94.9 111.8 %collective-permute-start.8 = (f32[24,8192]{1,0:T(8,128)S(1)}, f32[24,8192]{1,0:T(8,128)S(1)}, u32[]{:S(2)}, u32[]{:S(2)}) collective-permute-start(f32[24,8192]{1,0:T(8,128)S(1)} %pack_block.23.refs_1_), channel_id=1, source_target_pairs={{0,5},{1,4},{2,7},{3,6},{4,1},{5,0},{6,3},{7,2},{8,13},{9,12},{10,... | collective-permute-start | bytes 2359304 | tf_op jit(solution)/shard_map/ppermute | solution.py:284
  128.1 96.9 %collective-permute-start.7 = (f32[24,8192]{1,0:T(8,128)S(1)}, f32[24,8192]{1,0:T(8,128)S(1)}, u32[]{:S(2)}, u32[]{:S(2)}) collective-permute-start(f32[24,8192]{1,0:T(8,128)S(1)} %pack_block.24.refs_1_), channel_id=1, source_target_pairs={{0,11},{1,10},{2,9},{3,8},{4,15},{5,14},{6,13},{7,12},{8,3},{9,2},... | collective-permute-start | bytes 2359304 | tf_op jit(solution)/shard_map/ppermute | solution.py:284
  176.3 70.9 %collective-permute-start.6 = (f32[24,8192]{1,0:T(8,128)}, f32[24,8192]{1,0:T(8,128)}, u32[]{:S(2)}, u32[]{:S(2)}) collective-permute-start(f32[24,8192]{1,0:T(8,128)} %pack_block.25.refs_1_), channel_id=1, source_target_pairs={{0,7},{1,6},{2,5},{3,4},{4,3},{5,2},{6,1},{7,0},{8,15},{9,14},{10,... | collective-permute-start | bytes 2359304 | tf_op jit(solution)/shard_map/ppermute | solution.py:284
  177.5 86.9 %collective-permute-start.13 = (f32[24,8192]{1,0:T(8,128)S(1)}, f32[24,8192]{1,0:T(8,128)}, u32[]{:S(2)}, u32[]{:S(2)}) collective-permute-start(f32[24,8192]{1,0:T(8,128)S(1)} %pack_block.26.refs_1_), channel_id=1, source_target_pairs={{0,13},{1,12},{2,15},{3,14},{4,9},{5,8},{6,11},{7,10},{8,5},{9,4},... | collective-permute-start | bytes 2359304 | tf_op jit(solution)/shard_map/ppermute | solution.py:284
  206.5 57.8 %collective-permute-start.11 = (f32[24,8192]{1,0:T(8,128)S(1)}, f32[24,8192]{1,0:T(8,128)}, u32[]{:S(2)}, u32[]{:S(2)}) collective-permute-start(f32[24,8192]{1,0:T(8,128)S(1)} %pack_block.27.refs_1_), channel_id=1, source_target_pairs={{0,1},{1,0},{2,3},{3,2},{4,5},{5,4},{6,7},{7,6},{8,9},{9,8},{10,11... | collective-permute-start | bytes 2359304 | tf_op jit(solution)/shard_map/ppermute | solution.py:284
  208.1 56.2 %collective-permute-start.14 = (f32[24,8192]{1,0:T(8,128)S(1)}, f32[24,8192]{1,0:T(8,128)}, u32[]{:S(2)}, u32[]{:S(2)}) collective-permute-start(f32[24,8192]{1,0:T(8,128)S(1)} %pack_block.28.refs_1_), channel_id=1, source_target_pairs={{0,15},{1,14},{2,13},{3,12},{4,11},{5,10},{6,9},{7,8},{8,7},{9,6},... | collective-permute-start | bytes 2359304 | tf_op jit(solution)/shard_map/ppermute | solution.py:284
  226.4 38.2 %collective-permute-start.12 = (f32[24,8192]{1,0:T(8,128)S(1)}, f32[24,8192]{1,0:T(8,128)}, u32[]{:S(2)}, u32[]{:S(2)}) collective-permute-start(f32[24,8192]{1,0:T(8,128)S(1)} %pack_block.29.refs_1_), channel_id=1, source_target_pairs={{0,3},{1,2},{2,1},{3,0},{4,7},{5,6},{6,5},{7,4},{8,11},{9,10},{10,... | collective-permute-start | bytes 2359304 | tf_op jit(solution)/shard_map/ppermute | solution.py:284
  257.4 104.5 %all-to-all-start = ((f32[16,8,8448]{2,1,0:T(8,128)}), f32[16,8,8448]{2,1,0:T(8,128)}, u32[]{:S(2)}, u32[]{:S(2)}) async-start(f32[16,8,8448]{2,1,0:T(8,128)} %pack_all.1), calls=%async_computation | async-start | bytes 8650752 | tf_op jit(solution)/shard_map/all_to_all | solution.py:434
  293.0 20.6 %collective-permute-start.16 = (f32[4,64,384]{2,1,0:T(8,128)S(1)}, f32[4,64,384]{2,1,0:T(8,128)S(1)}, u32[]{:S(2)}, u32[]{:S(2)}) collective-permute-start(f32[4,64,384]{2,1,0:T(8,128)S(1)} %dynamic-slice_bitcast_fusion), channel_id=1, source_target_pairs={{0,2},{1,3},{2,0},{3,1},{4,6},{5,7},{6,4},{7,5},{8,10},{9,11},{10,... | collective-permute-start | bytes 1179656 | tf_op jit(solution)/shard_map/ppermute | solution.py:284
  313.7 48.1 %collective-permute-start.17 = (f32[2,64,384]{2,1,0:T(8,128)S(1)}, f32[2,64,384]{2,1,0:T(8,128)S(1)}, u32[]{:S(2)}, u32[]{:S(2)}) collective-permute-start(f32[2,64,384]{2,1,0:T(8,128)S(1)} %dynamic-slice_bitcast_fusion.1), channel_id=1, source_target_pairs={{0,4},{1,5},{2,6},{3,7},{4,0},{5,1},{6,2},{7,3},{8,12},{9,13},{10,... | collective-permute-start | bytes 589832 | tf_op jit(solution)/shard_map/ppermute | solution.py:284
  377.0 11.1 %collective-permute-start.19 = (f32[8,64,128]{2,1,0:T(8,128)S(1)}, f32[8,64,128]{2,1,0:T(8,128)S(1)}, u32[]{:S(2)}, u32[]{:S(2)}) collective-permute-start(f32[8,64,128]{2,1,0:T(8,128)S(1)} %get-tuple-element.16.after_ref), channel_id=1, source_target_pairs={{0,1},{1,0},{2,3},{3,2},{4,5},{5,4},{6,7},{7,6},{8,9},{9,8},{10,11... | collective-permute-start | bytes 786440 | tf_op jit(solution)/shard_map/ppermute | solution.py:284
  377.2 18.7 %collective-permute-start.18 = (f32[1,64,384]{2,1,0:T(8,128)S(1)}, f32[1,64,384]{2,1,0:T(8,128)S(1)}, u32[]{:S(2)}, u32[]{:S(2)}) collective-permute-start(f32[1,64,384]{2,1,0:T(8,128)S(1)} %get-tuple-element.27.refs_0_), channel_id=1, source_target_pairs={{0,8},{1,9},{2,10},{3,11},{4,12},{5,13},{6,14},{7,15},{8,0},{9,1},... | collective-permute-start | bytes 294920 | tf_op jit(solution)/shard_map/ppermute | solution.py:284
  388.2 7.7 %collective-permute-start.20 = (f32[64,128]{1,0:T(8,128)S(1)}, f32[64,128]{1,0:T(8,128)S(1)}, u32[]{:S(2)}, u32[]{:S(2)}) collective-permute-start(f32[64,128]{1,0:T(8,128)S(1)} %get-tuple-element.19), channel_id=1, source_target_pairs={{0,14},{1,15},{2,12},{3,13},{4,10},{5,11},{6,8},{7,9},{8,6},{9,7},... | collective-permute-start | bytes 98312 | tf_op jit(solution)/shard_map/ppermute | solution.py:284
  390.4 5.9 %collective-permute-start.21 = (f32[64,128]{1,0:T(8,128)S(1)}, f32[64,128]{1,0:T(8,128)S(1)}, u32[]{:S(2)}, u32[]{:S(2)}) collective-permute-start(f32[64,128]{1,0:T(8,128)S(1)} %get-tuple-element.20), channel_id=1, source_target_pairs={{0,12},{1,13},{2,14},{3,15},{4,8},{5,9},{6,10},{7,11},{8,4},{9,5},... | collective-permute-start | bytes 98312 | tf_op jit(solution)/shard_map/ppermute | solution.py:284
  390.4 10.4 %collective-permute-start.22 = (f32[64,128]{1,0:T(8,128)S(1)}, f32[64,128]{1,0:T(8,128)S(1)}, u32[]{:S(2)}, u32[]{:S(2)}) collective-permute-start(f32[64,128]{1,0:T(8,128)S(1)} %get-tuple-element.21), channel_id=1, source_target_pairs={{0,10},{1,11},{2,8},{3,9},{4,14},{5,15},{6,12},{7,13},{8,2},{9,3},... | collective-permute-start | bytes 98312 | tf_op jit(solution)/shard_map/ppermute | solution.py:284
  392.6 8.2 %collective-permute-start.23 = (f32[64,128]{1,0:T(8,128)S(1)}, f32[64,128]{1,0:T(8,128)S(1)}, u32[]{:S(2)}, u32[]{:S(2)}) collective-permute-start(f32[64,128]{1,0:T(8,128)S(1)} %get-tuple-element.22), channel_id=1, source_target_pairs={{0,8},{1,9},{2,10},{3,11},{4,12},{5,13},{6,14},{7,15},{8,0},{9,1},... | collective-permute-start | bytes 98312 | tf_op jit(solution)/shard_map/ppermute | solution.py:284
  (21 other events, 364.6 us)

commit v6 on v5

--- a/solution.py
+++ b/solution.py
@@ -172,23 +172,24 @@
     )
 
 
-def fold_kernel(me_ref, kept_ref, came_ref, *out_refs):
+def fold_kernel(me_ref, kept_ref, came_ref, after_ref, *out_refs):
+    del after_ref
     for k, out_ref in enumerate(out_refs):
         pair = (me_ref[0] >> 1) ^ k
         out_ref[...] = kept_ref[pair] + came_ref[pair]
 
 
-def last_sums(me, kept, given, ways):
+def last_sums(me, kept, given, after, ways):
     pairs = ways // 2
     shape = jax.ShapeDtypeStruct(kept.shape[1:], jnp.float32)
     blocks = pl.pallas_call(
         fold_kernel,
-        in_specs=[SCALARS, WHOLE, WHOLE],
+        in_specs=[SCALARS, WHOLE, WHOLE, ANY],
         out_specs=[WHOLE] * pairs,
         out_shape=[shape] * pairs,
         compiler_params=SMALL,
         name="pair_sums",
-    )(me, kept, swap(given, 1, ways))
+    )(me, kept, swap(given, 1, ways), after)
     return [blocks[0]] + [swap(blocks[k], 2 * k, ways) for k in reversed(range(1, pairs))]
 
 
@@ -449,7 +450,7 @@
     strong = strength(
         last, riders.shape[2], classes, normal_stress, static_friction, dynamic_friction, weakening_slip, given
     )
-    return slip_rate(shear_load, strong, places, first_terms, last_sums(here, kept, given, ways))
+    return slip_rate(shear_load, strong, places, first_terms, last_sums(here, kept, given, strong, ways))
 
 
 def solution(mesh):

time: 404 us -> 405 us (level)
  transfers between devices with their start and end apart: 28 -> 28, of which waited for: 8 -> 9; matrix products, arithmetic and copies ran while one was open for 1% -> 1% of each run, Pallas kernels for 31% -> 31%
where the time goes in v6:
time: 405 us; the launch traced here: 404 us
  starting transfers between devices  154 us (38%)
  Pallas kernels  140 us (35%)
  waiting for transfers between devices  98.1 us (24%)
  local copies, waits for them, and re-layouts  9.12 us (2%)
    ppermute x27, starting transfers between devices, swap(): return lax.ppermute(x, 'src', [(i, i ^ bit) for i in range(ways)])  147 us
    ppermute x27, waiting for transfers between devices, swap(): return lax.ppermute(x, 'src', [(i, i ^ bit) for i in range(ways)])  98.1 us
    pallas_call x3, Pallas kernels, product(): pl.pallas_call(kernel, grid_spec=pltpu.PrefetchScalarGridSpec(num_scalar_...  62.7 us
    pallas_call x1, Pallas kernels, split(): pl.pallas_call(split_kernel, grid=(4, depth // tile), in_specs=[pl.BlockS...  28.2 us
    pallas_call x15, Pallas kernels, pack(): pl.pallas_call(pack_kernel, grid_spec=pltpu.PrefetchScalarGridSpec(num_sc...  22.8 us
    pallas_call x1, Pallas kernels, gather(): pl.pallas_call(gather_kernel, in_specs=[SCALARS, ANY, AFTER], out_specs=W...  14.2 us
    pallas_call x1, Pallas kernels, pack_all(): pl.pallas_call(pack_all_kernel, grid=(ways,), in_specs=[pl.BlockSpec((row...  10.2 us
  transfers between devices with their start and end apart: 28, of which 9 were waited for; matrix products, arithmetic and copies ran while one was open for 1% of the time, Pallas kernels for 31%

profile of v6, /device:TPU:0, one launch (start us, length us, event | category | flops | bytes accessed | tf_op | source)
XLA Modules:
  0.0 403.7 jit_solution(16098177824796899410)
XLA Ops:
  1.8 4.1 %collective-permute-start.1 = (f32[24,8192]{1,0:T(8,128)S(1)}, f32[24,8192]{1,0:T(8,128)S(1)}, u32[]{:S(2)}, u32[]{:S(2)}) collective-permute-start(f32[24,8192]{1,0:T(8,128)S(1)} %pack_block.15.refs_1_), channel_id=1, source_target_pairs={{0,8},{1,9},{2,10},{3,11},{4,12},{5,13},{6,14},{7,15},{8,0},{9,1},... | collective-permute-start | bytes 2359304 | tf_op jit(solution)/shard_map/ppermute | solution.py:285
  15.6 3.9 collective-permute-start.3
  19.4 22.6 %collective-permute-done.1.refs_0_.refs_4_ = f32[24,8192]{1,0:T(8,128)S(1)} collective-permute-done((f32[24,8192]{1,0:T(8,128)S(1)}, f32[24,8192]{1,0:T(8,128)S(1)}, u32[]{:S(2)}, u32[]{:S(2)}) %collective-permute-start.1) | collective-permute-done | bytes 786464 | tf_op jit(solution)/shard_map/ppermute | solution.py:285
  44.1 6.0 %collective-permute-start.2 = (f32[24,8192]{1,0:T(8,128)}, f32[24,8192]{1,0:T(8,128)}, u32[]{:S(2)}, u32[]{:S(2)}) collective-permute-start(f32[24,8192]{1,0:T(8,128)} %pack_block.20.refs_1_), channel_id=1, source_target_pairs={{0,2},{1,3},{2,0},{3,1},{4,6},{5,7},{6,4},{7,5},{8,10},{9,11},{10,... | collective-permute-start | bytes 2359304 | tf_op jit(solution)/shard_map/ppermute | solution.py:285
  50.1 2.1 pack_block.21.refs_1_
  52.2 24.2 %collective-permute-done.after_ref.refs_5_ = f32[24,8192]{1,0:T(8,128)S(1)} collective-permute-done((f32[24,8192]{1,0:T(8,128)S(1)}, f32[24,8192]{1,0:T(8,128)S(1)}, u32[]{:S(2)}, u32[]{:S(2)}) %collective-permute-start) | collective-permute-done | bytes 786464 | tf_op jit(solution)/shard_map/ppermute | solution.py:285
  77.3 14.2 %slip_at_receivers.1.refs_0_ = f32[32,1024]{1,0:T(8,128)} custom-call(s32[1024]{0:T(1024)} %elements_ref.1, f32[32,131072]{1,0:T(8,128)} %slip_ref.33, f32[24,8192]{1,0:T(8,128)} %copy-done.1), custom_call_target="tpu_custom_call" | custom-call | bytes 16777216 | tf_op jit(solution)/shard_map/slip_at_receivers/pallas_call | solution.py:273
  94.9 3.8 collective-permute-start.8
  98.7 28.2 %band_halves.1.refs_0_.band_ref = bf16[1024,16384]{1,0:T(8,128)(2,1)} custom-call(f32[1024,8192]{1,0:T(8,128)} %band_ref.1, f32[24,8192]{1,0:T(8,128)S(1)} %collective-permute-done.3.after_ref.refs_6_), custom_call_target="tpu_custom_call" | custom-call | bytes 67108864 | tf_op jit(solution)/shard_map/band_halves/pallas_call | solution.py:39
  128.1 46.2 %collective-permute-start.7 = (f32[24,8192]{1,0:T(8,128)S(1)}, f32[24,8192]{1,0:T(8,128)S(1)}, u32[]{:S(2)}, u32[]{:S(2)}) collective-permute-start(f32[24,8192]{1,0:T(8,128)S(1)} %pack_block.24.refs_1_), channel_id=1, source_target_pairs={{0,11},{1,10},{2,9},{3,8},{4,15},{5,14},{6,13},{7,12},{8,3},{9,2},... | collective-permute-start | bytes 2359304 | tf_op jit(solution)/shard_map/ppermute | solution.py:285
  180.2 23.9 %like_product.1.refs_0_.refs_8_ = f32[1024,192]{1,0:T(8,128)} custom-call(s32[1]{0:T(128)} %bitcast.1.me_ref, bf16[1024,16384]{1,0:T(8,128)(2,1)} %band_halves.1.refs_0_.band_ref, f32[32,131072]{1,0:T(8,128)} %slip_ref.33, f32[24,8192]{1,0:T(8,128)} %collective-permute-done.2.refs_0_.refs_1_, f32[24,8192]{1,0:T(8,128)S(1)} %collective-permute-done.5.refs_0_.refs_2_, ...), custom_call_target="tpu_custom_call" | custom-call | flops 12884901888 | bytes 39845888 | tf_op jit(solution)/shard_map/like_product/pallas_call | solution.py:123
  208.1 16.8 %collective-permute-start.14 = (f32[24,8192]{1,0:T(8,128)S(1)}, f32[24,8192]{1,0:T(8,128)}, u32[]{:S(2)}, u32[]{:S(2)}) collective-permute-start(f32[24,8192]{1,0:T(8,128)S(1)} %pack_block.28.refs_1_), channel_id=1, source_target_pairs={{0,15},{1,14},{2,13},{3,12},{4,11},{5,10},{6,9},{7,8},{8,7},{9,6},... | collective-permute-start | bytes 2359304 | tf_op jit(solution)/shard_map/ppermute | solution.py:285
  229.3 17.8 %collective-permute-done.6.refs_0_.refs_3_ = f32[24,8192]{1,0:T(8,128)} collective-permute-done((f32[24,8192]{1,0:T(8,128)}, f32[24,8192]{1,0:T(8,128)}, u32[]{:S(2)}, u32[]{:S(2)}) %collective-permute-start.6) | collective-permute-done | bytes 786464 | tf_op jit(solution)/shard_map/ppermute | solution.py:285
  247.2 10.2 %pack_all.1 = f32[16,8,8448]{2,1,0:T(8,128)} custom-call(f32[32,131072]{1,0:T(8,128)} %slip_ref.33, f32[16,8,256]{2,1,0:T(8,128)} %reshape.36.riders_ref, f32[24,8192]{1,0:T(8,128)} %collective-permute-done.6.refs_0_.refs_3_, f32[24,8192]{1,0:T(8,128)} %copy-done.3), custom_call_target="tpu_custom_call" | custom-call | bytes 8650752 | tf_op jit(solution)/shard_map/pack_all/pallas_call | solution.py:228
  257.4 7.0 %all-to-all-start = ((f32[16,8,8448]{2,1,0:T(8,128)}), f32[16,8,8448]{2,1,0:T(8,128)}, u32[]{:S(2)}, u32[]{:S(2)}) async-start(f32[16,8,8448]{2,1,0:T(8,128)} %pack_all.1), calls=%async_computation | async-start | bytes 8650752 | tf_op jit(solution)/shard_map/all_to_all | solution.py:435
  266.9 23.7 %unlike_product.1 = (f32[8,64,384]{2,1,0:T(8,128)S(1)}, f32[8,64,384]{2,1,0:T(8,128)S(1)}) custom-call(s32[1]{0:T(128)} %bitcast.1.me_ref, bf16[1024,16384]{1,0:T(8,128)(2,1)} %band_halves.1.refs_0_.band_ref, f32[24,8192]{1,0:T(8,128)} %collective-permute-done.11.refs_0_, f32[24,8192]{1,0:T(8,128)} %collective-permute-done.12.refs_1_, ...), custom_call_target="tpu_custom_call" | custom-call | flops 128849018880 | bytes 39845888 | tf_op jit(solution)/shard_map/unlike_product/pallas_call | solution.py:123
  290.8 2.1 collective-permute-done.15
  295.5 18.1 %collective-permute-done.16 = f32[4,64,384]{2,1,0:T(8,128)S(1)} collective-permute-done((f32[4,64,384]{2,1,0:T(8,128)S(1)}, f32[4,64,384]{2,1,0:T(8,128)S(1)}, u32[]{:S(2)}, u32[]{:S(2)}) %collective-permute-start.16) | collective-permute-done | bytes 393248 | tf_op jit(solution)/shard_map/ppermute | solution.py:285
  313.7 36.7 %collective-permute-start.17 = (f32[2,64,384]{2,1,0:T(8,128)S(1)}, f32[2,64,384]{2,1,0:T(8,128)S(1)}, u32[]{:S(2)}, u32[]{:S(2)}) collective-permute-start(f32[2,64,384]{2,1,0:T(8,128)S(1)} %dynamic-slice_bitcast_fusion.1), channel_id=1, source_target_pairs={{0,4},{1,5},{2,6},{3,7},{4,0},{5,1},{6,2},{7,3},{8,12},{9,13},{10,... | collective-permute-start | bytes 589832 | tf_op jit(solution)/shard_map/ppermute | solution.py:285
  350.7 11.1 %collective-permute-done.17 = f32[2,64,384]{2,1,0:T(8,128)S(1)} collective-permute-done((f32[2,64,384]{2,1,0:T(8,128)S(1)}, f32[2,64,384]{2,1,0:T(8,128)S(1)}, u32[]{:S(2)}, u32[]{:S(2)}) %collective-permute-start.17) | collective-permute-done | bytes 196640 | tf_op jit(solution)/shard_map/ppermute | solution.py:285
  361.9 15.1 %last_product.1 = (f32[8,64,128]{2,1,0:T(8,128)S(1)}, f32[8,64,128]{2,1,0:T(8,128)S(1)}) custom-call(s32[1]{0:T(128)} %bitcast.1.me_ref, bf16[1024,16384]{1,0:T(8,128)(2,1)} %band_halves.1.refs_0_.band_ref, f32[128,8448]{1,0:T(8,128)} %bitcast.4.slip_ref, f32[1,64,384]{2,1,0:T(8,128)S(1)} %get-tuple-element.27.refs_0_, ...), custom_call_target="tpu_custom_call" | custom-call | flops 8589934592 | bytes 37748736 | tf_op jit(solution)/shard_map/last_product/pallas_call | solution.py:123
  377.2 11.0 %collective-permute-start.18 = (f32[1,64,384]{2,1,0:T(8,128)S(1)}, f32[1,64,384]{2,1,0:T(8,128)S(1)}, u32[]{:S(2)}, u32[]{:S(2)}) collective-permute-start(f32[1,64,384]{2,1,0:T(8,128)S(1)} %get-tuple-element.27.refs_0_), channel_id=1, source_target_pairs={{0,8},{1,9},{2,10},{3,11},{4,12},{5,13},{6,14},{7,15},{8,0},{9,1},... | collective-permute-start | bytes 294920 | tf_op jit(solution)/shard_map/ppermute | solution.py:285
  392.6 4.7 %collective-permute-start.23 = (f32[64,128]{1,0:T(8,128)S(1)}, f32[64,128]{1,0:T(8,128)S(1)}, u32[]{:S(2)}, u32[]{:S(2)}) collective-permute-start(f32[64,128]{1,0:T(8,128)S(1)} %get-tuple-element.22), channel_id=1, source_target_pairs={{0,8},{1,9},{2,10},{3,11},{4,12},{5,13},{6,14},{7,15},{8,0},{9,1},... | collective-permute-start | bytes 98312 | tf_op jit(solution)/shard_map/ppermute | solution.py:285
  397.4 3.4 collective-permute-start.26
  (108 shorter events, 45.8 us)
Async XLA Ops:
  1.8 40.2 %collective-permute-start.1 = (f32[24,8192]{1,0:T(8,128)S(1)}, f32[24,8192]{1,0:T(8,128)S(1)}, u32[]{:S(2)}, u32[]{:S(2)}) collective-permute-start(f32[24,8192]{1,0:T(8,128)S(1)} %pack_block.15.refs_1_), channel_id=1, source_target_pairs={{0,8},{1,9},{2,10},{3,11},{4,12},{5,13},{6,14},{7,15},{8,0},{9,1},... | collective-permute-start | bytes 2359304 | tf_op jit(solution)/shard_map/ppermute | solution.py:285
  7.1 43.0 %collective-permute-start.5 = (f32[24,8192]{1,0:T(8,128)S(1)}, f32[24,8192]{1,0:T(8,128)S(1)}, u32[]{:S(2)}, u32[]{:S(2)}) collective-permute-start(f32[24,8192]{1,0:T(8,128)S(1)} %pack_block.16.refs_1_), channel_id=1, source_target_pairs={{0,4},{1,5},{2,6},{3,7},{4,0},{5,1},{6,2},{7,3},{8,12},{9,13},{10,... | collective-permute-start | bytes 2359304 | tf_op jit(solution)/shard_map/ppermute | solution.py:285
  9.9 66.5 %collective-permute-start = (f32[24,8192]{1,0:T(8,128)S(1)}, f32[24,8192]{1,0:T(8,128)S(1)}, u32[]{:S(2)}, u32[]{:S(2)}) collective-permute-start(f32[24,8192]{1,0:T(8,128)S(1)} %pack_block.17.refs_1_), channel_id=1, source_target_pairs={{0,10},{1,11},{2,8},{3,9},{4,14},{5,15},{6,12},{7,13},{8,2},{9,3},... | collective-permute-start | bytes 2359304 | tf_op jit(solution)/shard_map/ppermute | solution.py:285
  13.4 80.3 %collective-permute-start.4 = (f32[24,8192]{1,0:T(8,128)}, f32[24,8192]{1,0:T(8,128)}, u32[]{:S(2)}, u32[]{:S(2)}) collective-permute-start(f32[24,8192]{1,0:T(8,128)} %pack_block.18.refs_1_), channel_id=1, source_target_pairs={{0,6},{1,7},{2,4},{3,5},{4,2},{5,3},{6,0},{7,1},{8,14},{9,15},{10,... | collective-permute-start | bytes 2359304 | tf_op jit(solution)/shard_map/ppermute | solution.py:285
  15.6 83.1 %collective-permute-start.3 = (f32[24,8192]{1,0:T(8,128)}, f32[24,8192]{1,0:T(8,128)S(1)}, u32[]{:S(2)}, u32[]{:S(2)}) collective-permute-start(f32[24,8192]{1,0:T(8,128)} %pack_block.19.refs_1_), channel_id=1, source_target_pairs={{0,12},{1,13},{2,14},{3,15},{4,8},{5,9},{6,10},{7,11},{8,4},{9,5},... | collective-permute-start | bytes 2359304 | tf_op jit(solution)/shard_map/ppermute | solution.py:285
  44.1 130.1 %collective-permute-start.2 = (f32[24,8192]{1,0:T(8,128)}, f32[24,8192]{1,0:T(8,128)}, u32[]{:S(2)}, u32[]{:S(2)}) collective-permute-start(f32[24,8192]{1,0:T(8,128)} %pack_block.20.refs_1_), channel_id=1, source_target_pairs={{0,2},{1,3},{2,0},{3,1},{4,6},{5,7},{6,4},{7,5},{8,10},{9,11},{10,... | collective-permute-start | bytes 2359304 | tf_op jit(solution)/shard_map/ppermute | solution.py:285
  52.2 124.1 %collective-permute-start.9 = (f32[24,8192]{1,0:T(8,128)}, f32[24,8192]{1,0:T(8,128)}, u32[]{:S(2)}, u32[]{:S(2)}) collective-permute-start(f32[24,8192]{1,0:T(8,128)} %pack_block.21.refs_1_), channel_id=1, source_target_pairs={{0,14},{1,15},{2,12},{3,13},{4,10},{5,11},{6,8},{7,9},{8,6},{9,7},... | collective-permute-start | bytes 2359304 | tf_op jit(solution)/shard_map/ppermute | solution.py:285
  93.6 85.7 %collective-permute-start.10 = (f32[24,8192]{1,0:T(8,128)S(1)}, f32[24,8192]{1,0:T(8,128)S(1)}, u32[]{:S(2)}, u32[]{:S(2)}) collective-permute-start(f32[24,8192]{1,0:T(8,128)S(1)} %pack_block.22.refs_1_), channel_id=1, source_target_pairs={{0,9},{1,8},{2,11},{3,10},{4,13},{5,12},{6,15},{7,14},{8,1},{9,0},... | collective-permute-start | bytes 2359304 | tf_op jit(solution)/shard_map/ppermute | solution.py:285
  94.9 111.8 %collective-permute-start.8 = (f32[24,8192]{1,0:T(8,128)S(1)}, f32[24,8192]{1,0:T(8,128)S(1)}, u32[]{:S(2)}, u32[]{:S(2)}) collective-permute-start(f32[24,8192]{1,0:T(8,128)S(1)} %pack_block.23.refs_1_), channel_id=1, source_target_pairs={{0,5},{1,4},{2,7},{3,6},{4,1},{5,0},{6,3},{7,2},{8,13},{9,12},{10,... | collective-permute-start | bytes 2359304 | tf_op jit(solution)/shard_map/ppermute | solution.py:285
  128.1 96.9 %collective-permute-start.7 = (f32[24,8192]{1,0:T(8,128)S(1)}, f32[24,8192]{1,0:T(8,128)S(1)}, u32[]{:S(2)}, u32[]{:S(2)}) collective-permute-start(f32[24,8192]{1,0:T(8,128)S(1)} %pack_block.24.refs_1_), channel_id=1, source_target_pairs={{0,11},{1,10},{2,9},{3,8},{4,15},{5,14},{6,13},{7,12},{8,3},{9,2},... | collective-permute-start | bytes 2359304 | tf_op jit(solution)/shard_map/ppermute | solution.py:285
  176.3 70.9 %collective-permute-start.6 = (f32[24,8192]{1,0:T(8,128)}, f32[24,8192]{1,0:T(8,128)}, u32[]{:S(2)}, u32[]{:S(2)}) collective-permute-start(f32[24,8192]{1,0:T(8,128)} %pack_block.25.refs_1_), channel_id=1, source_target_pairs={{0,7},{1,6},{2,5},{3,4},{4,3},{5,2},{6,1},{7,0},{8,15},{9,14},{10,... | collective-permute-start | bytes 2359304 | tf_op jit(solution)/shard_map/ppermute | solution.py:285
  177.5 86.9 %collective-permute-start.13 = (f32[24,8192]{1,0:T(8,128)S(1)}, f32[24,8192]{1,0:T(8,128)}, u32[]{:S(2)}, u32[]{:S(2)}) collective-permute-start(f32[24,8192]{1,0:T(8,128)S(1)} %pack_block.26.refs_1_), channel_id=1, source_target_pairs={{0,13},{1,12},{2,15},{3,14},{4,9},{5,8},{6,11},{7,10},{8,5},{9,4},... | collective-permute-start | bytes 2359304 | tf_op jit(solution)/shard_map/ppermute | solution.py:285
  206.5 57.8 %collective-permute-start.11 = (f32[24,8192]{1,0:T(8,128)S(1)}, f32[24,8192]{1,0:T(8,128)}, u32[]{:S(2)}, u32[]{:S(2)}) collective-permute-start(f32[24,8192]{1,0:T(8,128)S(1)} %pack_block.27.refs_1_), channel_id=1, source_target_pairs={{0,1},{1,0},{2,3},{3,2},{4,5},{5,4},{6,7},{7,6},{8,9},{9,8},{10,11... | collective-permute-start | bytes 2359304 | tf_op jit(solution)/shard_map/ppermute | solution.py:285
  208.1 56.2 %collective-permute-start.14 = (f32[24,8192]{1,0:T(8,128)S(1)}, f32[24,8192]{1,0:T(8,128)}, u32[]{:S(2)}, u32[]{:S(2)}) collective-permute-start(f32[24,8192]{1,0:T(8,128)S(1)} %pack_block.28.refs_1_), channel_id=1, source_target_pairs={{0,15},{1,14},{2,13},{3,12},{4,11},{5,10},{6,9},{7,8},{8,7},{9,6},... | collective-permute-start | bytes 2359304 | tf_op jit(solution)/shard_map/ppermute | solution.py:285
  226.4 38.2 %collective-permute-start.12 = (f32[24,8192]{1,0:T(8,128)S(1)}, f32[24,8192]{1,0:T(8,128)}, u32[]{:S(2)}, u32[]{:S(2)}) collective-permute-start(f32[24,8192]{1,0:T(8,128)S(1)} %pack_block.29.refs_1_), channel_id=1, source_target_pairs={{0,3},{1,2},{2,1},{3,0},{4,7},{5,6},{6,5},{7,4},{8,11},{9,10},{10,... | collective-permute-start | bytes 2359304 | tf_op jit(solution)/shard_map/ppermute | solution.py:285
  257.4 104.5 %all-to-all-start = ((f32[16,8,8448]{2,1,0:T(8,128)}), f32[16,8,8448]{2,1,0:T(8,128)}, u32[]{:S(2)}, u32[]{:S(2)}) async-start(f32[16,8,8448]{2,1,0:T(8,128)} %pack_all.1), calls=%async_computation | async-start | bytes 8650752 | tf_op jit(solution)/shard_map/all_to_all | solution.py:435
  293.0 20.6 %collective-permute-start.16 = (f32[4,64,384]{2,1,0:T(8,128)S(1)}, f32[4,64,384]{2,1,0:T(8,128)S(1)}, u32[]{:S(2)}, u32[]{:S(2)}) collective-permute-start(f32[4,64,384]{2,1,0:T(8,128)S(1)} %dynamic-slice_bitcast_fusion), channel_id=1, source_target_pairs={{0,2},{1,3},{2,0},{3,1},{4,6},{5,7},{6,4},{7,5},{8,10},{9,11},{10,... | collective-permute-start | bytes 1179656 | tf_op jit(solution)/shard_map/ppermute | solution.py:285
  313.7 48.1 %collective-permute-start.17 = (f32[2,64,384]{2,1,0:T(8,128)S(1)}, f32[2,64,384]{2,1,0:T(8,128)S(1)}, u32[]{:S(2)}, u32[]{:S(2)}) collective-permute-start(f32[2,64,384]{2,1,0:T(8,128)S(1)} %dynamic-slice_bitcast_fusion.1), channel_id=1, source_target_pairs={{0,4},{1,5},{2,6},{3,7},{4,0},{5,1},{6,2},{7,3},{8,12},{9,13},{10,... | collective-permute-start | bytes 589832 | tf_op jit(solution)/shard_map/ppermute | solution.py:285
  377.0 12.5 %collective-permute-start.19 = (f32[8,64,128]{2,1,0:T(8,128)S(1)}, f32[8,64,128]{2,1,0:T(8,128)S(1)}, u32[]{:S(2)}, u32[]{:S(2)}) collective-permute-start(f32[8,64,128]{2,1,0:T(8,128)S(1)} %get-tuple-element.16.after_ref), channel_id=1, source_target_pairs={{0,1},{1,0},{2,3},{3,2},{4,5},{5,4},{6,7},{7,6},{8,9},{9,8},{10,11... | collective-permute-start | bytes 786440 | tf_op jit(solution)/shard_map/ppermute | solution.py:285
  377.2 20.2 %collective-permute-start.18 = (f32[1,64,384]{2,1,0:T(8,128)S(1)}, f32[1,64,384]{2,1,0:T(8,128)S(1)}, u32[]{:S(2)}, u32[]{:S(2)}) collective-permute-start(f32[1,64,384]{2,1,0:T(8,128)S(1)} %get-tuple-element.27.refs_0_), channel_id=1, source_target_pairs={{0,8},{1,9},{2,10},{3,11},{4,12},{5,13},{6,14},{7,15},{8,0},{9,1},... | collective-permute-start | bytes 294920 | tf_op jit(solution)/shard_map/ppermute | solution.py:285
  389.6 7.7 %collective-permute-start.20 = (f32[64,128]{1,0:T(8,128)S(1)}, f32[64,128]{1,0:T(8,128)S(1)}, u32[]{:S(2)}, u32[]{:S(2)}) collective-permute-start(f32[64,128]{1,0:T(8,128)S(1)} %get-tuple-element.19), channel_id=1, source_target_pairs={{0,14},{1,15},{2,12},{3,13},{4,10},{5,11},{6,8},{7,9},{8,6},{9,7},... | collective-permute-start | bytes 98312 | tf_op jit(solution)/shard_map/ppermute | solution.py:285
  390.5 7.0 %collective-permute-start.21 = (f32[64,128]{1,0:T(8,128)S(1)}, f32[64,128]{1,0:T(8,128)S(1)}, u32[]{:S(2)}, u32[]{:S(2)}) collective-permute-start(f32[64,128]{1,0:T(8,128)S(1)} %get-tuple-element.20), channel_id=1, source_target_pairs={{0,12},{1,13},{2,14},{3,15},{4,8},{5,9},{6,10},{7,11},{8,4},{9,5},... | collective-permute-start | bytes 98312 | tf_op jit(solution)/shard_map/ppermute | solution.py:285
  391.0 9.9 %collective-permute-start.22 = (f32[64,128]{1,0:T(8,128)S(1)}, f32[64,128]{1,0:T(8,128)S(1)}, u32[]{:S(2)}, u32[]{:S(2)}) collective-permute-start(f32[64,128]{1,0:T(8,128)S(1)} %get-tuple-element.21), channel_id=1, source_target_pairs={{0,10},{1,11},{2,8},{3,9},{4,14},{5,15},{6,12},{7,13},{8,2},{9,3},... | collective-permute-start | bytes 98312 | tf_op jit(solution)/shard_map/ppermute | solution.py:285
  392.6 8.2 %collective-permute-start.23 = (f32[64,128]{1,0:T(8,128)S(1)}, f32[64,128]{1,0:T(8,128)S(1)}, u32[]{:S(2)}, u32[]{:S(2)}) collective-permute-start(f32[64,128]{1,0:T(8,128)S(1)} %get-tuple-element.22), channel_id=1, source_target_pairs={{0,8},{1,9},{2,10},{3,11},{4,12},{5,13},{6,14},{7,15},{8,0},{9,1},... | collective-permute-start | bytes 98312 | tf_op jit(solution)/shard_map/ppermute | solution.py:285
  (21 other events, 309.8 us)
